TPU v7x, 256 devices: a whole 4x4x8 slice. The times are simulated.
256 devices in a mesh: row: 8 (over y_hi, x), col: 32 (over y_lo, z, core).
Axes of the slice: x: 4, y: 4 (y_hi: 2, y_lo: 2; y = y_hi * 2 + y_lo), z: 8, core: 2. Of those that a mesh axis runs over, the one named last changes fastest.
Arguments:
- features: bfloat16 [1, 512, 1024, 128], P(None, 'row', 'col'), may hold values from -6 to 6
- conv_mid: bfloat16 [3, 3, 128, 128], replicated, may hold values from -0.1875 to 0.1875
- conv_out: bfloat16 [3, 3, 128, 3], replicated, may hold values from -0.5 to 0.5
- target: bfloat16 [1, 512, 1024, 3], P(None, 'row', 'col'), may hold values from -6 to 6
- vgg_first: bfloat16 [3, 3, 3, 64], replicated, may hold values from -1.25 to 1.25
- vgg_second: bfloat16 [3, 3, 64, 64], replicated, may hold values from -0.25 to 0.25
- perceptual_weights: float32 [64], replicated, may hold values from 0.2 to 2
- crop_anchors: int32 [1, 64, 2], replicated, may hold values from 0 to 768, as said below
- crop_owner: int32 [1, 64, 1], replicated, may hold values from 0 to 31; in each aligned block of 64 rows (0 to 63, 64 to 127, ..., all dimensions but the last counted through in order) at most 5 rows name the same one
- critic_first: bfloat16 [32, 4, 4, 3, 64], P('col'), may hold values from -0.875 to 0.875
- critic_second: bfloat16 [32, 4, 4, 64, 128], P('col'), may hold values from -0.1875 to 0.1875
- critic_score: bfloat16 [32, 128], P('col'), may hold values from -0.5 to 0.5
Outputs:
- decoder_grad: bfloat16 [1, 512, 1024, 128], P(None, 'row', 'col')
Inputs may be any that keep to these rules, and one draw needn't show every extreme that they name: `crop_anchors`: [..., 0] is a top row, at most 256; [..., 1] a left column, at most 768; both reach 0 and their largest value. `crop_owner`: every critic scores at least one crop and none more than 5; one scores exactly 5.
All inputs are finite; a program needn't handle non-finite values.
Results may differ from a plain program's by a relative error of at most 0.017.
Values may be sent and summed in bfloat16 or wider, within the bound.
No kernel may reach another device: no remote copies, remote signals or barrier semaphores. Data moves between devices by JAX's collectives and lax.ppermute only.
A program may use at most 128 MiB of HBM per device.

v0:
```python
import jax
import jax.numpy as jnp
import numpy as np
from jax import lax
from jax.experimental import pallas as pl
from jax.experimental.pallas import tpu as pltpu
from jax.sharding import PartitionSpec as P

BF = jnp.bfloat16
F32 = jnp.float32

LOSS_SCALE = 32.0
EPSILON = 1e-06
CROP = 256
TH, TW = 64, 32
IMG_H, IMG_W = 512, 1024
ROWS, COLS = 8, 32
CROPS = 64
DEC_HALO = 11
FEAT_HALO = 13
COL_HALO = 8
WIDE = TW + 2 * COL_HALO
TGT_HALO = 6
GRAD_PAD = 10
VMEM = 56 * 1024 * 1024


def sigmoid(v):
    return 0.5 * jnp.tanh(0.5 * v) + 0.5


def silu_parts(v):
    sig = sigmoid(v)
    act = v * sig
    return act, sig + act * (1.0 - sig)


def mm(a, b, ca=1, cb=0):
    return lax.dot_general(a, b, (((ca,), (cb,)), ((), ())), preferred_element_type=F32)


def iota(shape, dim):
    return lax.broadcasted_iota(jnp.int32, shape, dim)


def aligned(start, unit):
    return pl.multiple_of(start, unit) if not isinstance(start, int) else start


def conv_rows(src, row0, rows, weight, transposed=False, shift=0):
    n = rows * WIDE
    lhs = jnp.concatenate(
        [src[pl.ds(aligned((row0 + dy) * WIDE, 16), n), :] for dy in range(3)], axis=1
    )
    z = mm(lhs, weight, 1, 1 if transposed else 0)
    parts = []
    for dx in range(3):
        amount = (1 - dx - shift) % n
        part = z[:, dx * 128 : (dx + 1) * 128]
        parts.append(pltpu.roll(part, amount, 0) if amount else part)
    return parts[0] + parts[1] + parts[2]


def inside(row_first, col_first, rows):
    y = row_first + iota((rows, WIDE, 1), 0)
    x = col_first + iota((rows, WIDE, 1), 1)
    ok = (y >= 0) & (y < IMG_H) & (x >= 0) & (x < IMG_W)
    return ok.astype(F32).reshape(rows * WIDE, 1) > 0.0


def lanes_inside(row, col_first, low, high):
    lane = iota((8, 128), 1)
    x = col_first + lane
    return (x >= 0) & (x < IMG_W) & (lane >= low) & (lane < high) & (row >= 0) & (row < IMG_H)


def fold_taps(z, first, shift):
    total = None
    for dx in range(3):
        part = None
        for dy in range(3):
            k = (dx * 3 + dy) * 8
            piece = z[first + dy, k : k + 8, :]
            part = piece if part is None else part + piece
        amount = (1 - dx - shift) % 128
        part = pltpu.roll(part, amount, 1) if amount else part
        total = part if total is None else total + part
    return total


def three_shifts(v):
    return jnp.concatenate(
        [pltpu.roll(v, 1, 1), v, pltpu.roll(v, 127, 1), jnp.zeros_like(v)], axis=0
    ).astype(BF)


def decode_kernel(
    where, top, mid, bot, left, right, w_mid, w_out, pay, dec, slope_out, s1, s2, z, w
):
    r, c = where[0], where[1]
    for dy in range(3):
        for dx in range(3):
            w[dy * 128 : (dy + 1) * 128, dx * 128 : (dx + 1) * 128] = w_mid[dy, dx]

    def fill(first, rows, centre):
        n = rows * WIDE
        parts = [left[pl.ds(first, rows)], centre, right[pl.ds(first, rows)]]
        v = jnp.concatenate([p.astype(F32) for p in parts], axis=1).reshape(n, 128)
        s1[pl.ds(aligned(first * WIDE, 16), n), :] = (v * sigmoid(v)).astype(BF)

    fill(0, FEAT_HALO, top[...])
    fill(FEAT_HALO + TH, FEAT_HALO, bot[...])

    def fill_mid(i, carry):
        fill(FEAT_HALO + i * 8, 8, mid[pl.ds(i * 8, 8)])
        return carry

    lax.fori_loop(0, TH // 8, fill_mid, 0)

    def middle(i, carry):
        v = conv_rows(s1, i * 8, 8, w[...])
        act, slope = silu_parts(v)
        ok = inside(r * TH - 12 + i * 8, c * TW - COL_HALO, 8)
        s2[pl.ds(aligned(i * 8 * WIDE, 16), 8 * WIDE), :] = jnp.where(ok, act, 0.0).astype(BF)
        slope_out[pl.ds(i * 8, 8)] = (
            pltpu.roll(slope, 8 * WIDE - 6, 0).reshape(8, WIDE, 128).astype(BF)
        )
        return carry

    lax.fori_loop(0, 11, middle, 0)

    def taps(i, carry):
        for k in range(4):
            m = i * 4 + k
            z[m, :, 0:WIDE] = mm(w_out[...], s2[pl.ds(aligned(m * WIDE, 16), WIDE), :], 1, 1)
        return carry

    lax.fori_loop(0, 22, taps, 0)
    dec[86 * 8 :, :] = jnp.zeros((1024 - 86 * 8, 128), F32)

    def fold(i, carry):
        for k in range(2):
            d = i * 2 + k
            ok = lanes_inside(r * TH - DEC_HALO + d, c * TW - COL_HALO, 2, WIDE - 2)
            v = jnp.where(ok, fold_taps(z, d, 0), 0.0)
            dec[pl.ds(aligned(d * 8, 8), 8), :] = v.astype(BF).astype(F32)
        return carry

    lax.fori_loop(0, 43, fold, 0)
    planes = [
        dec[pl.ds(k, 128, stride=8), :].T[COL_HALO : COL_HALO + TW, :].astype(BF) for k in range(3)
    ]
    packed = jnp.concatenate(planes, axis=1)
    for k in range(COLS):
        pay[k] = packed


def percept_kernel(
    where, dec, tgt, w_first, w_second, w_back, w_last, weights, out, d3, pre, one, feat, bv, z
):
    r, c = where[0], where[1]
    col_first = c * TW - COL_HALO

    def gather(i, carry):
        for k in range(2):
            q = i * 2 + k
            v = dec[pl.ds(aligned((q + 5) * 8, 8), 8), :] + tgt[pl.ds(aligned(q * 8, 8), 8), :]
            d3[pl.ds(aligned(q * 32, 32), 32), :] = three_shifts(v)
        return carry

    lax.fori_loop(0, 38, gather, 0)

    def first(i, carry):
        for k in range(2):
            p = i * 2 + k
            v = mm(d3[pl.ds(aligned(p * 32, 32), 96), 0:WIDE], w_first[...], 0, 0)
            act = v * sigmoid(v)
            ok = inside(r * TH - 5 + p, col_first, 1)
            pre[pl.ds(aligned(p * WIDE, 16), WIDE), :] = v
            one[pl.ds(aligned(p * WIDE, 16), WIDE), :] = jnp.where(ok, act, 0.0).astype(BF)
        return carry

    lax.fori_loop(0, 37, first, 0)
    ones = ((iota((128, 128), 0) >> 6) == (iota((128, 128), 1) >> 6)).astype(F32).astype(BF)

    def half_sum(v):
        high = v.astype(BF)
        low = (v - high.astype(F32)).astype(BF)
        return mm(high, ones) + mm(low, ones)

    def second(i, carry):
        v = conv_rows(one, i * 8, 8, w_second[...])
        f, slope = silu_parts(v)
        scale = lax.rsqrt(half_sum(f * f) + EPSILON)
        unit = f * scale
        weighted = weights[...] * (unit - pltpu.roll(unit, 64, 1))
        g = scale * (weighted - unit * half_sum(weighted * unit)) * slope
        ok = inside(r * TH - 4 + i * 8, col_first, 8)
        feat[pl.ds(aligned(i * 8 * WIDE, 16), 8 * WIDE), :] = jnp.where(ok, g, 0.0).astype(BF)
        return carry

    lax.fori_loop(0, 9, second, 0)

    def back(i, carry):
        v = conv_rows(feat, i * 10, 10, w_back[...])
        x = pre[pl.ds(aligned((i * 10 + 2) * WIDE, 16), 10 * WIDE), :]
        v = v * silu_parts(x)[1]
        ok = inside(r * TH - 3 + i * 10, col_first, 10)
        bv[pl.ds(aligned(i * 10 * WIDE, 16), 10 * WIDE), :] = jnp.where(ok, v, 0.0).astype(BF)
        return carry

    lax.fori_loop(0, 7, back, 0)

    def taps(i, carry):
        for k in range(5):
            m = i * 5 + k
            z[m, :, 0:WIDE] = mm(w_last[...], bv[pl.ds(aligned(m * WIDE, 16), WIDE), :], 1, 1)
        return carry

    lax.fori_loop(0, 14, taps, 0)

    def fold(i, carry):
        for k in range(2):
            m = i * 2 + k
            out[pl.ds(aligned(m * 8, 8), 8), :] = fold_taps(z, m, 6)
        return carry

    lax.fori_loop(0, 34, fold, 0)


TILES = 22
LANES = TILES * 128


def critic_kernel(
    where, anchors, owners, strip, pick, rows_of, rows_back, w_first, w_second, score, out,
    strip32, grads, w_back, x_all, pre, act, two, cols,
):
    r, me = where[0], where[1]
    strip32[0:IMG_W, :] = strip[...].astype(F32)
    strip32[IMG_W:, :] = jnp.zeros((8, 384), F32)
    grads[...] = jnp.zeros(grads.shape, F32)
    w_back[...] = jnp.zeros(w_back.shape, BF)
    for par in range(2):
        for p in range(2):
            for t in range(2):
                i = par + 2 * t
                for kind, j in ((0, 1 + p), (1 + p, 3 - 3 * p)):
                    w_back[
                        (par * 2 + p) * 64 : (par * 2 + p + 1) * 64,
                        (t * 3 + kind) * 128 : (t * 3 + kind + 1) * 128,
                    ] = w_second[i, j * 64 : (j + 1) * 64, :]
    two[:, 0:128] = jnp.zeros((384, 128), BF)
    two[:, 11 * 128 :] = jnp.zeros((384, 128), BF)
    lane = iota((1, 128), 1)
    upper = lane >= 64
    first_x = (lane & 63) == 0
    last_x = (lane & 63) == 63
    wide_lane = iota((1, 384), 1) & 127

    def score_crop(top, left):
        y0 = r * TH - 2 - top
        v0 = lax.shift_right_arithmetic(y0 - 3, 2)
        e = 4 * v0 - y0 + 6
        crop_row = y0 - 9 + wide_lane
        in_crop = (crop_row >= 0) & (crop_row < CROP)
        window = strip32[pl.ds(aligned((left >> 3) * 8, 8), CROP + 8), :]
        window = pltpu.roll(window, lax.rem((CROP + 8) - (left & 7), CROP + 8), 0)[0:CROP]
        window = jnp.where(in_crop, window, 0.0).astype(BF)
        cols_of = mm(window, pick[...], 0, 0)
        halves = [
            jnp.concatenate(
                [cols_of[k * 128 + 40 * h : k * 128 + 40 * h + 64, :] for k in range(3)], axis=0
            )
            for h in range(2)
        ]
        mixed = []
        for m in range(6):
            tile = slice((m // 2) * 128, (m // 2 + 1) * 128)
            low, high = halves[0][:, tile], halves[1][:, tile]
            if m % 2 == 0:
                high = pltpu.roll(high, 64, 1)
            else:
                low = pltpu.roll(low, 64, 1)
            mixed.append(jnp.where(upper, high, low))
        patches = mm(rows_of[e], jnp.concatenate(mixed, axis=1).astype(BF)).astype(BF)
        for t in range(TILES):
            for m in range(6):
                x_all[m * 16 : (m + 1) * 16, t * 128 : (t + 1) * 128] = patches[
                    t * 16 : (t + 1) * 16, m * 128 : (m + 1) * 128
                ]
        pre[...] = mm(w_first[...], x_all[...], 0, 0)

        def activate(s, carry):
            for par in range(2):
                at = pl.ds(aligned((par * 11 + s) * 128, 128), 128)
                n = 2 * s + par + jnp.where(upper, 20, 0)
                u = 2 * v0 - 1 + n
                ok = (u >= 0) & (u < CROP // 2)
                a, slope = silu_parts(pre[:, at])
                a = jnp.where(ok, a, 0.0)
                pre[:, at] = jnp.where(ok, slope, 0.0)
                even, odd = a[:64], a[64:]
                act[0:64, at] = jnp.where(first_x, 0.0, pltpu.roll(odd, 1, 1)).astype(BF)
                act[64:128, at] = even.astype(BF)
                act[128:192, at] = odd.astype(BF)
                act[192:256, at] = jnp.where(last_x, 0.0, pltpu.roll(even, 127, 1)).astype(BF)
            return carry

        lax.fori_loop(0, 11, activate, 0)
        pre_two = mm(w_second[0], act[:, 0:1280], 0, 0)
        pre_two = pre_two + mm(w_second[1], act[:, 1408 : 1408 + 1280], 0, 0)
        pre_two = pre_two + mm(w_second[2], act[:, 128 : 128 + 1280], 0, 0)
        pre_two = pre_two + mm(w_second[3], act[:, 1408 + 128 : 1408 + 1408], 0, 0)
        for t in range(10):
            f, slope = silu_parts(pre_two[:, t * 128 : (t + 1) * 128])
            logit = jnp.sum(f * score[...], axis=0, keepdims=True)
            v = v0 + t + jnp.where(upper, 10, 0)
            ok = (v >= 0) & (v < CROP // 4)
            grad = jnp.where(ok, -LOSS_SCALE * sigmoid(-logit), 0.0)
            b = grad * score[...] * slope
            at = slice((t + 1) * 128, (t + 2) * 128)
            two[0:128, at] = b.astype(BF)
            two[128:256, at] = jnp.where(first_x, 0.0, pltpu.roll(b, 1, 1)).astype(BF)
            two[256:384, at] = jnp.where(last_x, 0.0, pltpu.roll(b, 127, 1)).astype(BF)
        up = mm(w_back[...], jnp.concatenate([two[:, 128:], two[:, 0 : 11 * 128]], axis=0))
        one = jnp.concatenate(
            [(up[0:128] * pre[:, 0:1408]).astype(BF), (up[128:256] * pre[:, 1408:]).astype(BF)],
            axis=1,
        )
        x_all[...] = mm(w_first[...], one).astype(BF)
        spread = jnp.concatenate(
            [
                jnp.concatenate(
                    [
                        x_all[m * 16 : (m + 1) * 16, t * 128 : (t + 1) * 128]
                        for t in range(TILES)
                    ],
                    axis=0,
                )
                for m in range(6)
            ],
            axis=1,
        )
        back = mm(rows_back[e], spread)
        cols[...] = jnp.zeros(cols.shape, F32)
        for h in range(2):
            tiles = []
            for k in range(3):
                low = back[:, 2 * k * 128 : (2 * k + 1) * 128]
                high = back[:, (2 * k + 1) * 128 : (2 * k + 2) * 128]
                if h == 0:
                    high = pltpu.roll(high, 64, 1)
                else:
                    low = pltpu.roll(low, 64, 1)
                tiles.append(jnp.where(upper, high, low))
            part = jnp.concatenate(tiles, axis=1)
            for k in range(3):
                at = slice(k * 128 + 40 * h, k * 128 + 40 * h + 64)
                cols[at, :] = cols[at, :] + part[k * 64 : (k + 1) * 64, :]
        placed = mm(pick[...], cols[...].astype(BF), 1, 1)
        keep = in_crop & (wide_lane >= 9) & (wide_lane < 77)
        placed = jnp.concatenate([jnp.where(keep, placed, 0.0), jnp.zeros((8, 384), F32)], axis=0)
        start = left + GRAD_PAD
        here = pl.ds(aligned((start >> 3) * 8, 8), CROP + 8)
        grads[here, :] = grads[here, :] + pltpu.roll(placed, start & 7, 0)

    def one_crop(q, carry):
        top, left = anchors[q, 0], anchors[q, 1]
        y0 = r * TH - 2 - top

        @pl.when((owners[q] == me) & (y0 < CROP) & (y0 + TH + 4 > 0))
        def _():
            score_crop(top, left)

        return carry

    lax.fori_loop(0, CROPS, one_crop, 0)

    def pack(k, carry):
        block = grads[pl.ds(aligned(k * TW + 8, 8), 40), :]
        a = pltpu.roll(block[:, 0:128], 128 - 9, 1)
        b = pltpu.roll(block[:, 128:256], 63, 1)
        d = pltpu.roll(block[:, 256:384], 7, 1)
        out[k] = jnp.concatenate(
            [jnp.where(lane < 72, a, b), jnp.where(lane < 16, b, d)], axis=1
        ).astype(BF)
        return carry

    lax.fori_loop(0, COLS, pack, 0)


def finish_kernel(
    where, parts, lpips, slope, feats, w_mid, w_out, out, square, turned, planes, ib, bm, w
):
    r, c = where[0], where[1]
    for dy in range(3):
        for dx in range(3):
            w[dx * 128 : (dx + 1) * 128, dy * 128 : (dy + 1) * 128] = w_mid[2 - dy, 2 - dx]
    total = parts[0].astype(F32)
    for k in range(1, COLS):
        total = total + parts[k].astype(F32)
    square[...] = jnp.zeros(square.shape, F32)
    square[0:40, :] = total
    turned[...] = square[...].T
    planes[...] = jnp.zeros(planes.shape, F32)
    for k in range(3):
        planes[pl.ds(k, 72, stride=8), :] = turned[k * 72 : (k + 1) * 72, :]

    def gather(i, carry):
        for k in range(2):
            m = i * 2 + k
            at = pl.ds(aligned(m * 8, 8), 8)
            ok = lanes_inside(r * TH - 2 + m, c * TW - 2, 0, 36)
            v = jnp.where(ok, lpips[at, :] + planes[at, :], 0.0)
            ib[pl.ds(aligned(m * 32, 32), 32), :] = three_shifts(v)
        return carry

    lax.fori_loop(0, 34, gather, 0)

    def middle(i, carry):
        for k in range(2):
            n = i * 2 + k
            v = mm(ib[pl.ds(aligned(n * 32, 32), 96), 0:WIDE], w_out[...], 0, 0)
            v = v * slope[n + 11].astype(F32)
            ok = inside(r * TH - 1 + n, c * TW - 2, 1)
            bm[pl.ds(aligned(n * WIDE, 16), WIDE), :] = jnp.where(ok, v, 0.0).astype(BF)
        return carry

    lax.fori_loop(0, 33, middle, 0)

    def last(i, carry):
        v = conv_rows(bm, i * 8, 8, w[...], transposed=True, shift=2)
        v = v.reshape(8, WIDE, 128)[:, 0:TW, :]
        x = feats[pl.ds(i * 8, 8)].astype(F32)
        out[pl.ds(i * 8, 8)] = (v * silu_parts(x)[1]).astype(BF)
        return carry

    lax.fori_loop(0, TH // 8, last, 0)


def call(kernel, outs, scratch, args, scalars=1):
    specs = [pl.BlockSpec(memory_space=pltpu.SMEM)] * scalars
    specs += [pl.BlockSpec(memory_space=pltpu.VMEM)] * (len(args) - scalars)
    return pl.pallas_call(
        kernel,
        in_specs=specs,
        out_specs=jax.tree.map(lambda _: pl.BlockSpec(memory_space=pltpu.VMEM), outs),
        out_shape=outs,
        scratch_shapes=[pltpu.VMEM(s, t) for s, t in scratch],
        compiler_params=pltpu.CompilerParams(vmem_limit_bytes=VMEM),
        interpret=INTERPRET,
    )(*args)


INTERPRET = False


def shape(dims, kind):
    return jax.ShapeDtypeStruct(dims, kind)


def row_tables():
    table = np.zeros((4, TILES, 16, 3, 64), np.float32)
    for e in range(4):
        for t in range(TILES):
            u = 2 * (t % 11) + t // 11
            for i in range(4):
                for k in range(3):
                    table[e, t, i * 4 + k, k, 2 * u + i + e] = 1.0
    return table.reshape(4, TILES * 16, 192)


def column_table():
    table = np.zeros((CROP, 6, 64), np.float32)
    for m in range(6):
        for x in range(64):
            if 0 <= 4 * x + m - 1 < CROP:
                table[4 * x + m - 1, m, x] = 1.0
    return table.reshape(CROP, 384)


def decode(where, top, mid, bot, left, right, conv_mid, conv_out):
    w = jnp.transpose(conv_out, (1, 0, 3, 2))
    w = jnp.pad(w, ((0, 0), (0, 0), (0, 5), (0, 0))).reshape(72, 128)
    w = jnp.pad(w, ((0, 8), (0, 0)))
    return call(
        decode_kernel,
        (
            shape((COLS, TW, 384), BF),
            shape((1024, 128), F32),
            shape((88, WIDE, 128), BF),
        ),
        [((90 * WIDE, 128), BF), ((88 * WIDE, 128), BF), ((88, 80, 128), F32), ((384, 384), BF)],
        (where, top, mid, bot, left, right, conv_mid, w),
    )


def percept(where, dec, tgt, vgg_first, vgg_second, weights):
    none = jnp.zeros((3, 3, 3, 64), BF)
    w_first = jnp.concatenate(
        [jnp.concatenate([vgg_first, none], -1), jnp.concatenate([none, vgg_first], -1)], 2
    )
    w_first = jnp.pad(w_first, ((0, 0), (0, 1), (0, 2), (0, 0))).reshape(96, 128)
    both = jnp.eye(2, dtype=BF)[None, :, None, None, :, None]
    w_second = (jnp.transpose(vgg_second, (0, 2, 1, 3))[:, None, :, :, None, :] * both).reshape(
        384, 384
    )
    w_back = jnp.transpose(jnp.flip(vgg_second, (0, 1)), (0, 3, 1, 2))
    w_back = jnp.pad(w_back, ((0, 0), (0, 64), (0, 0), (0, 64))).reshape(384, 384)
    w_last = jnp.transpose(jnp.flip(vgg_first, (0, 1)), (1, 0, 2, 3))
    w_last = jnp.pad(w_last, ((0, 0), (0, 0), (0, 5), (0, 64))).reshape(72, 128)
    w_last = jnp.pad(w_last, ((0, 8), (0, 0)))
    scaled = jnp.pad(2.0 * LOSS_SCALE * weights, (0, 64)).reshape(1, 128)
    return call(
        percept_kernel,
        shape((68 * 8, 128), F32),
        [
            ((76 * 32, 128), BF),
            ((74 * WIDE, 128), F32),
            ((74 * WIDE, 128), BF),
            ((72 * WIDE, 128), BF),
            ((70 * WIDE, 128), BF),
            ((70, 80, 128), F32),
        ],
        (where, dec, tgt, w_first, w_second, w_back, w_last, scaled),
    )


def critics(where, anchors, owners, strip, first, second, score):
    w = jnp.pad(first, ((0, 0), (0, 0), (0, 1), (0, 0)))
    w = jnp.transpose(w, (1, 0, 2, 3)).reshape(4, 16, 64)
    w = jnp.concatenate(
        [jnp.pad(w, ((0, 2), (0, 0), (0, 0))), jnp.pad(w, ((2, 0), (0, 0), (0, 0)))], -1
    ).reshape(96, 128)
    rows_of = row_tables()
    return call(
        critic_kernel,
        shape((COLS, 40, 256), BF),
        [
            ((IMG_W + 8, 384), F32),
            ((IMG_W + 24, 384), F32),
            ((256, 768), BF),
            ((96, LANES), BF),
            ((128, LANES), F32),
            ((256, LANES), BF),
            ((384, 12 * 128), BF),
            ((384, 384), F32),
        ],
        (
            where,
            anchors,
            owners,
            strip,
            jnp.asarray(column_table(), BF),
            jnp.asarray(rows_of, BF),
            jnp.asarray(np.swapaxes(rows_of, 1, 2), BF),
            w,
            second.reshape(4, 256, 128),
            score.astype(F32).reshape(128, 1),
        ),
        scalars=3,
    )


def finish(where, parts, lpips, slope, feats, conv_mid, conv_out):
    w = jnp.transpose(jnp.flip(conv_out, (0, 1)), (0, 1, 3, 2))
    w = jnp.pad(w, ((0, 0), (0, 1), (0, 5), (0, 0))).reshape(96, 128)
    return call(
        finish_kernel,
        shape((TH, TW, 128), BF),
        [
            ((128, 256), F32),
            ((256, 128), F32),
            ((72 * 8, 128), F32),
            ((68 * 32, 128), BF),
            ((66 * WIDE, 128), BF),
            ((384, 384), BF),
        ],
        (where, parts, lpips, slope, feats, conv_mid, w),
    )


def neighbours(block, axis, dim, width):
    count = lax.axis_size(axis)
    forward = [(i, i + 1) for i in range(count - 1)]
    backward = [(target, source) for source, target in forward]
    size = block.shape[dim]
    low = lax.ppermute(lax.slice_in_dim(block, size - width, size, axis=dim), axis, forward)
    high = lax.ppermute(lax.slice_in_dim(block, 0, width, axis=dim), axis, backward)
    return low, high


def local(
    features, conv_mid, conv_out, target, vgg_first, vgg_second, perceptual_weights,
    crop_anchors, crop_owner, critic_first, critic_second, critic_score,
):
    where = jnp.stack([lax.axis_index("row"), lax.axis_index("col")]).astype(jnp.int32)
    feats = features[0]
    planar = jnp.transpose(target[0], (0, 2, 1))
    top, bot = neighbours(feats, "row", 0, FEAT_HALO)
    t_top, t_bot = neighbours(planar, "row", 0, TGT_HALO)

    def edge(first, last):
        return jnp.concatenate([a[:, first:last] for a in (top, feats, bot)], 0)

    count = lax.axis_size("col")
    forward = [(i, i + 1) for i in range(count - 1)]
    backward = [(t, s) for s, t in forward]
    left = lax.ppermute(edge(TW - COL_HALO, TW), "col", forward)
    right = lax.ppermute(edge(0, COL_HALO), "col", backward)
    tall = jnp.concatenate([t_top, planar, t_bot], 0)
    t_left, t_right = neighbours(tall, "col", 2, TGT_HALO)
    tgt = jnp.concatenate([t_left, tall, t_right], 2).astype(F32)
    tgt = jnp.pad(tgt, ((0, 0), (3, 2), (2, 128 - 2 - TW - 2 * TGT_HALO))).reshape(76 * 8, 128)
    pay, dec, slope = decode(where, top, feats, bot, left, right, conv_mid, conv_out)
    strip = lax.all_to_all(pay, "col", split_axis=0, concat_axis=0, tiled=True)
    lpips = percept(where, dec, tgt, vgg_first, vgg_second, perceptual_weights)
    grads = critics(
        where,
        crop_anchors.reshape(CROPS, 2),
        crop_owner.reshape(CROPS),
        strip.reshape(IMG_W, 384),
        critic_first[0],
        critic_second[0],
        critic_score[0],
    )
    parts = lax.all_to_all(grads, "col", split_axis=0, concat_axis=0, tiled=True)
    return finish(where, parts, lpips, slope, feats, conv_mid, conv_out)[None]


def solution(mesh):
    placed = (
        P(None, "row", "col", None),
        P(),
        P(),
        P(None, "row", "col", None),
        P(),
        P(),
        P(),
        P(),
        P(),
        P("col", None, None, None, None),
        P("col", None, None, None, None),
        P("col", None),
    )
    return jax.shard_map(
        local, mesh=mesh, in_specs=placed, out_specs=P(None, "row", "col", None), check_vma=False
    )
```

profile of v0, /device:TPU:15, one launch (start us, length us, event | category | flops | bytes accessed | tf_op | source)
XLA Modules:
  0.0 173.8 jit_solution(5158735356713992023)
XLA Ops:
  0.0 1.0 slice_bitcast_fusion
  1.0 3.8 %collective-permute-start = (bf16[13,32,128]{2,1,0:T(8,128)(2,1)S(1)}, bf16[13,32,128]{2,1,0:T(8,128)(2,1)S(1)}, u32[]{:S(2)}, u32[]{:S(2)}) collective-permute-start(bf16[13,32,128]{2,1,0:T(8,128)(2,1)S(1)} %get-tuple-element.14), channel_id=1, source_target_pairs={{0,32},{32,64},{64,96},{96,128},{128,160},{160,192},{192,224},{1,3... | collective-permute-start | bytes 319496 | tf_op jit(solution)/shard_map/ppermute | solution.py:589
  4.8 1.9 %collective-permute-start.1 = (bf16[13,32,128]{2,1,0:T(8,128)(2,1)S(1)}, bf16[13,32,128]{2,1,0:T(8,128)(2,1)S(1)}, u32[]{:S(2)}, u32[]{:S(2)}) collective-permute-start(bf16[13,32,128]{2,1,0:T(8,128)(2,1)S(1)} %get-tuple-element.13), channel_id=1, source_target_pairs={{32,0},{64,32},{96,64},{128,96},{160,128},{192,160},{224,192},{33,... | collective-permute-start | bytes 319496 | tf_op jit(solution)/shard_map/ppermute | solution.py:590
  6.8 1.0 fusion.6
  7.8 6.1 %collective-permute-done.1.bot = bf16[13,32,128]{2,1,0:T(8,128)(2,1)S(1)} collective-permute-done((bf16[13,32,128]{2,1,0:T(8,128)(2,1)S(1)}, bf16[13,32,128]{2,1,0:T(8,128)(2,1)S(1)}, u32[]{:S(2)}, u32[]{:S(2)}) %collective-permute-start.1) | collective-permute-done | bytes 106528 | tf_op jit(solution)/shard_map/ppermute | solution.py:590
  13.9 0.0 collective-permute-done.top
  13.9 0.0 copy-start.4
  14.0 5.5 %collective-permute-start.2 = (bf16[90,8,128]{2,1,0:T(8,128)(2,1)S(1)}, bf16[90,8,128]{2,1,0:T(8,128)(2,1)S(1)}, u32[]{:S(2)}, u32[]{:S(2)}) collective-permute-start(bf16[90,8,128]{2,1,0:T(8,128)(2,1)S(1)} %pad_maximum_fusion), channel_id=1, source_target_pairs={{0,1},{1,2},{2,3},{3,4},{4,5},{5,6},{6,7},{7,8},{8,9},{9,10},{10,1... | collective-permute-start | bytes 552968 | tf_op jit(solution)/shard_map/ppermute | solution.py:610
  19.5 1.9 %collective-permute-start.3 = (bf16[90,8,128]{2,1,0:T(8,128)(2,1)S(1)}, bf16[90,8,128]{2,1,0:T(8,128)(2,1)S(1)}, u32[]{:S(2)}, u32[]{:S(2)}) collective-permute-start(bf16[90,8,128]{2,1,0:T(8,128)(2,1)S(1)} %pad_maximum_fusion.1), channel_id=1, source_target_pairs={{1,0},{2,1},{3,2},{4,3},{5,4},{6,5},{7,6},{8,7},{9,8},{10,9},{11,1... | collective-permute-start | bytes 552968 | tf_op jit(solution)/shard_map/ppermute | solution.py:611
  21.5 0.0 copy-done.9
  21.5 0.6 pad.51.w_out
  22.1 0.6 pad_add_fusion.where
  22.7 0.0 collective-permute-done.2.left
  22.7 3.7 %collective-permute-done.3.right = bf16[90,8,128]{2,1,0:T(8,128)(2,1)S(1)} collective-permute-done((bf16[90,8,128]{2,1,0:T(8,128)(2,1)S(1)}, bf16[90,8,128]{2,1,0:T(8,128)(2,1)S(1)}, u32[]{:S(2)}, u32[]{:S(2)}) %collective-permute-start.3) | collective-permute-done | bytes 184352 | tf_op jit(solution)/shard_map/ppermute | solution.py:611
  26.4 0.0 copy-done.5
  26.4 0.0 copy-done.4
  26.4 0.0 copy-done.6
  26.4 0.0 copy-start.7
  26.4 0.7 copy-done.7
  27.1 15.6 %shard_map.145 = (bf16[32,32,384]{2,1,0:T(8,128)(2,1)}, f32[1024,128]{1,0:T(8,128)}, bf16[88,48,128]{2,1,0:T(8,128)(2,1)}) custom-call(s32[2]{0:T(128)} %pad_add_fusion.where, bf16[13,32,128]{2,1,0:T(8,128)(2,1)} %copy-done.4, bf16[64,32,128]{2,1,0:T(8,128)(2,1)} %bitcast.46, bf16[13,32,128]{2,1,0:T(8,128)(2,1)} %copy-done.5, bf16[90,8,128]{2,1,0:T(8,128)(2,1)} %copy-done.6, ...), custom_call_target="tpu_custom_call" | custom-call | tf_op jit(solution)/shard_map/pallas_call | solution.py:445
  42.7 0.0 copy-start.10
  42.7 0.0 copy-start.12
  42.7 0.0 copy-start.8
  42.7 9.8 %all-to-all-start = ((bf16[32,32,384]{2,1,0:T(8,128)(2,1)}), bf16[32,32,384]{2,1,0:T(8,128)(2,1)S(1)}, u32[]{:S(2)}, u32[]{:S(2)}) async-start(bf16[32,32,384]{2,1,0:T(8,128)(2,1)} %get-tuple-element.8), calls=%async_computation | async-start | bytes 1572864 | tf_op jit(solution)/shard_map/all_to_all | solution.py:617
  52.6 0.0 copy-done.3
  52.6 0.1 fusion.9
  52.6 1.9 %collective-permute-start.5 = (bf16[6,3,32]{0,2,1:T(8,128)(2,1)S(1)}, bf16[6,3,32]{0,2,1:T(8,128)(2,1)S(1)}, u32[]{:S(2)}, u32[]{:S(2)}) collective-permute-start(bf16[6,3,32]{0,2,1:T(8,128)(2,1)S(1)} %get-tuple-element.22), channel_id=1, source_target_pairs={{32,0},{64,32},{96,64},{128,96},{160,128},{192,160},{224,192},{33,... | collective-permute-start | bytes 3464 | tf_op jit(solution)/shard_map/ppermute | solution.py:590
  54.6 7.0 %collective-permute-start.4 = (bf16[6,3,32]{0,2,1:T(8,128)(2,1)S(1)}, bf16[6,3,32]{0,2,1:T(8,128)(2,1)S(1)}, u32[]{:S(2)}, u32[]{:S(2)}) collective-permute-start(bf16[6,3,32]{0,2,1:T(8,128)(2,1)S(1)} %get-tuple-element.21), channel_id=1, source_target_pairs={{0,32},{32,64},{64,96},{96,128},{128,160},{160,192},{192,224},{1,3... | collective-permute-start | bytes 3464 | tf_op jit(solution)/shard_map/ppermute | solution.py:589
  61.5 0.0 copy-done.11
  61.6 0.7 copy.46.anchors
  62.2 0.0 copy-done.10
  62.3 0.0 copy-done.12
  62.3 0.7 copy.47.score
  63.0 0.0 copy-done.8
  63.0 0.7 fusion.4
  63.7 9.9 %all-to-all-done = bf16[32,32,384]{2,1,0:T(8,128)(2,1)S(1)} async-done(((bf16[32,32,384]{2,1,0:T(8,128)(2,1)}), bf16[32,32,384]{2,1,0:T(8,128)(2,1)S(1)}, u32[]{:S(2)}, u32[]{:S(2)}) %all-to-all-start) | async-done | bytes 786464 | tf_op jit(solution)/shard_map/all_to_all | solution.py:617
  73.6 0.9 copy-done
  74.5 17.0 %shard_map.146 = bf16[32,40,256]{2,1,0:T(8,128)(2,1)} custom-call(s32[2]{0:T(128)} %pad_add_fusion.where, s32[64,2]{1,0:T(8,128)} %copy.46.anchors, s32[64]{0:T(128)} %bitcast.65, bf16[1024,384]{1,0:T(8,128)(2,1)} %bitcast.48, bf16[256,384]{1,0:T(8,128)(2,1)} %constant.24.clone.pick, bf16[4,352,192]{2,1,0:T(8,128)(2,1)} %constant.25.clone.rows_of, ...), custom_call_target="tpu_custom_call" | custom-call | tf_op jit(solution)/shard_map/pallas_call | solution.py:445
  91.5 21.4 %all-to-all-start.1 = ((bf16[32,40,256]{2,1,0:T(8,128)(2,1)}), bf16[32,40,256]{2,1,0:T(8,128)(2,1)S(1)}, u32[]{:S(2)}, u32[]{:S(2)}) async-start(bf16[32,40,256]{2,1,0:T(8,128)(2,1)} %shard_map.146), calls=%async_computation.1 | async-start | bytes 1310720 | tf_op jit(solution)/shard_map/all_to_all | solution.py:628
  112.9 0.1 copy.49
  113.1 0.1 fusion.5
  113.2 0.5 broadcast_multiply_fusion
  113.7 0.0 collective-permute-done.5
  113.8 0.0 collective-permute-done.4
  113.8 0.1 pad_maximum_fusion.5
  113.9 2.3 %collective-permute-start.7 = (bf16[76,3,6]{0,2,1:T(8,128)(2,1)S(1)}, bf16[76,3,6]{0,2,1:T(8,128)(2,1)S(1)}, u32[]{:S(2)}, u32[]{:S(2)}) collective-permute-start(bf16[76,3,6]{0,2,1:T(8,128)(2,1)S(1)} %get-tuple-element.20), channel_id=1, source_target_pairs={{1,0},{2,1},{3,2},{4,3},{5,4},{6,5},{7,6},{8,7},{9,8},{10,9},{11,1... | collective-permute-start | bytes 8216 | tf_op jit(solution)/shard_map/ppermute | solution.py:590
  116.1 3.3 %collective-permute-start.6 = (bf16[76,3,6]{0,2,1:T(8,128)(2,1)S(1)}, bf16[76,3,6]{0,2,1:T(8,128)(2,1)S(1)}, u32[]{:S(2)}, u32[]{:S(2)}) collective-permute-start(bf16[76,3,6]{0,2,1:T(8,128)(2,1)S(1)} %get-tuple-element.19), channel_id=1, source_target_pairs={{0,1},{1,2},{2,3},{3,4},{4,5},{5,6},{6,7},{7,8},{8,9},{9,10},{10,1... | collective-permute-start | bytes 8216 | tf_op jit(solution)/shard_map/ppermute | solution.py:589
  119.4 0.5 pad_bitcast_fusion.weights
  119.9 0.6 pad.56
  120.6 1.1 mul.26.w_second
  121.7 0.2 copy.53
  121.8 0.2 pad.57.clone
  122.0 0.8 copy.57
  122.8 0.6 pad.59.w_last
  123.4 0.6 pad.61
  124.0 5.5 %collective-permute-done.7 = bf16[76,3,6]{0,2,1:T(8,128)(2,1)S(1)} collective-permute-done((bf16[76,3,6]{0,2,1:T(8,128)(2,1)S(1)}, bf16[76,3,6]{0,2,1:T(8,128)(2,1)S(1)}, u32[]{:S(2)}, u32[]{:S(2)}) %collective-permute-start.7) | collective-permute-done | bytes 2768 | tf_op jit(solution)/shard_map/ppermute | solution.py:590
  129.5 0.0 collective-permute-done.6
  129.5 0.1 pad_maximum_fusion.2
  129.6 0.1 copy.48
  129.8 0.9 bitcast_convert_fusion.tgt
  130.6 27.8 %shard_map.147.lpips = f32[544,128]{1,0:T(8,128)} custom-call(s32[2]{0:T(128)} %pad_add_fusion.where, f32[1024,128]{1,0:T(8,128)} %get-tuple-element.9.dec, f32[608,128]{1,0:T(8,128)} %bitcast_convert_fusion.tgt, bf16[96,128]{1,0:T(8,128)(2,1)} %bitcast.58, bf16[384,384]{1,0:T(8,128)(2,1)} %mul.26.w_second, bf16[384,384]{1,0:T(8,128)(2,1)} %bitcast.50, ...), custom_call_target="tpu_custom_call" | custom-call | tf_op jit(solution)/shard_map/pallas_call | solution.py:445
  158.5 0.0 all-to-all-done.1.parts
  158.5 0.8 copy-done.1
  159.3 14.5 %shard_map.148 = bf16[64,32,128]{2,1,0:T(8,128)(2,1)} custom-call(s32[2]{0:T(128)} %pad_add_fusion.where, bf16[32,40,256]{2,1,0:T(8,128)(2,1)} %copy-done.1, f32[544,128]{1,0:T(8,128)} %shard_map.147.lpips, bf16[88,48,128]{2,1,0:T(8,128)(2,1)} %get-tuple-element.10.slope, bf16[64,32,128]{2,1,0:T(8,128)(2,1)} %bitcast.47, bf16[3,3,128,128]{3,2,1,0:T(8,128)(2,1)} %w_mid.3, ...), custom_call_target="tpu_custom_call" | custom-call | tf_op jit(solution)/shard_map/pallas_call | solution.py:445
  (27 shorter events, 0.2 us)
Async XLA Ops:
  0.0 21.5 %copy-start.9 = (bf16[3,3,128,3]{2,3,1,0:T(4,128)(2,1)S(1)}, bf16[3,3,128,3]{2,3,1,0:T(4,128)(2,1)}, u32[]{:S(2)}) copy-start(bf16[3,3,128,3]{2,3,1,0:T(4,128)(2,1)} %param.17) | copy-start | bytes 20740
  1.0 12.9 %collective-permute-start = (bf16[13,32,128]{2,1,0:T(8,128)(2,1)S(1)}, bf16[13,32,128]{2,1,0:T(8,128)(2,1)S(1)}, u32[]{:S(2)}, u32[]{:S(2)}) collective-permute-start(bf16[13,32,128]{2,1,0:T(8,128)(2,1)S(1)} %get-tuple-element.14), channel_id=1, source_target_pairs={{0,32},{32,64},{64,96},{96,128},{128,160},{160,192},{192,224},{1,3... | collective-permute-start | bytes 319496 | tf_op jit(solution)/shard_map/ppermute | solution.py:589
  4.8 9.1 %collective-permute-start.1 = (bf16[13,32,128]{2,1,0:T(8,128)(2,1)S(1)}, bf16[13,32,128]{2,1,0:T(8,128)(2,1)S(1)}, u32[]{:S(2)}, u32[]{:S(2)}) collective-permute-start(bf16[13,32,128]{2,1,0:T(8,128)(2,1)S(1)} %get-tuple-element.13), channel_id=1, source_target_pairs={{32,0},{64,32},{96,64},{128,96},{160,128},{192,160},{224,192},{33,... | collective-permute-start | bytes 319496 | tf_op jit(solution)/shard_map/ppermute | solution.py:590
  13.9 12.5 %copy-start.5 = (bf16[13,32,128]{2,1,0:T(8,128)(2,1)}, bf16[13,32,128]{2,1,0:T(8,128)(2,1)S(1)}, u32[]{:S(2)}) copy-start(bf16[13,32,128]{2,1,0:T(8,128)(2,1)S(1)} %collective-permute-done.1.bot) | copy-start | bytes 319492
  13.9 12.5 %copy-start.4 = (bf16[13,32,128]{2,1,0:T(8,128)(2,1)}, bf16[13,32,128]{2,1,0:T(8,128)(2,1)S(1)}, u32[]{:S(2)}) copy-start(bf16[13,32,128]{2,1,0:T(8,128)(2,1)S(1)} %collective-permute-done.top) | copy-start | bytes 319492
  14.0 8.7 %collective-permute-start.2 = (bf16[90,8,128]{2,1,0:T(8,128)(2,1)S(1)}, bf16[90,8,128]{2,1,0:T(8,128)(2,1)S(1)}, u32[]{:S(2)}, u32[]{:S(2)}) collective-permute-start(bf16[90,8,128]{2,1,0:T(8,128)(2,1)S(1)} %pad_maximum_fusion), channel_id=1, source_target_pairs={{0,1},{1,2},{2,3},{3,4},{4,5},{5,6},{6,7},{7,8},{8,9},{9,10},{10,1... | collective-permute-start | bytes 552968 | tf_op jit(solution)/shard_map/ppermute | solution.py:610
  19.5 6.9 %collective-permute-start.3 = (bf16[90,8,128]{2,1,0:T(8,128)(2,1)S(1)}, bf16[90,8,128]{2,1,0:T(8,128)(2,1)S(1)}, u32[]{:S(2)}, u32[]{:S(2)}) collective-permute-start(bf16[90,8,128]{2,1,0:T(8,128)(2,1)S(1)} %pad_maximum_fusion.1), channel_id=1, source_target_pairs={{1,0},{2,1},{3,2},{4,3},{5,4},{6,5},{7,6},{8,7},{9,8},{10,9},{11,1... | collective-permute-start | bytes 552968 | tf_op jit(solution)/shard_map/ppermute | solution.py:611
  22.7 3.7 %copy-start.6 = (bf16[90,8,128]{2,1,0:T(8,128)(2,1)}, bf16[90,8,128]{2,1,0:T(8,128)(2,1)S(1)}, u32[]{:S(2)}) copy-start(bf16[90,8,128]{2,1,0:T(8,128)(2,1)S(1)} %collective-permute-done.2.left) | copy-start | bytes 552964
  26.4 0.7 copy-start.7
  42.7 9.9 %copy-start.3 = (bf16[1,64,32,3]{1,2,3,0:T(8,128)(2,1)S(1)}, bf16[1,64,32,3]{1,2,3,0:T(8,128)(2,1)}, u32[]{:S(2)}) copy-start(bf16[1,64,32,3]{1,2,3,0:T(8,128)(2,1)} %param.18) | copy-start | bytes 36868
  42.7 18.9 %copy-start.11 = (s32[1,64,2]{1,2,0:T(2,128)S(1)}, s32[1,64,2]{1,2,0:T(2,128)}, u32[]{:S(2)}) copy-start(s32[1,64,2]{1,2,0:T(2,128)} %param.22) | copy-start | bytes 1540
  42.7 19.6 %copy-start.10 = (bf16[1,4,4,3,64]{4,2,3,1,0:T(4,128)(2,1)S(1)}, bf16[1,4,4,3,64]{4,2,3,1,0:T(4,128)(2,1)}, u32[]{:S(2)}) copy-start(bf16[1,4,4,3,64]{4,2,3,1,0:T(4,128)(2,1)} %param.24) | copy-start | bytes 18436
  42.7 19.6 %copy-start.12 = (bf16[1,128]{1,0:T(2,128)(2,1)S(1)}, bf16[1,128]{1,0:T(2,128)(2,1)}, u32[]{:S(2)}) copy-start(bf16[1,128]{1,0:T(2,128)(2,1)} %param.26) | copy-start | bytes 772
  42.7 20.3 %copy-start.8 = (bf16[3,3,3,64]{3,2,1,0:T(4,128)(2,1)S(1)}, bf16[3,3,3,64]{3,2,1,0:T(4,128)(2,1)}, u32[]{:S(2)}) copy-start(bf16[3,3,3,64]{3,2,1,0:T(4,128)(2,1)} %param.19) | copy-start | bytes 10372
  42.7 30.9 %all-to-all-start = ((bf16[32,32,384]{2,1,0:T(8,128)(2,1)}), bf16[32,32,384]{2,1,0:T(8,128)(2,1)S(1)}, u32[]{:S(2)}, u32[]{:S(2)}) async-start(bf16[32,32,384]{2,1,0:T(8,128)(2,1)} %get-tuple-element.8), calls=%async_computation | async-start | bytes 1572864 | tf_op jit(solution)/shard_map/all_to_all | solution.py:617
  52.6 61.1 %collective-permute-start.5 = (bf16[6,3,32]{0,2,1:T(8,128)(2,1)S(1)}, bf16[6,3,32]{0,2,1:T(8,128)(2,1)S(1)}, u32[]{:S(2)}, u32[]{:S(2)}) collective-permute-start(bf16[6,3,32]{0,2,1:T(8,128)(2,1)S(1)} %get-tuple-element.22), channel_id=1, source_target_pairs={{32,0},{64,32},{96,64},{128,96},{160,128},{192,160},{224,192},{33,... | collective-permute-start | bytes 3464 | tf_op jit(solution)/shard_map/ppermute | solution.py:590
  54.6 59.2 %collective-permute-start.4 = (bf16[6,3,32]{0,2,1:T(8,128)(2,1)S(1)}, bf16[6,3,32]{0,2,1:T(8,128)(2,1)S(1)}, u32[]{:S(2)}, u32[]{:S(2)}) collective-permute-start(bf16[6,3,32]{0,2,1:T(8,128)(2,1)S(1)} %get-tuple-element.21), channel_id=1, source_target_pairs={{0,32},{32,64},{64,96},{96,128},{128,160},{160,192},{192,224},{1,3... | collective-permute-start | bytes 3464 | tf_op jit(solution)/shard_map/ppermute | solution.py:589
  73.6 0.9 copy-start
  91.4 21.5 %copy-start.2 = (bf16[3,3,64,64]{3,2,1,0:T(8,128)(2,1)S(1)}, bf16[3,3,64,64]{3,2,1,0:T(8,128)(2,1)}, u32[]{:S(2)}) copy-start(bf16[3,3,64,64]{3,2,1,0:T(8,128)(2,1)} %param.20) | copy-start | bytes 221188
  91.5 21.7 %copy-start.13 = (f32[64]{0:T(128)S(1)}, f32[64]{0:T(128)}, u32[]{:S(2)}) copy-start(f32[64]{0:T(128)} %param.21) | copy-start | bytes 772
  91.5 67.0 %all-to-all-start.1 = ((bf16[32,40,256]{2,1,0:T(8,128)(2,1)}), bf16[32,40,256]{2,1,0:T(8,128)(2,1)S(1)}, u32[]{:S(2)}, u32[]{:S(2)}) async-start(bf16[32,40,256]{2,1,0:T(8,128)(2,1)} %shard_map.146), calls=%async_computation.1 | async-start | bytes 1310720 | tf_op jit(solution)/shard_map/all_to_all | solution.py:628
  113.9 15.7 %collective-permute-start.7 = (bf16[76,3,6]{0,2,1:T(8,128)(2,1)S(1)}, bf16[76,3,6]{0,2,1:T(8,128)(2,1)S(1)}, u32[]{:S(2)}, u32[]{:S(2)}) collective-permute-start(bf16[76,3,6]{0,2,1:T(8,128)(2,1)S(1)} %get-tuple-element.20), channel_id=1, source_target_pairs={{1,0},{2,1},{3,2},{4,3},{5,4},{6,5},{7,6},{8,7},{9,8},{10,9},{11,1... | collective-permute-start | bytes 8216 | tf_op jit(solution)/shard_map/ppermute | solution.py:590
  116.1 13.4 %collective-permute-start.6 = (bf16[76,3,6]{0,2,1:T(8,128)(2,1)S(1)}, bf16[76,3,6]{0,2,1:T(8,128)(2,1)S(1)}, u32[]{:S(2)}, u32[]{:S(2)}) collective-permute-start(bf16[76,3,6]{0,2,1:T(8,128)(2,1)S(1)} %get-tuple-element.19), channel_id=1, source_target_pairs={{0,1},{1,2},{2,3},{3,4},{4,5},{5,6},{6,7},{7,8},{8,9},{9,10},{10,1... | collective-permute-start | bytes 8216 | tf_op jit(solution)/shard_map/ppermute | solution.py:589
  158.5 0.8 copy-start.1
where the time goes:
time: 175 us; the launch traced here: 174 us
  Pallas kernels  74.8 us (43%)
  starting transfers between devices  58.9 us (34%)
  waiting for transfers between devices  25.2 us (14%)
  local copies, waits for them, and re-layouts  11.5 us (7%)
  other arithmetic  3 us (2%)
    pallas_call x4, Pallas kernels, call(): pl.pallas_call(kernel, in_specs=specs, out_specs=jax.tree.map(lambda _: p...  74.8 us
    all_to_all x1, starting transfers between devices, local(): lax.all_to_all(grads, 'col', split_axis=0, concat_axis=0, tiled=True)  21.4 us
    ppermute x3, starting transfers between devices, neighbours(): lax.ppermute(lax.slice_in_dim(block, size - width, size, axis=dim), axis,...  14.1 us
    ppermute x3, waiting for transfers between devices, neighbours(): lax.ppermute(lax.slice_in_dim(block, 0, width, axis=dim), axis, backward)  11.7 us
    all_to_all x1, waiting for transfers between devices, local(): strip = lax.all_to_all(pay, 'col', split_axis=0, concat_axis=0, tiled=True)  9.86 us
    all_to_all x1, starting transfers between devices, local(): strip = lax.all_to_all(pay, 'col', split_axis=0, concat_axis=0, tiled=True)  9.85 us
    ppermute x3, starting transfers between devices, neighbours(): lax.ppermute(lax.slice_in_dim(block, 0, width, axis=dim), axis, backward)  6.09 us
    ppermute x1, starting transfers between devices, local(): left = lax.ppermute(edge(TW - COL_HALO, TW), 'col', forward)  5.54 us
  transfers between devices with their start and end apart: 10, of which 4 were waited for; matrix products, arithmetic and copies ran while one was open for 6% of the time, Pallas kernels for 26%

commit v1 on v0

v1 whole, which is shorter than its diff:
```python
import jax
import jax.numpy as jnp
import numpy as np
from jax import lax
from jax.experimental import pallas as pl
from jax.experimental.pallas import tpu as pltpu
from jax.sharding import PartitionSpec as P

BF = jnp.bfloat16
F32 = jnp.float32

LOSS_SCALE = 32.0
EPSILON = 1e-06
CROP = 256
TH, TW = 64, 32
IMG_H, IMG_W = 512, 1024
ROWS, COLS = 8, 32
CROPS = 64
DEC_HALO = 11
FEAT_HALO = 13
COL_HALO = 8
WIDE = TW + 2 * COL_HALO
TGT_HALO = 6
GRAD_PAD = 10
SHARE = 34
VMEM = 56 * 1024 * 1024


def sigmoid(v):
    return 0.5 * jnp.tanh(0.5 * v) + 0.5


def silu_parts(v):
    sig = sigmoid(v)
    act = v * sig
    return act, sig + act * (1.0 - sig)


def mm(a, b, ca=1, cb=0):
    return lax.dot_general(a, b, (((ca,), (cb,)), ((), ())), preferred_element_type=F32)


def iota(shape, dim):
    return lax.broadcasted_iota(jnp.int32, shape, dim)


def aligned(start, unit):
    return pl.multiple_of(start, unit) if not isinstance(start, int) else start


def conv_rows(src, row0, rows, weight, transposed=False, shift=0):
    n = rows * WIDE
    lhs = jnp.concatenate(
        [src[pl.ds(aligned((row0 + dy) * WIDE, 16), n), :] for dy in range(3)], axis=1
    )
    z = mm(lhs, weight, 1, 1 if transposed else 0)
    parts = []
    for dx in range(3):
        amount = (1 - dx - shift) % n
        part = z[:, dx * 128 : (dx + 1) * 128]
        parts.append(pltpu.roll(part, amount, 0) if amount else part)
    return parts[0] + parts[1] + parts[2]


def column_mask(col_first):
    x = col_first + iota((1, WIDE, 128), 1)
    return ((x >= 0) & (x < IMG_W)).astype(F32)


def keep_inside(v, row_first, rows, col_ok):
    y = row_first + iota((rows, 1, 128), 0)
    row_ok = ((y >= 0) & (y < IMG_H)).astype(F32)
    return (v.reshape(rows, WIDE, 128) * (col_ok * row_ok)).reshape(rows * WIDE, 128)


def planar_inside(row_first, col_first, low, high, rows, limit):
    lane = iota((rows * 8, 128), 1)
    row = iota((rows * 8, 128), 0) >> 3
    x = col_first + lane
    y = row_first + row
    ok = (x >= 0) & (x < IMG_W) & (lane >= low) & (lane < high) & (y >= 0) & (y < IMG_H)
    return ok & (row < limit)


def taller(v):
    return jnp.concatenate([v, jnp.zeros((128 - v.shape[0], 128), F32)], axis=0)


def colour_weights(w, small):
    k = iota((32, 384), 0)
    n = iota((32, 384), 1)
    copies = (((n >> 7) * 8 + (n & 7)) == k).astype(F32).astype(BF)
    for dy in range(3):
        w[dy * 128 : (dy + 1) * 128, :] = mm(small(dy).astype(BF), copies, 0, 0).astype(BF)


def to_colours(src, first, w):
    group = iota((WIDE, 128), 1) >> 3
    tile = jnp.zeros((WIDE, 128), F32)
    for half in range(2):
        v = conv_rows(src, first + half * 8, 8, w[...])
        for k in range(8):
            tile = jnp.where(group == half * 8 + k, v[k * WIDE : (k + 1) * WIDE], tile)
    return taller(tile).T


def patch_tile(v):
    after, before = pltpu.roll(v, 1, 1), pltpu.roll(v, 127, 1)
    none = jnp.zeros((8, 128), F32)
    parts = []
    for k in range(4):
        at = slice(k * 8, (k + 1) * 8)
        parts += [after[at], v[at], before[at], none]
    return jnp.concatenate(parts, axis=0).T[0:WIDE].astype(BF)


def patch_weights(w, small):
    w[...] = jnp.zeros(w.shape, BF)
    for k in range(4):
        for dy in range(3):
            w[(k + dy) * 32 : (k + dy + 1) * 32, k * 128 : (k + 1) * 128] = small(dy).astype(BF)


def from_colours(px, tile, count, w):
    at = [pl.ds(aligned((tile + k) * WIDE, 16), count * WIDE) for k in range(2)]
    return mm(jnp.concatenate([px[at[0], :], px[at[1], :]], axis=1), w[...])


def decode_kernel(
    where, top, mid, bot, left, right, w_mid, w_out, pay, dec, slope_out, s1, s2, w, w3
):
    r, c = where[0], where[1]
    for dy in range(3):
        for dx in range(3):
            w[dy * 128 : (dy + 1) * 128, dx * 128 : (dx + 1) * 128] = w_mid[dy, dx]
    colour_weights(w3, lambda dy: w_out[dy])

    def fill(first, rows, centre):
        n = rows * WIDE
        parts = [left[pl.ds(first, rows)], centre, right[pl.ds(first, rows)]]
        v = jnp.concatenate([p.astype(F32) for p in parts], axis=1).reshape(n, 128)
        s1[pl.ds(aligned(first * WIDE, 16), n), :] = (v * sigmoid(v)).astype(BF)

    fill(0, FEAT_HALO, top[0:FEAT_HALO])
    fill(FEAT_HALO + TH, FEAT_HALO, bot[0:FEAT_HALO])

    def fill_mid(i, carry):
        fill(FEAT_HALO + i * 8, 8, mid[pl.ds(i * 8, 8)])
        return carry

    lax.fori_loop(0, TH // 8, fill_mid, 0, unroll=2)
    col_ok = column_mask(c * TW - COL_HALO)

    def middle(i, carry):
        v = conv_rows(s1, i * 8, 8, w[...])
        act, slope = silu_parts(v)
        act = keep_inside(act, r * TH - 12 + i * 8, 8, col_ok)
        s2[pl.ds(aligned(i * 8 * WIDE, 16), 8 * WIDE), :] = act.astype(BF)
        slope_out[pl.ds(i * 8, 8)] = (
            pltpu.roll(slope, 8 * WIDE - 6, 0).reshape(8, WIDE, 128).astype(BF)
        )
        return carry

    lax.fori_loop(0, 11, middle, 0, unroll=True)
    s2[88 * WIDE :, :] = jnp.zeros((10 * WIDE, 128), BF)
    dec[768:, :] = jnp.zeros((256, 128), F32)

    def colours(i, carry):
        v = to_colours(s2, i * 16, w3)
        ok = planar_inside(
            r * TH - DEC_HALO + i * 16, c * TW - COL_HALO, 2, WIDE - 2, 16, 86 - i * 16
        )
        dec[pl.ds(aligned(i * 128, 128), 128), :] = jnp.where(ok, v, 0.0).astype(BF).astype(F32)
        return carry

    lax.fori_loop(0, 6, colours, 0, unroll=True)
    planes = [
        dec[pl.ds(k, 128, stride=8), :].T[COL_HALO : COL_HALO + TW, :] for k in range(3)
    ]
    upper = iota((16, 128), 1) >= 64
    for half in range(2):
        low, high = [], []
        for x in range(2):
            for p in planes:
                p = p[x * 16 : (x + 1) * 16]
                start = half * SHARE
                low.append(pltpu.roll(p, 128 - start, 1) if start else p)
                high.append(pltpu.roll(p, 64 - start, 1))
        packed = [jnp.where(upper, high[k + 1], low[k]) for k in (0, 2, 4)]
        packed = jnp.concatenate(packed, axis=1).astype(BF)
        for k in range(COLS // 2):
            pay[2 * k + half] = packed


def percept_kernel(
    where, dec, tall, left, right, v_first, v_second, weights, feat, slope_one,
    planes, px, one, w1, w2,
):
    r, c = where[0], where[1]
    col_first = c * TW - COL_HALO
    col_ok = column_mask(col_first)

    def first_small(dy):
        v = v_first[dy]
        return v + pltpu.roll(pltpu.roll(v, 3, 0), 64, 1)

    patch_weights(w1, first_small)
    for dy in range(3):
        for dx in range(3):
            v = v_second[dy, dx].astype(F32)
            v = jnp.concatenate([v, jnp.zeros((64, 64), F32)], axis=1)
            u = pltpu.roll(v, 64, 1)
            w2[dy * 128 : (dy + 1) * 128, dx * 128 : (dx + 1) * 128] = jnp.concatenate(
                [v, u], axis=0
            ).astype(BF)

    planes[...] = jnp.zeros(planes.shape, F32)
    for k in range(3):
        v = jnp.concatenate(
            [a.astype(F32) for a in (left[90 + k], tall[k], right[90 + k])], axis=0
        )
        planes[pl.ds(3 + k, 80, stride=8), :] = taller(v).T[0:80]

    def gather(i, carry):
        v = dec[pl.ds(aligned(i * 32 + 40, 8), 32), :] + planes[pl.ds(aligned(i * 32, 32), 32), :]
        px[pl.ds(aligned(i * WIDE, 16), WIDE), :] = patch_tile(v)
        return carry

    lax.fori_loop(0, 19, gather, 0, unroll=True)
    px[19 * WIDE :, :] = jnp.zeros((WIDE, 128), BF)

    def first(tile, count):
        v = from_colours(px, tile, count, w1)
        for j in range(count):
            for k in range(4):
                p = (tile + j) * 4 + k
                x = v[j * WIDE : (j + 1) * WIDE, k * 128 : (k + 1) * 128]
                act, slope = silu_parts(x)
                act = keep_inside(act, r * TH - 5 + p, 1, col_ok)
                slope_one[pl.ds(aligned(p * WIDE, 16), WIDE), :] = slope.astype(BF)
                one[pl.ds(aligned(p * WIDE, 16), WIDE), :] = act.astype(BF)

    def first_group(i, carry):
        first(i * 4, 4)
        return carry

    lax.fori_loop(0, 4, first_group, 0, unroll=True)
    first(16, 3)
    ones = ((iota((128, 128), 0) >> 6) == (iota((128, 128), 1) >> 6)).astype(F32).astype(BF)

    def half_sum(v):
        high = v.astype(BF)
        low = (v - high.astype(F32)).astype(BF)
        return mm(high, ones) + mm(low, ones)

    def second(i, carry):
        v = conv_rows(one, i * 8, 8, w2[...])
        f, slope = silu_parts(v)
        scale = lax.rsqrt(half_sum(f * f) + EPSILON)
        unit = f * scale
        weighted = weights[...] * (unit - pltpu.roll(unit, 64, 1))
        g = scale * (weighted - unit * half_sum(weighted * unit)) * slope
        g = keep_inside(g, r * TH - 4 + i * 8, 8, col_ok)
        feat[pl.ds(aligned(i * 8 * WIDE, 16), 8 * WIDE), :] = g.astype(BF)
        return carry

    lax.fori_loop(0, 9, second, 0, unroll=3)


def percept_back_kernel(where, feat, slope_one, v_first, v_second, out, bv, w3, w4):
    r, c = where[0], where[1]
    col_ok = column_mask(c * TW - COL_HALO)

    def last_small(dy):
        parts = [v_first[2 - dy, (2 - dx) * 8 : (3 - dx) * 8, :] for dx in range(3)]
        return jnp.concatenate(parts + [jnp.zeros((8, 128), F32)], axis=0)

    colour_weights(w4, last_small)
    for dy in range(3):
        for dx in range(3):
            v = v_second[dy, dx].astype(F32)
            v = jnp.concatenate([v, jnp.zeros((64, 64), F32)], axis=1)
            w3[(2 - dx) * 128 : (3 - dx) * 128, (2 - dy) * 128 : (3 - dy) * 128] = jnp.concatenate(
                [v, jnp.zeros((64, 128), F32)], axis=0
            ).astype(BF)

    def back(i, carry):
        v = conv_rows(feat, i * 10, 10, w3[...], transposed=True)
        x = slope_one[pl.ds(aligned((i * 10 + 2) * WIDE, 16), 10 * WIDE), :]
        v = keep_inside(v * x.astype(F32), r * TH - 3 + i * 10, 10, col_ok)
        bv[pl.ds(aligned(i * 10 * WIDE, 16), 10 * WIDE), :] = v.astype(BF)
        return carry

    lax.fori_loop(0, 7, back, 0, unroll=True)
    bv[70 * WIDE :, :] = jnp.zeros((12 * WIDE, 128), BF)

    def colours(i, carry):
        v = to_colours(bv, i * 16, w4)
        out[pl.ds(aligned(i * 128, 128), 128), :] = pltpu.roll(v, 122, 1)
        return carry

    lax.fori_loop(0, 5, colours, 0, unroll=True)


STEPS = 6
HALF = STEPS + 1
TILES = 2 * HALF
LANES = TILES * 128
EVEN = HALF * 128


def critic_kernel(
    where, anchors, owners, strip, pick, rows_of, rows_back, mine, other, _, out,
    strip32, grads, w_pre, w_one, w_two, w_back, score, x_all, pre, act, two, cols,
):
    r, me = where[0], where[1]
    first_row = r * TH - 2 + SHARE * (me & 1)
    lane = iota((1, 128), 1)
    upper = lane >= 64
    first_x = (lane & 63) == 0
    last_x = (lane & 63) == 63

    def unpack(k, carry):
        v = strip[k].astype(F32)
        b, d = pltpu.roll(v[:, 128:256], 64, 1), pltpu.roll(v[:, 256:384], 64, 1)
        at = aligned(k * TW, 32)
        strip32[pl.ds(at, 16), :] = v[:, 0:256]
        strip32[pl.ds(at + 16, 16), :] = jnp.concatenate([jnp.where(upper, d, b), d], axis=1)
        return carry

    lax.fori_loop(0, COLS, unpack, 0, unroll=8)
    strip32[IMG_W:, :] = jnp.zeros((8, 256), F32)
    grads[...] = jnp.zeros(grads.shape, F32)
    w_back[...] = jnp.zeros(w_back.shape, BF)
    for g, source in enumerate((mine, other)):
        w_one[g] = source[1024:1120, :]
        w_pre[g] = taller(source[1024:1120, :].astype(F32)).T.astype(BF)
        score[g] = taller(source[1120:1136, :].astype(F32)).T
        for i in range(4):
            w_two[g, i] = jnp.concatenate(
                [
                    source[i * 256 + k * 128 : i * 256 + (k + 1) * 128, :].astype(F32).T
                    for k in range(2)
                ],
                axis=1,
            ).astype(BF)
        for par in range(2):
            for p in range(2):
                for t in range(2):
                    i = par + 2 * t
                    for kind, j in ((0, 1 + p), (1 + p, 3 - 3 * p)):
                        w_back[
                            g,
                            (par * 2 + p) * 64 : (par * 2 + p + 1) * 64,
                            (t * 3 + kind) * 128 : (t * 3 + kind + 1) * 128,
                        ] = source[i * 256 + j * 64 : i * 256 + (j + 1) * 64, :]
    two[:, 0:128] = jnp.zeros((384, 128), BF)
    two[:, (STEPS + 1) * 128 :] = jnp.zeros((384, 128), BF)
    cols[192:, :] = jnp.zeros((64, 384), F32)
    wide = iota((1, 256), 1)

    def score_crop(top, left, g):
        y0 = first_row - top
        v0 = lax.shift_right_arithmetic(y0 - 3, 2)
        e = 4 * v0 - y0 + 6
        crop_row = y0 - 9 + (wide & 63)
        in_crop = (crop_row >= 0) & (crop_row < CROP) & (wide < 192)
        window = strip32[pl.ds(aligned((left >> 3) * 8, 8), CROP + 8), :]
        window = pltpu.roll(window, lax.rem((CROP + 8) - (left & 7), CROP + 8), 0)[0:CROP]
        window = jnp.where(in_crop, window, 0.0).astype(BF)
        cols_of = mm(window, pick[...], 0, 0)
        none = jnp.zeros((8, 384), F32)
        halves = [
            jnp.concatenate(
                [cols_of[k * 64 + 24 * h : k * 64 + 24 * h + 40, :] for k in range(3)] + [none],
                axis=0,
            )
            for h in range(2)
        ]
        mixed = []
        for m in range(6):
            tile = slice((m // 2) * 128, (m // 2 + 1) * 128)
            low, high = halves[0][:, tile], halves[1][:, tile]
            if m % 2 == 0:
                high = pltpu.roll(high, 64, 1)
            else:
                low = pltpu.roll(low, 64, 1)
            mixed.append(jnp.where(upper, high, low))
        patches = mm(rows_of[e], jnp.concatenate(mixed, axis=1).astype(BF)).astype(BF)
        for t in range(TILES):
            for m in range(6):
                x_all[m * 16 : (m + 1) * 16, t * 128 : (t + 1) * 128] = patches[
                    t * 16 : (t + 1) * 16, m * 128 : (m + 1) * 128
                ]
        weight = w_pre[g][:, 0:96]
        for t0 in range(0, TILES, 2):
            at = slice(t0 * 128, (t0 + 2) * 128)
            value = mm(weight, x_all[:, at])
            for t in range(t0, t0 + 2):
                at = slice(t * 128, (t + 1) * 128)
                n = 2 * (t % HALF) + t // HALF + jnp.where(upper, 2 * STEPS, 0)
                u = 2 * v0 - 1 + n
                ok = ((u >= 0) & (u < CROP // 2)).astype(F32)
                a, slope = silu_parts(value[:, (t - t0) * 128 : (t - t0 + 1) * 128])
                a = a * ok
                pre[:, at] = slope * ok
                even, odd = a[:64], a[64:]
                act[0:64, at] = jnp.where(first_x, 0.0, pltpu.roll(odd, 1, 1)).astype(BF)
                act[64:128, at] = even.astype(BF)
                act[128:192, at] = odd.astype(BF)
                act[192:256, at] = jnp.where(last_x, 0.0, pltpu.roll(even, 127, 1)).astype(BF)
        column = score[g][:, 0:1]
        for t0 in range(0, STEPS, 2):
            value = None
            for i in range(4):
                start = (i % 2) * EVEN + (i // 2 + t0) * 128
                part = mm(w_two[g, i], act[:, start : start + 256])
                value = part if value is None else value + part
            for t in range(t0, t0 + 2):
                f, slope = silu_parts(value[:, (t - t0) * 128 : (t - t0 + 1) * 128])
                logit = jnp.sum(f * column, axis=0, keepdims=True)
                v = v0 + t + jnp.where(upper, STEPS, 0)
                ok = (v >= 0) & (v < CROP // 4)
                grad = jnp.where(ok, -LOSS_SCALE * sigmoid(-logit), 0.0)
                b = grad * (column * slope)
                at = slice((t + 1) * 128, (t + 2) * 128)
                two[0:128, at] = b.astype(BF)
                two[128:256, at] = jnp.where(first_x, 0.0, pltpu.roll(b, 1, 1)).astype(BF)
                two[256:384, at] = jnp.where(last_x, 0.0, pltpu.roll(b, 127, 1)).astype(BF)
        for s0 in range(0, HALF, 2):
            n = min(2, HALF - s0) * 128
            at = s0 * 128
            both = jnp.concatenate([two[:, 128 + at : 128 + at + n], two[:, at : at + n]], axis=0)
            up = mm(w_back[g], both)
            for par in range(2):
                here = slice(par * EVEN + at, par * EVEN + at + n)
                one = (up[par * 128 : (par + 1) * 128] * pre[:, here]).astype(BF)
                x_all[:, here] = mm(w_one[g], one).astype(BF)
        spread = jnp.concatenate(
            [
                jnp.concatenate(
                    [
                        x_all[m * 16 : (m + 1) * 16, t * 128 : (t + 1) * 128]
                        for t in range(TILES)
                    ],
                    axis=0,
                )
                for m in range(6)
            ],
            axis=1,
        )
        back = mm(rows_back[e], spread)
        parts = []
        for h in range(2):
            tiles = []
            for k in range(3):
                low = back[:, 2 * k * 128 : (2 * k + 1) * 128]
                high = back[:, (2 * k + 1) * 128 : (2 * k + 2) * 128]
                if h == 0:
                    high = pltpu.roll(high, 64, 1)
                else:
                    low = pltpu.roll(low, 64, 1)
                tiles.append(jnp.where(upper, high, low))
            parts.append(jnp.concatenate(tiles, axis=1))
        for k in range(3):
            low, high = (part[k * 40 : (k + 1) * 40, :] for part in parts)
            cols[k * 64 : (k + 1) * 64, :] = jnp.concatenate(
                [low[0:24], low[24:40] + high[0:16], high[16:40]], axis=0
            )
        placed = mm(pick[...], cols[...].astype(BF), 1, 1)
        y = wide & 63
        keep = in_crop & (y >= 9) & (y < 9 + SHARE)
        placed = jnp.concatenate([jnp.where(keep, placed, 0.0), jnp.zeros((8, 256), F32)], axis=0)
        start = left + GRAD_PAD
        here = pl.ds(aligned((start >> 3) * 8, 8), CROP + 8)
        grads[here, :] = grads[here, :] + pltpu.roll(placed, start & 7, 0)

    def one_crop(q, carry):
        top, left, owner = anchors[q, 0], anchors[q, 1], owners[q]
        y0 = first_row - top

        @pl.when(((owner >> 1) == (me >> 1)) & (y0 < CROP) & (y0 + SHARE > 0))
        def _():
            score_crop(top, left, (owner ^ me) & 1)

        return carry

    lax.fori_loop(0, CROPS, one_crop, 0)

    def pack(k, carry):
        block = grads[pl.ds(aligned(k * TW + 8, 8), 40), :]
        a, b = block[:, 0:128], block[:, 128:256]
        out[k] = jnp.where(
            lane < 40,
            pltpu.roll(a, 128 - 9, 1),
            jnp.where(lane < 80, pltpu.roll(a, 128 - 33, 1), pltpu.roll(b, 71, 1)),
        ).astype(BF)
        return carry

    lax.fori_loop(0, COLS, pack, 0, unroll=4)


def finish_kernel(
    where, parts, lpips, slope, feats, w_mid, w_out, out, turned, planes, px, bm, w, w1
):
    r, c = where[0], where[1]
    for dy in range(3):
        for dx in range(3):
            w[dx * 128 : (dx + 1) * 128, dy * 128 : (dy + 1) * 128] = w_mid[2 - dy, 2 - dx]

    def small(dy):
        flipped = [w_out[2 - dy, (2 - dx) * 8 : (3 - dx) * 8, :] for dx in range(3)]
        return jnp.concatenate(flipped + [jnp.zeros((8, 128), F32)], axis=0)

    patch_weights(w1, small)
    col_ok = column_mask(c * TW - 2)
    planes[...] = jnp.zeros(planes.shape, F32)
    for half in range(2):
        total = parts[half].astype(F32)
        for k in range(1, COLS // 2):
            total = total + parts[2 * k + half].astype(F32)
        turned[...] = taller(total).T
        for k in range(3):
            planes[pl.ds(half * SHARE * 8 + k, 40, stride=8), :] = turned[k * 40 : (k + 1) * 40, :]

    def gather(i, carry):
        at = pl.ds(aligned(i * 32, 32), 32)
        ok = planar_inside(r * TH - 2 + i * 4, c * TW - 2, 0, 36, 4, 4)
        px[pl.ds(aligned(i * WIDE, 16), WIDE), :] = patch_tile(
            jnp.where(ok, lpips[at, :] + planes[at, :], 0.0)
        )
        return carry

    lax.fori_loop(0, 17, gather, 0, unroll=True)
    px[17 * WIDE :, :] = jnp.zeros((WIDE, 128), BF)

    def middle(tile, count):
        v = from_colours(px, tile, count, w1)
        for j in range(count):
            for k in range(4):
                n = (tile + j) * 4 + k
                x = v[j * WIDE : (j + 1) * WIDE, k * 128 : (k + 1) * 128]
                x = keep_inside(x * slope[n + 11].astype(F32), r * TH - 1 + n, 1, col_ok)
                bm[pl.ds(aligned(n * WIDE, 16), WIDE), :] = x.astype(BF)

    def middle_group(i, carry):
        middle(i * 4, 4)
        return carry

    lax.fori_loop(0, 4, middle_group, 0, unroll=True)
    middle(16, 1)

    def last(i, carry):
        v = conv_rows(bm, i * 8, 8, w[...], transposed=True, shift=2)
        v = v.reshape(8, WIDE, 128)[:, 0:TW, :]
        x = feats[pl.ds(i * 8, 8)].astype(F32)
        out[pl.ds(i * 8, 8)] = (v * silu_parts(x)[1]).astype(BF)
        return carry

    lax.fori_loop(0, TH // 8, last, 0, unroll=4)


def call(kernel, outs, scratch, args, scalars=1, unused=0):
    specs = [pl.BlockSpec(memory_space=pltpu.SMEM)] * scalars
    specs += [pl.BlockSpec(memory_space=pltpu.VMEM)] * (len(args) - scalars - unused)
    specs += [pl.BlockSpec(memory_space=pl.ANY)] * unused
    return pl.pallas_call(
        kernel,
        in_specs=specs,
        out_specs=jax.tree.map(lambda _: pl.BlockSpec(memory_space=pltpu.VMEM), outs),
        out_shape=outs,
        scratch_shapes=[pltpu.VMEM(s, t) for s, t in scratch],
        compiler_params=pltpu.CompilerParams(vmem_limit_bytes=VMEM),
        interpret=INTERPRET,
    )(*args)


INTERPRET = False


def shape(dims, kind):
    return jax.ShapeDtypeStruct(dims, kind)


def row_tables():
    table = np.zeros((4, TILES, 16, 128), np.float32)
    for e in range(4):
        for t in range(TILES):
            u = 2 * (t % HALF) + t // HALF
            for i in range(4):
                for k in range(3):
                    table[e, t, i * 4 + k, k * 40 + 2 * u + i + e] = 1.0
    return table.reshape(4, TILES * 16, 128)


def column_table():
    table = np.zeros((CROP, 6, 64), np.float32)
    for m in range(6):
        for x in range(64):
            if 0 <= 4 * x + m - 1 < CROP:
                table[4 * x + m - 1, m, x] = 1.0
    return table.reshape(CROP, 384)


def colour_first(w):
    w = jnp.pad(w.astype(F32), ((0, 0), (0, 1), (0, 5), (0, 128 - w.shape[-1])))
    return w.reshape(3, 32, 128)


def decode(where, top, mid, bot, left, right, conv_mid, small):
    return call(
        decode_kernel,
        (
            shape((COLS, TW // 2, 384), BF),
            shape((1024, 128), F32),
            shape((88, WIDE, 128), BF),
        ),
        [((90 * WIDE, 128), BF), ((98 * WIDE, 128), BF), ((384, 384), BF), ((384, 384), BF)],
        (where, top, mid, bot, left, right, conv_mid, small),
    )


def percept(where, dec, tall, left, right, small, vgg_second, weights):
    scaled = jnp.pad(2.0 * LOSS_SCALE * weights, (0, 64)).reshape(1, 128)
    return call(
        percept_kernel,
        (shape((72 * WIDE, 128), BF), shape((76 * WIDE, 128), BF)),
        [
            ((80 * 8, 128), F32),
            ((20 * WIDE, 128), BF),
            ((76 * WIDE, 128), BF),
            ((256, 512), BF),
            ((384, 384), BF),
        ],
        (where, dec, tall, left, right, small, vgg_second, scaled),
    )


def percept_back(where, feat, slope_one, small, vgg_second):
    return call(
        percept_back_kernel,
        shape((80 * 8, 128), F32),
        [((82 * WIDE, 128), BF), ((384, 384), BF), ((384, 384), BF)],
        (where, feat, slope_one, small, vgg_second),
    )


def critic_weights(first, second, score):
    w = jnp.pad(first, ((0, 0), (0, 0), (0, 1), (0, 0)))
    w = jnp.transpose(w, (1, 0, 2, 3)).reshape(4, 16, 64)
    w = jnp.concatenate(
        [jnp.pad(w, ((0, 2), (0, 0), (0, 0))), jnp.pad(w, ((2, 0), (0, 0), (0, 0)))], -1
    ).reshape(96, 128)
    score = jnp.pad(score[None], ((0, 15), (0, 0)))
    return jnp.concatenate([second.reshape(1024, 128), w, score], 0)


def critics(where, anchors, owners, strip, mine, other, after):
    rows_of = row_tables()
    return call(
        critic_kernel,
        shape((COLS, 40, 128), BF),
        [
            ((IMG_W + 8, 256), F32),
            ((IMG_W + 24, 256), F32),
            ((2, 128, 128), BF),
            ((2, 96, 128), BF),
            ((2, 4, 128, 256), BF),
            ((2, 256, 768), BF),
            ((2, 128, 128), F32),
            ((96, LANES), BF),
            ((128, LANES), F32),
            ((256, LANES), BF),
            ((384, (STEPS + 2) * 128), BF),
            ((256, 384), F32),
        ],
        (
            where,
            anchors,
            owners,
            strip,
            jnp.asarray(column_table(), BF),
            jnp.asarray(rows_of, BF),
            jnp.asarray(np.swapaxes(rows_of, 1, 2), BF),
            mine,
            other,
            after,
        ),
        scalars=3,
        unused=1,
    )


def finish(where, parts, lpips, slope, feats, conv_mid, small):
    return call(
        finish_kernel,
        shape((TH, TW, 128), BF),
        [
            ((128, 128), F32),
            ((80 * 8, 128), F32),
            ((18 * WIDE, 128), BF),
            ((68 * WIDE, 128), BF),
            ((384, 384), BF),
            ((256, 512), BF),
        ],
        (where, parts, lpips, slope, feats, conv_mid, small),
    )


def exchange(low, high, axis):
    count = lax.axis_size(axis)
    forward = [(i, i + 1) for i in range(count - 1)]
    backward = [(target, source) for source, target in forward]
    return lax.ppermute(low, axis, forward), lax.ppermute(high, axis, backward)


def local(
    features, conv_mid, conv_out, target, vgg_first, vgg_second, perceptual_weights,
    crop_anchors, crop_owner, critic_first, critic_second, critic_score,
):
    where = jnp.stack([lax.axis_index("row"), lax.axis_index("col")]).astype(jnp.int32)
    feats = features[0]
    planar = jnp.transpose(target[0], (2, 1, 0))

    def row_part(rows, colours):
        colours = jnp.transpose(colours, (1, 0, 2)).reshape(TW, 3 * TGT_HALO)
        colours = jnp.pad(colours, ((0, 0), (0, 128 - 3 * TGT_HALO)))
        return jnp.concatenate([rows, colours[None]], 0)

    top, bot = exchange(
        row_part(feats[TH - FEAT_HALO :], planar[:, :, TH - TGT_HALO :]),
        row_part(feats[:FEAT_HALO], planar[:, :, :TGT_HALO]),
        "row",
    )

    def colours_of(part):
        part = part[FEAT_HALO, :, : 3 * TGT_HALO].reshape(TW, 3, TGT_HALO)
        return jnp.transpose(part, (1, 0, 2))

    tall = jnp.concatenate(
        [
            colours_of(top),
            planar,
            colours_of(bot),
            jnp.zeros((3, TW, 128 - TH - 2 * TGT_HALO), BF),
        ],
        2,
    )

    def edge(first, last):
        parts = (top[:FEAT_HALO], feats, bot[:FEAT_HALO], tall)
        return jnp.concatenate([a[:, first:last] for a in parts], 0)

    left, right = exchange(edge(TW - COL_HALO, TW), edge(0, COL_HALO), "col")
    out_small = colour_first(jnp.transpose(conv_out, (0, 1, 3, 2)))
    vgg_small = colour_first(vgg_first)
    pay, dec, slope = decode(where, top, feats, bot, left, right, conv_mid, out_small)
    strip = lax.all_to_all(pay, "col", split_axis=0, concat_axis=0, tiled=True)
    mine = critic_weights(critic_first[0], critic_second[0], critic_score[0])
    other = lax.ppermute(mine, "col", [(i, i ^ 1) for i in range(COLS)])
    feat, slope_one = percept(
        where, dec, tall, left, right, vgg_small, vgg_second, perceptual_weights
    )
    grads = critics(
        where,
        crop_anchors.reshape(CROPS, 2),
        crop_owner.reshape(CROPS),
        strip,
        mine,
        other,
        feat,
    )
    parts = lax.all_to_all(grads, "col", split_axis=0, concat_axis=0, tiled=True)
    lpips = percept_back(where, feat, slope_one, vgg_small, vgg_second)
    return finish(where, parts, lpips, slope, feats, conv_mid, out_small)[None]


def solution(mesh):
    placed = (
        P(None, "row", "col", None),
        P(),
        P(),
        P(None, "row", "col", None),
        P(),
        P(),
        P(),
        P(),
        P(),
        P("col", None, None, None, None),
        P("col", None, None, None, None),
        P("col", None),
    )
    return jax.shard_map(
        local, mesh=mesh, in_specs=placed, out_specs=P(None, "row", "col", None), check_vma=False
    )
```

time: 175 us -> 115 us (0.66)
  the two profiles are of different devices: /device:TPU:15 before, /device:TPU:6 now
where the time goes in v1:
time: 115 us; the launch traced here: 114 us
  Pallas kernels  44.2 us (38%)
  starting transfers between devices  40.5 us (35%)
  waiting for transfers between devices  20 us (17%)
  local copies, waits for them, and re-layouts  7.06 us (6%)
  other arithmetic  2.15 us (2%)
    pallas_call x5, Pallas kernels, call(): pl.pallas_call(kernel, in_specs=specs, out_specs=jax.tree.map(lambda _: p...  44.2 us
    all_to_all x1, starting transfers between devices, local(): lax.all_to_all(grads, 'col', split_axis=0, concat_axis=0, tiled=True)  16 us
    all_to_all x1, starting transfers between devices, local(): strip = lax.all_to_all(pay, 'col', split_axis=0, concat_axis=0, tiled=True)  12.7 us
    all_to_all x1, waiting for transfers between devices, local(): lax.all_to_all(grads, 'col', split_axis=0, concat_axis=0, tiled=True)  8.45 us
    ppermute x2, starting transfers between devices, exchange(): lax.ppermute(low, axis, forward)  8.06 us
    ppermute x2, waiting for transfers between devices, exchange(): lax.ppermute(high, axis, backward)  7.93 us
    all_to_all x1, waiting for transfers between devices, local(): strip = lax.all_to_all(pay, 'col', split_axis=0, concat_axis=0, tiled=True)  3.55 us
    ppermute x2, starting transfers between devices, exchange(): lax.ppermute(high, axis, backward)  3.21 us
  transfers between devices with their start and end apart: 7, of which 3 were waited for; matrix products, arithmetic and copies ran while one was open for 3% of the time, Pallas kernels for 14%

profile of v1, /device:TPU:6, one launch (start us, length us, event | category | flops | bytes accessed | tf_op | source)
XLA Modules:
  0.0 114.2 jit_solution(8936861315757512301)
XLA Ops:
  0.0 0.0 copy-start.10
  0.0 0.0 copy-start
  0.0 0.0 copy-start.12
  0.0 1.0 slice_bitcast_fusion.2
  1.0 0.1 copy.19
  1.1 0.1 copy.20
  1.2 1.0 slice_bitcast_fusion
  2.2 5.0 %collective-permute-start = (bf16[14,32,128]{2,1,0:T(8,128)(2,1)S(1)}, bf16[14,32,128]{2,1,0:T(8,128)(2,1)S(1)}, u32[]{:S(2)}, u32[]{:S(2)}) collective-permute-start(bf16[14,32,128]{2,1,0:T(8,128)(2,1)S(1)} %pad_maximum_fusion.2), channel_id=1, source_target_pairs={{0,32},{32,64},{64,96},{96,128},{128,160},{160,192},{192,224},{1,3... | collective-permute-start | bytes 344072 | tf_op jit(solution)/shard_map/ppermute | solution.py:714
  7.2 0.1 copy.21
  7.3 0.0 copy-start.13
  7.3 0.1 copy.22
  7.5 1.9 %collective-permute-start.1 = (bf16[14,32,128]{2,1,0:T(8,128)(2,1)S(1)}, bf16[14,32,128]{2,1,0:T(8,128)(2,1)S(1)}, u32[]{:S(2)}, u32[]{:S(2)}) collective-permute-start(bf16[14,32,128]{2,1,0:T(8,128)(2,1)S(1)} %pad_maximum_fusion.3), channel_id=1, source_target_pairs={{32,0},{64,32},{96,64},{128,96},{160,128},{192,160},{224,192},{33,... | collective-permute-start | bytes 344072 | tf_op jit(solution)/shard_map/ppermute | solution.py:714
  9.4 0.0 copy-done
  9.4 0.0 copy-done.12
  9.5 0.1 pad.62.clone
  9.6 0.0 collective-permute-done.top
  9.6 0.0 copy-start.7
  9.6 0.1 copy.23
  9.7 0.1 copy.24
  9.8 7.9 %collective-permute-done.1.bot = bf16[14,32,128]{2,1,0:T(8,128)(2,1)S(1)} collective-permute-done((bf16[14,32,128]{2,1,0:T(8,128)(2,1)S(1)}, bf16[14,32,128]{2,1,0:T(8,128)(2,1)S(1)}, u32[]{:S(2)}, u32[]{:S(2)}) %collective-permute-start.1) | collective-permute-done | bytes 114720 | tf_op jit(solution)/shard_map/ppermute | solution.py:714
  17.8 0.0 copy-start.8
  17.8 0.1 copy.25
  17.9 0.1 copy.26
  18.0 0.0 copy-done.10
  18.0 0.1 maximum_maximum_fusion.tall
  18.1 0.0 copy-start.11
  18.2 1.3 %collective-permute-start.3 = (bf16[93,8,128]{2,1,0:T(8,128)(2,1)S(1)}, bf16[93,8,128]{2,1,0:T(8,128)(2,1)S(1)}, u32[]{:S(2)}, u32[]{:S(2)}) collective-permute-start(bf16[93,8,128]{2,1,0:T(8,128)(2,1)S(1)} %pad_maximum_fusion.1), channel_id=1, source_target_pairs={{1,0},{2,1},{3,2},{4,3},{5,4},{6,5},{7,6},{8,7},{9,8},{10,9},{11,1... | collective-permute-start | bytes 571400 | tf_op jit(solution)/shard_map/ppermute | solution.py:714
  19.5 3.0 %collective-permute-start.2 = (bf16[93,8,128]{2,1,0:T(8,128)(2,1)S(1)}, bf16[93,8,128]{2,1,0:T(8,128)(2,1)S(1)}, u32[]{:S(2)}, u32[]{:S(2)}) collective-permute-start(bf16[93,8,128]{2,1,0:T(8,128)(2,1)S(1)} %pad_maximum_fusion), channel_id=1, source_target_pairs={{0,1},{1,2},{2,3},{3,4},{4,5},{5,6},{6,7},{7,8},{8,9},{9,10},{10,1... | collective-permute-start | bytes 571400 | tf_op jit(solution)/shard_map/ppermute | solution.py:714
  22.6 0.7 pad_add_fusion.where
  23.2 0.0 copy-done.13
  23.2 0.6 bitcast_convert_fusion.w_out
  23.9 0.0 collective-permute-done.3.right
  23.9 0.0 copy-start.4
  23.9 0.0 collective-permute-done.2.left
  23.9 0.0 copy-done.7
  23.9 0.0 copy-done.8
  23.9 0.6 copy-done.4
  24.6 0.7 copy-done.5
  25.2 7.9 %shard_map.145 = (bf16[32,16,384]{2,1,0:T(8,128)(2,1)}, f32[1024,128]{1,0:T(8,128)}, bf16[88,48,128]{2,1,0:T(8,128)(2,1)}) custom-call(s32[2]{0:T(128)} %pad_add_fusion.where, bf16[14,32,128]{2,1,0:T(8,128)(2,1)} %copy-done.7, bf16[64,32,128]{2,1,0:T(8,128)(2,1)} %bitcast.46, bf16[14,32,128]{2,1,0:T(8,128)(2,1)} %copy-done.8, bf16[93,8,128]{2,1,0:T(8,128)(2,1)} %copy-done.5, ...), custom_call_target="tpu_custom_call" | custom-call | tf_op jit(solution)/shard_map/pallas_call | solution.py:567
  33.1 0.0 copy-done.11
  33.1 12.7 %all-to-all-start = ((bf16[32,16,384]{2,1,0:T(8,128)(2,1)}), bf16[32,16,384]{2,1,0:T(8,128)(2,1)S(1)}, u32[]{:S(2)}, u32[]{:S(2)}) async-start(bf16[32,16,384]{2,1,0:T(8,128)(2,1)} %get-tuple-element.10), calls=%async_computation | async-start | bytes 786432 | tf_op jit(solution)/shard_map/all_to_all | solution.py:758
  45.8 0.1 fusion.4
  45.9 0.0 copy-done.9
  45.9 0.0 copy-done.16
  45.9 0.0 copy-start.3
  45.9 0.5 collective-permute-start.4
  46.5 0.0 copy-done.17
  46.5 0.0 copy-done.15
  46.5 0.7 copy.29.anchors
  47.2 0.6 pad_bitcast_fusion.2.weights
  47.8 0.0 copy-done.14
  47.8 0.6 bitcast_convert_fusion.1.v_first
  48.4 9.8 %shard_map.146 = (bf16[3456,128]{1,0:T(8,128)(2,1)}, bf16[3648,128]{1,0:T(8,128)(2,1)}) custom-call(s32[2]{0:T(128)} %pad_add_fusion.where, f32[1024,128]{1,0:T(8,128)} %get-tuple-element.11.dec, bf16[3,32,128]{2,1,0:T(8,128)(2,1)} %copy-done.11, bf16[93,8,128]{2,1,0:T(8,128)(2,1)} %copy-done.5, bf16[93,8,128]{2,1,0:T(8,128)(2,1)} %copy-done.4, ...), custom_call_target="tpu_custom_call" | custom-call | tf_op jit(solution)/shard_map/pallas_call | solution.py:567
  58.1 0.0 collective-permute-done.4.other
  58.2 3.6 %all-to-all-done.strip = bf16[32,16,384]{2,1,0:T(8,128)(2,1)S(1)} async-done(((bf16[32,16,384]{2,1,0:T(8,128)(2,1)}), bf16[32,16,384]{2,1,0:T(8,128)(2,1)S(1)}, u32[]{:S(2)}, u32[]{:S(2)}) %all-to-all-start) | async-done | bytes 393248 | tf_op jit(solution)/shard_map/all_to_all | solution.py:758
  61.7 0.0 copy-done.3
  61.7 0.0 copy-done.6
  61.7 0.7 copy-done.1
  62.5 15.3 %shard_map.147 = bf16[32,40,128]{2,1,0:T(8,128)(2,1)} custom-call(s32[2]{0:T(128)} %pad_add_fusion.where, s32[64,2]{1,0:T(8,128)} %copy.29.anchors, s32[64]{0:T(128)} %bitcast.59, bf16[32,16,384]{2,1,0:T(8,128)(2,1)} %copy-done.1, bf16[256,384]{1,0:T(8,128)(2,1)} %constant.24.clone.pick, bf16[4,224,128]{2,1,0:T(8,128)(2,1)} %constant.25.clone.rows_of, ...), custom_call_target="tpu_custom_call" | custom-call | tf_op jit(solution)/shard_map/pallas_call | solution.py:567
  77.7 16.0 %all-to-all-start.1 = ((bf16[32,40,128]{2,1,0:T(8,128)(2,1)}), bf16[32,40,128]{2,1,0:T(8,128)(2,1)S(1)}, u32[]{:S(2)}, u32[]{:S(2)}) async-start(bf16[32,40,128]{2,1,0:T(8,128)(2,1)} %shard_map.147), calls=%async_computation.1 | async-start | bytes 655360 | tf_op jit(solution)/shard_map/all_to_all | solution.py:773
  93.7 6.1 %shard_map.148.lpips = f32[640,128]{1,0:T(8,128)} custom-call(s32[2]{0:T(128)} %pad_add_fusion.where, bf16[3456,128]{1,0:T(8,128)(2,1)} %get-tuple-element.12._.feat, bf16[3648,128]{1,0:T(8,128)(2,1)} %get-tuple-element.13.slope_one, f32[3,32,128]{2,1,0:T(8,128)} %bitcast_convert_fusion.1.v_first, bf16[3,3,64,64]{3,2,1,0:T(8,128)(2,1)} %v_second.3), custom_call_target="tpu_custom_call" | custom-call | tf_op jit(solution)/shard_map/pallas_call | solution.py:567
  99.8 8.5 %all-to-all-done.1.parts = bf16[32,40,128]{2,1,0:T(8,128)(2,1)S(1)} async-done(((bf16[32,40,128]{2,1,0:T(8,128)(2,1)}), bf16[32,40,128]{2,1,0:T(8,128)(2,1)S(1)}, u32[]{:S(2)}, u32[]{:S(2)}) %all-to-all-start.1) | async-done | bytes 327712 | tf_op jit(solution)/shard_map/all_to_all | solution.py:773
  108.2 0.7 copy-done.2
  108.9 5.3 %shard_map.149 = bf16[64,32,128]{2,1,0:T(8,128)(2,1)} custom-call(s32[2]{0:T(128)} %pad_add_fusion.where, bf16[32,40,128]{2,1,0:T(8,128)(2,1)} %copy-done.2, f32[640,128]{1,0:T(8,128)} %shard_map.148.lpips, bf16[88,48,128]{2,1,0:T(8,128)(2,1)} %get-tuple-element.14.slope, bf16[64,32,128]{2,1,0:T(8,128)(2,1)} %bitcast.47, bf16[3,3,128,128]{3,2,1,0:T(8,128)(2,1)} %w_mid.3, ...), custom_call_target="tpu_custom_call" | custom-call | tf_op jit(solution)/shard_map/pallas_call | solution.py:567
  (30 shorter events, 0.3 us)
Async XLA Ops:
  0.0 18.0 %copy-start.10 = (bf16[1,64,32,3]{1,2,3,0:T(8,128)(2,1)S(1)}, bf16[1,64,32,3]{1,2,3,0:T(8,128)(2,1)}, u32[]{:S(2)}) copy-start(bf16[1,64,32,3]{1,2,3,0:T(8,128)(2,1)} %param.18) | copy-start | bytes 36868
  0.0 9.4 %copy-start = (bf16[1,64,32,128]{3,2,1,0:T(8,128)(2,1)S(1)}, bf16[1,64,32,128]{3,2,1,0:T(8,128)(2,1)}, u32[]{:S(2)}) copy-start(bf16[1,64,32,128]{3,2,1,0:T(8,128)(2,1)} %param.15) | copy-start | bytes 1572868
  0.0 9.4 %copy-start.12 = (bf16[1,4,4,3,64]{4,2,3,1,0:T(4,128)(2,1)S(1)}, bf16[1,4,4,3,64]{4,2,3,1,0:T(4,128)(2,1)}, u32[]{:S(2)}) copy-start(bf16[1,4,4,3,64]{4,2,3,1,0:T(4,128)(2,1)} %param.24) | copy-start | bytes 18436
  2.2 7.4 %collective-permute-start = (bf16[14,32,128]{2,1,0:T(8,128)(2,1)S(1)}, bf16[14,32,128]{2,1,0:T(8,128)(2,1)S(1)}, u32[]{:S(2)}, u32[]{:S(2)}) collective-permute-start(bf16[14,32,128]{2,1,0:T(8,128)(2,1)S(1)} %pad_maximum_fusion.2), channel_id=1, source_target_pairs={{0,32},{32,64},{64,96},{96,128},{128,160},{160,192},{192,224},{1,3... | collective-permute-start | bytes 344072 | tf_op jit(solution)/shard_map/ppermute | solution.py:714
  7.3 15.9 %copy-start.13 = (bf16[3,3,128,3]{2,3,1,0:T(4,128)(2,1)S(1)}, bf16[3,3,128,3]{2,3,1,0:T(4,128)(2,1)}, u32[]{:S(2)}) copy-start(bf16[3,3,128,3]{2,3,1,0:T(4,128)(2,1)} %param.17) | copy-start | bytes 20740
  7.5 10.3 %collective-permute-start.1 = (bf16[14,32,128]{2,1,0:T(8,128)(2,1)S(1)}, bf16[14,32,128]{2,1,0:T(8,128)(2,1)S(1)}, u32[]{:S(2)}, u32[]{:S(2)}) collective-permute-start(bf16[14,32,128]{2,1,0:T(8,128)(2,1)S(1)} %pad_maximum_fusion.3), channel_id=1, source_target_pairs={{32,0},{64,32},{96,64},{128,96},{160,128},{192,160},{224,192},{33,... | collective-permute-start | bytes 344072 | tf_op jit(solution)/shard_map/ppermute | solution.py:714
  9.6 14.3 %copy-start.7 = (bf16[14,32,128]{2,1,0:T(8,128)(2,1)}, bf16[14,32,128]{2,1,0:T(8,128)(2,1)S(1)}, u32[]{:S(2)}) copy-start(bf16[14,32,128]{2,1,0:T(8,128)(2,1)S(1)} %collective-permute-done.top) | copy-start | bytes 344068
  17.8 6.1 %copy-start.8 = (bf16[14,32,128]{2,1,0:T(8,128)(2,1)}, bf16[14,32,128]{2,1,0:T(8,128)(2,1)S(1)}, u32[]{:S(2)}) copy-start(bf16[14,32,128]{2,1,0:T(8,128)(2,1)S(1)} %collective-permute-done.1.bot) | copy-start | bytes 344068
  18.1 15.0 %copy-start.11 = (bf16[3,32,128]{2,1,0:T(8,128)(2,1)}, bf16[3,32,128]{2,1,0:T(8,128)(2,1)S(1)}, u32[]{:S(2)}) copy-start(bf16[3,32,128]{2,1,0:T(8,128)(2,1)S(1)} %maximum_maximum_fusion.tall) | copy-start | bytes 73732
  18.2 5.7 %collective-permute-start.3 = (bf16[93,8,128]{2,1,0:T(8,128)(2,1)S(1)}, bf16[93,8,128]{2,1,0:T(8,128)(2,1)S(1)}, u32[]{:S(2)}, u32[]{:S(2)}) collective-permute-start(bf16[93,8,128]{2,1,0:T(8,128)(2,1)S(1)} %pad_maximum_fusion.1), channel_id=1, source_target_pairs={{1,0},{2,1},{3,2},{4,3},{5,4},{6,5},{7,6},{8,7},{9,8},{10,9},{11,1... | collective-permute-start | bytes 571400 | tf_op jit(solution)/shard_map/ppermute | solution.py:714
  19.5 4.4 %collective-permute-start.2 = (bf16[93,8,128]{2,1,0:T(8,128)(2,1)S(1)}, bf16[93,8,128]{2,1,0:T(8,128)(2,1)S(1)}, u32[]{:S(2)}, u32[]{:S(2)}) collective-permute-start(bf16[93,8,128]{2,1,0:T(8,128)(2,1)S(1)} %pad_maximum_fusion), channel_id=1, source_target_pairs={{0,1},{1,2},{2,3},{3,4},{4,5},{5,6},{6,7},{7,8},{8,9},{9,10},{10,1... | collective-permute-start | bytes 571400 | tf_op jit(solution)/shard_map/ppermute | solution.py:714
  23.8 22.0 %copy-start.9 = (bf16[1,4,4,64,128]{4,3,2,1,0:T(8,128)(2,1)S(1)}, bf16[1,4,4,64,128]{4,3,2,1,0:T(8,128)(2,1)}, u32[]{:S(2)}) copy-start(bf16[1,4,4,64,128]{4,3,2,1,0:T(8,128)(2,1)} %param.25) | copy-start | bytes 786436
  23.9 22.0 %copy-start.16 = (bf16[1,128]{1,0:T(2,128)(2,1)S(1)}, bf16[1,128]{1,0:T(2,128)(2,1)}, u32[]{:S(2)}) copy-start(bf16[1,128]{1,0:T(2,128)(2,1)} %param.26) | copy-start | bytes 772
  23.9 22.6 %copy-start.17 = (f32[64]{0:T(128)S(1)}, f32[64]{0:T(128)}, u32[]{:S(2)}) copy-start(f32[64]{0:T(128)} %param.21) | copy-start | bytes 772
  23.9 22.6 %copy-start.15 = (s32[1,64,2]{1,2,0:T(2,128)S(1)}, s32[1,64,2]{1,2,0:T(2,128)}, u32[]{:S(2)}) copy-start(s32[1,64,2]{1,2,0:T(2,128)} %param.22) | copy-start | bytes 1540
  23.9 0.7 copy-start.4
  24.5 0.7 copy-start.5
  33.1 14.7 %copy-start.14 = (bf16[3,3,3,64]{3,2,1,0:T(4,128)(2,1)S(1)}, bf16[3,3,3,64]{3,2,1,0:T(4,128)(2,1)}, u32[]{:S(2)}) copy-start(bf16[3,3,3,64]{3,2,1,0:T(4,128)(2,1)} %param.19) | copy-start | bytes 10372
  33.1 28.6 %all-to-all-start = ((bf16[32,16,384]{2,1,0:T(8,128)(2,1)}), bf16[32,16,384]{2,1,0:T(8,128)(2,1)S(1)}, u32[]{:S(2)}, u32[]{:S(2)}) async-start(bf16[32,16,384]{2,1,0:T(8,128)(2,1)} %get-tuple-element.10), calls=%async_computation | async-start | bytes 786432 | tf_op jit(solution)/shard_map/all_to_all | solution.py:758
  45.9 15.8 %copy-start.3 = (bf16[1136,128]{1,0:T(8,128)(2,1)}, bf16[1136,128]{1,0:T(8,128)(2,1)S(1)}, u32[]{:S(2)}) copy-start(bf16[1136,128]{1,0:T(8,128)(2,1)S(1)} %fusion.1.mine) | copy-start | bytes 872452
  45.9 12.2 %collective-permute-start.4 = (bf16[1136,128]{1,0:T(8,128)(2,1)S(1)}, bf16[1136,128]{1,0:T(8,128)(2,1)S(1)}, u32[]{:S(2)}, u32[]{:S(2)}) collective-permute-start(bf16[1136,128]{1,0:T(8,128)(2,1)S(1)} %fusion.1.mine), channel_id=1, source_target_pairs={{0,1},{1,0},{2,3},{3,2},{4,5},{5,4},{6,7},{7,6},{8,9},{9,8},{10,11... | collective-permute-start | bytes 872456 | tf_op jit(solution)/shard_map/ppermute | solution.py:760
  58.1 3.6 %copy-start.6 = (bf16[1136,128]{1,0:T(8,128)(2,1)}, bf16[1136,128]{1,0:T(8,128)(2,1)S(1)}, u32[]{:S(2)}) copy-start(bf16[1136,128]{1,0:T(8,128)(2,1)S(1)} %collective-permute-done.4.other) | copy-start | bytes 872452
  61.7 0.7 copy-start.1
  77.7 30.5 %all-to-all-start.1 = ((bf16[32,40,128]{2,1,0:T(8,128)(2,1)}), bf16[32,40,128]{2,1,0:T(8,128)(2,1)S(1)}, u32[]{:S(2)}, u32[]{:S(2)}) async-start(bf16[32,40,128]{2,1,0:T(8,128)(2,1)} %shard_map.147), calls=%async_computation.1 | async-start | bytes 655360 | tf_op jit(solution)/shard_map/all_to_all | solution.py:773
  108.2 0.7 copy-start.2

commit v2 on v1

--- a/solution.py
+++ b/solution.py
@@ -21,9 +21,9 @@
 COL_HALO = 8
 WIDE = TW + 2 * COL_HALO
 TGT_HALO = 6
-GRAD_PAD = 10
+GRAD_PAD = 8
 SHARE = 34
-VMEM = 56 * 1024 * 1024
+VMEM = 20 * 1024 * 1024
 
 
 def sigmoid(v):
@@ -127,9 +127,9 @@
 
 
 def decode_kernel(
-    where, top, mid, bot, left, right, w_mid, w_out, pay, dec, slope_out, s1, s2, w, w3
+    meta, top, mid, bot, left, right, w_mid, w_out, pay, dec, slope_out, s1, s2, w, w3
 ):
-    r, c = where[0], where[1]
+    r, c = meta[0], meta[1]
     for dy in range(3):
         for dx in range(3):
             w[dy * 128 : (dy + 1) * 128, dx * 128 : (dx + 1) * 128] = w_mid[dy, dx]
@@ -156,12 +156,14 @@
         act, slope = silu_parts(v)
         act = keep_inside(act, r * TH - 12 + i * 8, 8, col_ok)
         s2[pl.ds(aligned(i * 8 * WIDE, 16), 8 * WIDE), :] = act.astype(BF)
-        slope_out[pl.ds(i * 8, 8)] = (
-            pltpu.roll(slope, 8 * WIDE - 6, 0).reshape(8, WIDE, 128).astype(BF)
-        )
-        return carry
-
-    lax.fori_loop(0, 11, middle, 0, unroll=True)
+        slope = pltpu.roll(slope, 8 * WIDE - 6, 0).reshape(8, WIDE, 128).astype(BF)
+        first, last = max(i * 8, 11), min(i * 8 + 8, 79)
+        if first < last:
+            slope_out[first - 11 : last - 11] = slope[first - i * 8 : last - i * 8]
+        return carry
+
+    for i in range(11):
+        middle(i, 0)
     s2[88 * WIDE :, :] = jnp.zeros((10 * WIDE, 128), BF)
     dec[768:, :] = jnp.zeros((256, 128), F32)
 
@@ -193,10 +195,10 @@
 
 
 def percept_kernel(
-    where, dec, tall, left, right, v_first, v_second, weights, feat, slope_one,
+    meta, dec, tall, left, right, v_first, v_second, weights, feat, slope_one, done,
     planes, px, one, w1, w2,
 ):
-    r, c = where[0], where[1]
+    r, c = meta[0], meta[1]
     col_first = c * TW - COL_HALO
     col_ok = column_mask(col_first)
 
@@ -220,6 +222,8 @@
             [a.astype(F32) for a in (left[90 + k], tall[k], right[90 + k])], axis=0
         )
         planes[pl.ds(3 + k, 80, stride=8), :] = taller(v).T[0:80]
+
+    done[...] = jnp.zeros((8, 128), F32)
 
     def gather(i, carry):
         v = dec[pl.ds(aligned(i * 32 + 40, 8), 32), :] + planes[pl.ds(aligned(i * 32, 32), 32), :]
@@ -267,8 +271,8 @@
     lax.fori_loop(0, 9, second, 0, unroll=3)
 
 
-def percept_back_kernel(where, feat, slope_one, v_first, v_second, out, bv, w3, w4):
-    r, c = where[0], where[1]
+def percept_back_kernel(meta, feat, slope_one, v_first, v_second, out, bv, w3, w4):
+    r, c = meta[0], meta[1]
     col_ok = column_mask(c * TW - COL_HALO)
 
     def last_small(dy):
@@ -302,6 +306,7 @@
     lax.fori_loop(0, 5, colours, 0, unroll=True)
 
 
+STOP = object()
 STEPS = 6
 HALF = STEPS + 1
 TILES = 2 * HALF
@@ -310,10 +315,11 @@
 
 
 def critic_kernel(
-    where, anchors, owners, strip, pick, rows_of, rows_back, mine, other, _, out,
-    strip32, grads, w_pre, w_one, w_two, w_back, score, x_all, pre, act, two, cols,
+    meta, strip, mine, other, _, out,
+    strip32, grads, w_pre, w_one, w_two, w_back, score, distance, row_gap, row_gap_back, x_all, x_all_b, pre, pre_b, act, act_b,
+    two, two_b, cols, cols_b, jobs,
 ):
-    r, me = where[0], where[1]
+    r, me = meta[0], meta[1]
     first_row = r * TH - 2 + SHARE * (me & 1)
     lane = iota((1, 128), 1)
     upper = lane >= 64
@@ -334,16 +340,19 @@
     w_back[...] = jnp.zeros(w_back.shape, BF)
     for g, source in enumerate((mine, other)):
         w_one[g] = source[1024:1120, :]
-        w_pre[g] = taller(source[1024:1120, :].astype(F32)).T.astype(BF)
+        w_pre[g] = (0.5 * taller(source[1024:1120, :].astype(F32))).T.astype(BF)
         score[g] = taller(source[1120:1136, :].astype(F32)).T
         for i in range(4):
-            w_two[g, i] = jnp.concatenate(
-                [
-                    source[i * 256 + k * 128 : i * 256 + (k + 1) * 128, :].astype(F32).T
-                    for k in range(2)
-                ],
-                axis=1,
-            ).astype(BF)
+            first, second = (
+                pltpu.roll(
+                    source[i * 256 + k * 128 : i * 256 + (k + 1) * 128, :].astype(F32).T, 64, 1
+                )
+                for k in range(2)
+            )
+            at = slice((i // 2) * 128, (i // 2 + 1) * 128)
+            w_two[g, i % 2, 0:128, at] = jnp.where(upper, second, first).astype(BF)
+            w_two[g, i % 2, 128:256, at] = jnp.where(upper, first, 0.0).astype(BF)
+            w_two[g, i % 2, 256:384, at] = jnp.where(upper, 0.0, second).astype(BF)
         for par in range(2):
             for p in range(2):
                 for t in range(2):
@@ -353,22 +362,45 @@
                             g,
                             (par * 2 + p) * 64 : (par * 2 + p + 1) * 64,
                             (t * 3 + kind) * 128 : (t * 3 + kind + 1) * 128,
-                        ] = source[i * 256 + j * 64 : i * 256 + (j + 1) * 64, :]
-    two[:, 0:128] = jnp.zeros((384, 128), BF)
-    two[:, (STEPS + 1) * 128 :] = jnp.zeros((384, 128), BF)
-    cols[192:, :] = jnp.zeros((64, 384), F32)
+                        ] = 0.5 * source[i * 256 + j * 64 : i * 256 + (j + 1) * 64, :]
+    for t in (two, two_b):
+        t[:, 0:128] = jnp.zeros((384, 128), BF)
+        t[:, (STEPS + 1) * 128 :] = jnp.zeros((384, 128), BF)
+    for t in (cols, cols_b):
+        t[192:, :] = jnp.zeros((64, 384), F32)
+    x, n = iota((CROP + 8, 384), 0), iota((CROP + 8, 384), 1)
+    wanted = 4 * (n & 63) + (n >> 6) - 1
+    wanted_ok = (wanted >= 0) & (wanted < CROP)
+    distance[...] = jnp.where(wanted_ok, x - wanted, -1).astype(F32)
+
+    def gap(dims, rho, n):
+        tile, i, k = rho >> 4, (rho >> 2) & 3, rho & 3
+        u = 2 * jnp.where(tile >= HALF, tile - HALF, tile) + jnp.where(tile >= HALF, 1, 0)
+        return jnp.where(k < 3, n - (k * 40 + 2 * u + i), -1).astype(F32)
+
+    dims = (TILES * 16, 128)
+    row_gap[...] = gap(dims, iota(dims, 0), iota(dims, 1))
+    dims = (128, TILES * 16)
+    row_gap_back[...] = gap(dims, iota(dims, 1), iota(dims, 0))
     wide = iota((1, 256), 1)
 
-    def score_crop(top, left, g):
+    def anchor(q, k):
+        return meta[2 + 2 * q + k]
+
+    def owner_of(q):
+        return meta[2 + 2 * CROPS + q]
+
+    def job(q, live, x_all, pre, act, two, cols):
+        top, left, g = anchor(q, 0), anchor(q, 1), (owner_of(q) ^ me) & 1
         y0 = first_row - top
         v0 = lax.shift_right_arithmetic(y0 - 3, 2)
         e = 4 * v0 - y0 + 6
         crop_row = y0 - 9 + (wide & 63)
         in_crop = (crop_row >= 0) & (crop_row < CROP) & (wide < 192)
-        window = strip32[pl.ds(aligned((left >> 3) * 8, 8), CROP + 8), :]
-        window = pltpu.roll(window, lax.rem((CROP + 8) - (left & 7), CROP + 8), 0)[0:CROP]
-        window = jnp.where(in_crop, window, 0.0).astype(BF)
-        cols_of = mm(window, pick[...], 0, 0)
+        here = pl.ds(aligned((left >> 3) * 8, 8), CROP + 8)
+        window = jnp.where(in_crop, strip32[here, :], 0.0).astype(BF)
+        pick = jnp.where(distance[...] == (left & 7).astype(F32), 1.0, 0.0).astype(BF)
+        cols_of = mm(window, pick, 0, 0)
         none = jnp.zeros((8, 384), F32)
         halves = [
             jnp.concatenate(
@@ -386,12 +418,15 @@
             else:
                 low = pltpu.roll(low, 64, 1)
             mixed.append(jnp.where(upper, high, low))
-        patches = mm(rows_of[e], jnp.concatenate(mixed, axis=1).astype(BF)).astype(BF)
+        yield
+        chosen = jnp.where(row_gap[...] == e.astype(F32), 1.0, 0.0).astype(BF)
+        patches = mm(chosen, jnp.concatenate(mixed, axis=1).astype(BF)).astype(BF)
         for t in range(TILES):
             for m in range(6):
                 x_all[m * 16 : (m + 1) * 16, t * 128 : (t + 1) * 128] = patches[
                     t * 16 : (t + 1) * 16, m * 128 : (m + 1) * 128
                 ]
+        yield
         weight = w_pre[g][:, 0:96]
         for t0 in range(0, TILES, 2):
             at = slice(t0 * 128, (t0 + 2) * 128)
@@ -401,23 +436,27 @@
                 n = 2 * (t % HALF) + t // HALF + jnp.where(upper, 2 * STEPS, 0)
                 u = 2 * v0 - 1 + n
                 ok = ((u >= 0) & (u < CROP // 2)).astype(F32)
-                a, slope = silu_parts(value[:, (t - t0) * 128 : (t - t0 + 1) * 128])
-                a = a * ok
-                pre[:, at] = slope * ok
-                even, odd = a[:64], a[64:]
-                act[0:64, at] = jnp.where(first_x, 0.0, pltpu.roll(odd, 1, 1)).astype(BF)
-                act[64:128, at] = even.astype(BF)
-                act[128:192, at] = odd.astype(BF)
-                act[192:256, at] = jnp.where(last_x, 0.0, pltpu.roll(even, 127, 1)).astype(BF)
+                half = value[:, (t - t0) * 128 : (t - t0 + 1) * 128]
+                rise = jnp.tanh(half) + 1.0
+                kept = rise * ok
+                pre[:, at] = kept * (1.0 + half * (2.0 - rise))
+                act[:, at] = (half * kept).astype(BF)
+            yield
         column = score[g][:, 0:1]
         for t0 in range(0, STEPS, 2):
-            value = None
-            for i in range(4):
-                start = (i % 2) * EVEN + (i // 2 + t0) * 128
-                part = mm(w_two[g, i], act[:, start : start + 256])
-                value = part if value is None else value + part
+            value = 0.0
+            for par in range(2):
+                at = par * EVEN + t0 * 128
+                taps = jnp.concatenate(
+                    [act[:, at : at + 256], act[:, at + 128 : at + 384]], axis=0
+                )
+                value = value + mm(w_two[g, par], taps)
             for t in range(t0, t0 + 2):
-                f, slope = silu_parts(value[:, (t - t0) * 128 : (t - t0 + 1) * 128])
+                at = slice((t - t0) * 128, (t - t0 + 1) * 128)
+                f = value[0:128, at]
+                f = f + jnp.where(first_x, 0.0, pltpu.roll(value[128:256, at], 1, 1))
+                f = f + jnp.where(last_x, 0.0, pltpu.roll(value[256:384, at], 127, 1))
+                f, slope = silu_parts(f)
                 logit = jnp.sum(f * column, axis=0, keepdims=True)
                 v = v0 + t + jnp.where(upper, STEPS, 0)
                 ok = (v >= 0) & (v < CROP // 4)
@@ -427,6 +466,7 @@
                 two[0:128, at] = b.astype(BF)
                 two[128:256, at] = jnp.where(first_x, 0.0, pltpu.roll(b, 1, 1)).astype(BF)
                 two[256:384, at] = jnp.where(last_x, 0.0, pltpu.roll(b, 127, 1)).astype(BF)
+            yield
         for s0 in range(0, HALF, 2):
             n = min(2, HALF - s0) * 128
             at = s0 * 128
@@ -436,6 +476,7 @@
                 here = slice(par * EVEN + at, par * EVEN + at + n)
                 one = (up[par * 128 : (par + 1) * 128] * pre[:, here]).astype(BF)
                 x_all[:, here] = mm(w_one[g], one).astype(BF)
+            yield
         spread = jnp.concatenate(
             [
                 jnp.concatenate(
@@ -449,7 +490,9 @@
             ],
             axis=1,
         )
-        back = mm(rows_back[e], spread)
+        chosen = jnp.where(row_gap_back[...] == e.astype(F32), 1.0, 0.0).astype(BF)
+        back = mm(chosen, spread)
+        yield
         parts = []
         for h in range(2):
             tiles = []
@@ -467,28 +510,36 @@
             cols[k * 64 : (k + 1) * 64, :] = jnp.concatenate(
                 [low[0:24], low[24:40] + high[0:16], high[16:40]], axis=0
             )
-        placed = mm(pick[...], cols[...].astype(BF), 1, 1)
+        yield
+        placed = mm(pick, cols[...].astype(BF), 1, 1)
         y = wide & 63
-        keep = in_crop & (y >= 9) & (y < 9 + SHARE)
-        placed = jnp.concatenate([jnp.where(keep, placed, 0.0), jnp.zeros((8, 256), F32)], axis=0)
-        start = left + GRAD_PAD
-        here = pl.ds(aligned((start >> 3) * 8, 8), CROP + 8)
-        grads[here, :] = grads[here, :] + pltpu.roll(placed, start & 7, 0)
-
-    def one_crop(q, carry):
-        top, left, owner = anchors[q, 0], anchors[q, 1], owners[q]
-        y0 = first_row - top
-
-        @pl.when(((owner >> 1) == (me >> 1)) & (y0 < CROP) & (y0 + SHARE > 0))
-        def _():
-            score_crop(top, left, (owner ^ me) & 1)
-
-        return carry
-
-    lax.fori_loop(0, CROPS, one_crop, 0)
+        keep = in_crop & (y >= 9) & (y < 9 + SHARE) & live
+        yield
+        here = pl.ds(aligned((left >> 3) * 8 + GRAD_PAD, 8), CROP + 8)
+        grads[here, :] = grads[here, :] + jnp.where(keep, placed, 0.0)
+
+    count = jnp.int32(0)
+    for q in range(CROPS):
+        y0 = first_row - anchor(q, 0)
+        shared = (owner_of(q) >> 1) == (me >> 1)
+        shared = shared & (y0 < CROP) & (y0 + SHARE > 0)
+        jobs[count] = q
+        count = count + shared.astype(jnp.int32)
+
+    def two_crops(k, carry):
+        last = jnp.minimum(2 * k + 1, count - 1)
+        running = [
+            job(jobs[2 * k], True, x_all, pre, act, two, cols),
+            job(jobs[last], 2 * k + 1 < count, x_all_b, pre_b, act_b, two_b, cols_b),
+        ]
+        while running:
+            running = [g for g in running if next(g, STOP) is not STOP]
+        return carry
+
+    lax.fori_loop(0, (count + 1) >> 1, two_crops, 0)
 
     def pack(k, carry):
-        block = grads[pl.ds(aligned(k * TW + 8, 8), 40), :]
+        block = grads[pl.ds(aligned(k * TW, 32), 48), :][GRAD_PAD - 2 : GRAD_PAD + 38]
         a, b = block[:, 0:128], block[:, 128:256]
         out[k] = jnp.where(
             lane < 40,
@@ -501,9 +552,9 @@
 
 
 def finish_kernel(
-    where, parts, lpips, slope, feats, w_mid, w_out, out, turned, planes, px, bm, w, w1
+    meta, parts, lpips, slope, feats, w_mid, w_out, out, turned, planes, px, bm, w, w1
 ):
-    r, c = where[0], where[1]
+    r, c = meta[0], meta[1]
     for dy in range(3):
         for dx in range(3):
             w[dx * 128 : (dx + 1) * 128, dy * 128 : (dy + 1) * 128] = w_mid[2 - dy, 2 - dx]
@@ -540,7 +591,7 @@
             for k in range(4):
                 n = (tile + j) * 4 + k
                 x = v[j * WIDE : (j + 1) * WIDE, k * 128 : (k + 1) * 128]
-                x = keep_inside(x * slope[n + 11].astype(F32), r * TH - 1 + n, 1, col_ok)
+                x = keep_inside(x * slope[n].astype(F32), r * TH - 1 + n, 1, col_ok)
                 bm[pl.ds(aligned(n * WIDE, 16), WIDE), :] = x.astype(BF)
 
     def middle_group(i, carry):
@@ -560,7 +611,7 @@
     lax.fori_loop(0, TH // 8, last, 0, unroll=4)
 
 
-def call(kernel, outs, scratch, args, scalars=1, unused=0):
+def call(kernel, outs, scratch, args, scalars=1, unused=0, lists=()):
     specs = [pl.BlockSpec(memory_space=pltpu.SMEM)] * scalars
     specs += [pl.BlockSpec(memory_space=pltpu.VMEM)] * (len(args) - scalars - unused)
     specs += [pl.BlockSpec(memory_space=pl.ANY)] * unused
@@ -569,7 +620,7 @@
         in_specs=specs,
         out_specs=jax.tree.map(lambda _: pl.BlockSpec(memory_space=pltpu.VMEM), outs),
         out_shape=outs,
-        scratch_shapes=[pltpu.VMEM(s, t) for s, t in scratch],
+        scratch_shapes=[pltpu.VMEM(s, t) for s, t in scratch] + list(lists),
         compiler_params=pltpu.CompilerParams(vmem_limit_bytes=VMEM),
         interpret=INTERPRET,
     )(*args)
@@ -582,49 +633,33 @@
     return jax.ShapeDtypeStruct(dims, kind)
 
 
-def row_tables():
-    table = np.zeros((4, TILES, 16, 128), np.float32)
-    for e in range(4):
-        for t in range(TILES):
-            u = 2 * (t % HALF) + t // HALF
-            for i in range(4):
-                for k in range(3):
-                    table[e, t, i * 4 + k, k * 40 + 2 * u + i + e] = 1.0
-    return table.reshape(4, TILES * 16, 128)
-
-
-def column_table():
-    table = np.zeros((CROP, 6, 64), np.float32)
-    for m in range(6):
-        for x in range(64):
-            if 0 <= 4 * x + m - 1 < CROP:
-                table[4 * x + m - 1, m, x] = 1.0
-    return table.reshape(CROP, 384)
-
-
 def colour_first(w):
     w = jnp.pad(w.astype(F32), ((0, 0), (0, 1), (0, 5), (0, 128 - w.shape[-1])))
     return w.reshape(3, 32, 128)
 
 
-def decode(where, top, mid, bot, left, right, conv_mid, small):
+def decode(meta, top, mid, bot, left, right, conv_mid, small):
     return call(
         decode_kernel,
         (
             shape((COLS, TW // 2, 384), BF),
             shape((1024, 128), F32),
-            shape((88, WIDE, 128), BF),
+            pltpu.HBM((68, WIDE, 128), BF),
         ),
         [((90 * WIDE, 128), BF), ((98 * WIDE, 128), BF), ((384, 384), BF), ((384, 384), BF)],
-        (where, top, mid, bot, left, right, conv_mid, small),
-    )
-
-
-def percept(where, dec, tall, left, right, small, vgg_second, weights):
+        (meta, top, mid, bot, left, right, conv_mid, small),
+    )
+
+
+def percept(meta, dec, tall, left, right, small, vgg_second, weights):
     scaled = jnp.pad(2.0 * LOSS_SCALE * weights, (0, 64)).reshape(1, 128)
     return call(
         percept_kernel,
-        (shape((72 * WIDE, 128), BF), shape((76 * WIDE, 128), BF)),
+        (
+            pltpu.HBM((72 * WIDE, 128), BF),
+            pltpu.HBM((76 * WIDE, 128), BF),
+            shape((8, 128), F32),
+        ),
         [
             ((80 * 8, 128), F32),
             ((20 * WIDE, 128), BF),
@@ -632,16 +667,16 @@
             ((256, 512), BF),
             ((384, 384), BF),
         ],
-        (where, dec, tall, left, right, small, vgg_second, scaled),
-    )
-
-
-def percept_back(where, feat, slope_one, small, vgg_second):
+        (meta, dec, tall, left, right, small, vgg_second, scaled),
+    )
+
+
+def percept_back(meta, feat, slope_one, small, vgg_second):
     return call(
         percept_back_kernel,
         shape((80 * 8, 128), F32),
         [((82 * WIDE, 128), BF), ((384, 384), BF), ((384, 384), BF)],
-        (where, feat, slope_one, small, vgg_second),
+        (meta, feat, slope_one, small, vgg_second),
     )
 
 
@@ -655,8 +690,14 @@
     return jnp.concatenate([second.reshape(1024, 128), w, score], 0)
 
 
-def critics(where, anchors, owners, strip, mine, other, after):
-    rows_of = row_tables()
+def critics(meta, strip, mine, other, after):
+    pair = [
+        ((96, LANES), BF),
+        ((128, LANES), F32),
+        ((128, LANES), BF),
+        ((384, (STEPS + 2) * 128), BF),
+        ((256, 384), F32),
+    ]
     return call(
         critic_kernel,
         shape((COLS, 40, 128), BF),
@@ -665,33 +706,21 @@
             ((IMG_W + 24, 256), F32),
             ((2, 128, 128), BF),
             ((2, 96, 128), BF),
-            ((2, 4, 128, 256), BF),
+            ((2, 2, 384, 256), BF),
             ((2, 256, 768), BF),
             ((2, 128, 128), F32),
-            ((96, LANES), BF),
-            ((128, LANES), F32),
-            ((256, LANES), BF),
-            ((384, (STEPS + 2) * 128), BF),
-            ((256, 384), F32),
-        ],
-        (
-            where,
-            anchors,
-            owners,
-            strip,
-            jnp.asarray(column_table(), BF),
-            jnp.asarray(rows_of, BF),
-            jnp.asarray(np.swapaxes(rows_of, 1, 2), BF),
-            mine,
-            other,
-            after,
-        ),
-        scalars=3,
+            ((CROP + 8, 384), F32),
+            ((TILES * 16, 128), F32),
+            ((128, TILES * 16), F32),
+        ]
+        + [buffer for buffer in pair for _ in range(2)],
+        (meta, strip, mine, other, after),
         unused=1,
-    )
-
-
-def finish(where, parts, lpips, slope, feats, conv_mid, small):
+        lists=[pltpu.SMEM((CROPS,), jnp.int32)],
+    )
+
+
+def finish(meta, parts, lpips, slope, feats, conv_mid, small):
     return call(
         finish_kernel,
         shape((TH, TW, 128), BF),
@@ -703,8 +732,12 @@
             ((384, 384), BF),
             ((256, 512), BF),
         ],
-        (where, parts, lpips, slope, feats, conv_mid, small),
-    )
+        (meta, parts, lpips, slope, feats, conv_mid, small),
+    )
+
+
+def in_hbm(x):
+    return pltpu.with_memory_space_constraint(x, pltpu.HBM)
 
 
 def exchange(low, high, axis):
@@ -718,7 +751,13 @@
     features, conv_mid, conv_out, target, vgg_first, vgg_second, perceptual_weights,
     crop_anchors, crop_owner, critic_first, critic_second, critic_score,
 ):
-    where = jnp.stack([lax.axis_index("row"), lax.axis_index("col")]).astype(jnp.int32)
+    meta = jnp.concatenate(
+        [
+            jnp.stack([lax.axis_index("row"), lax.axis_index("col")]).astype(jnp.int32),
+            crop_anchors.reshape(2 * CROPS),
+            crop_owner.reshape(CROPS),
+        ]
+    )
     feats = features[0]
     planar = jnp.transpose(target[0], (2, 1, 0))
 
@@ -754,25 +793,17 @@
     left, right = exchange(edge(TW - COL_HALO, TW), edge(0, COL_HALO), "col")
     out_small = colour_first(jnp.transpose(conv_out, (0, 1, 3, 2)))
     vgg_small = colour_first(vgg_first)
-    pay, dec, slope = decode(where, top, feats, bot, left, right, conv_mid, out_small)
+    pay, dec, slope = decode(meta, top, feats, bot, left, right, conv_mid, out_small)
     strip = lax.all_to_all(pay, "col", split_axis=0, concat_axis=0, tiled=True)
     mine = critic_weights(critic_first[0], critic_second[0], critic_score[0])
     other = lax.ppermute(mine, "col", [(i, i ^ 1) for i in range(COLS)])
-    feat, slope_one = percept(
-        where, dec, tall, left, right, vgg_small, vgg_second, perceptual_weights
-    )
-    grads = critics(
-        where,
-        crop_anchors.reshape(CROPS, 2),
-        crop_owner.reshape(CROPS),
-        strip,
-        mine,
-        other,
-        feat,
-    )
+    feat, slope_one, done = percept(
+        meta, dec, tall, left, right, vgg_small, vgg_second, perceptual_weights
+    )
+    grads = critics(meta, strip, mine, other, done)
     parts = lax.all_to_all(grads, "col", split_axis=0, concat_axis=0, tiled=True)
-    lpips = percept_back(where, feat, slope_one, vgg_small, vgg_second)
-    return finish(where, parts, lpips, slope, feats, conv_mid, out_small)[None]
+    lpips = percept_back(meta, in_hbm(feat), in_hbm(slope_one), vgg_small, vgg_second)
+    return finish(meta, parts, lpips, slope, feats, conv_mid, out_small)[None]
 
 
 def solution(mesh):

time: 115 us -> 106 us (0.922)
  starting transfers between devices: 40.5 us -> 32.2 us
  other arithmetic: 2.15 us -> 0.35 us
  waiting for transfers between devices: 20 us -> 21.7 us
    all_to_all x1, starting transfers between devices: 16 us -> 6.65 us  [local(): lax.all_to_all(grads, 'col', split_axis=0, concat_axis=0, tiled=True)]
    all_to_all x1, waiting for transfers between devices: 3.55 us -> 5.19 us  [local(): strip = lax.all_to_all(pay, 'col', split_axis=0, concat_axis=0, tiled=True)]
    ppermute x2, waiting for transfers between devices: 7.93 us -> 6.49 us  [exchange(): lax.ppermute(high, axis, backward)]
    reshape x2, other arithmetic: 1.24 us -> 0.01 us  [colour_first(): return w.reshape(3, 32, 128)]
    unnamed x36 -> x27, local copies, waits for them, and re-layouts: 2.81 us -> 3.16 us
  transfers between devices with their start and end apart: 7 -> 7, of which waited for: 3 -> 4; matrix products, arithmetic and copies ran while one was open for 3% -> 1% of each run, Pallas kernels for 14% -> 14%
where the time goes in v2:
time: 106 us; the launch traced here: 105 us
  Pallas kernels  44.4 us (42%)
  starting transfers between devices  32.2 us (30%)
  waiting for transfers between devices  21.7 us (20%)
  local copies, waits for them, and re-layouts  6.2 us (6%)
    pallas_call x5, Pallas kernels, call(): pl.pallas_call(kernel, in_specs=specs, out_specs=jax.tree.map(lambda _: p...  44.4 us
    all_to_all x1, starting transfers between devices, local(): strip = lax.all_to_all(pay, 'col', split_axis=0, concat_axis=0, tiled=True)  13.8 us
    all_to_all x1, waiting for transfers between devices, local(): lax.all_to_all(grads, 'col', split_axis=0, concat_axis=0, tiled=True)  9.12 us
    ppermute x2, starting transfers between devices, exchange(): lax.ppermute(low, axis, forward)  8.06 us
    all_to_all x1, starting transfers between devices, local(): lax.all_to_all(grads, 'col', split_axis=0, concat_axis=0, tiled=True)  6.65 us
    ppermute x2, waiting for transfers between devices, exchange(): lax.ppermute(high, axis, backward)  6.49 us
    all_to_all x1, waiting for transfers between devices, local(): strip = lax.all_to_all(pay, 'col', split_axis=0, concat_axis=0, tiled=True)  5.19 us
    ppermute x2, starting transfers between devices, exchange(): lax.ppermute(high, axis, backward)  3.34 us
  transfers between devices with their start and end apart: 7, of which 4 were waited for; matrix products, arithmetic and copies ran while one was open for 1% of the time, Pallas kernels for 14%

profile of v2, /device:TPU:6, one launch (start us, length us, event | category | flops | bytes accessed | tf_op | source)
XLA Modules:
  0.0 105.2 jit_solution(14989884800843557747)
XLA Ops:
  0.0 0.9 slice_bitcast_fusion.2
  0.9 0.0 copy-start
  0.9 0.1 copy.17
  1.0 0.1 copy.18
  1.1 1.0 slice_bitcast_fusion
  2.1 5.0 %collective-permute-start = (bf16[14,32,128]{2,1,0:T(8,128)(2,1)S(1)}, bf16[14,32,128]{2,1,0:T(8,128)(2,1)S(1)}, u32[]{:S(2)}, u32[]{:S(2)}) collective-permute-start(bf16[14,32,128]{2,1,0:T(8,128)(2,1)S(1)} %pad_maximum_fusion.2), channel_id=1, source_target_pairs={{0,32},{32,64},{64,96},{96,128},{128,160},{160,192},{192,224},{1,3... | collective-permute-start | bytes 344072 | tf_op jit(solution)/shard_map/ppermute | solution.py:747
  7.2 0.1 copy.19
  7.3 0.1 copy.20
  7.4 1.9 %collective-permute-start.1 = (bf16[14,32,128]{2,1,0:T(8,128)(2,1)S(1)}, bf16[14,32,128]{2,1,0:T(8,128)(2,1)S(1)}, u32[]{:S(2)}, u32[]{:S(2)}) collective-permute-start(bf16[14,32,128]{2,1,0:T(8,128)(2,1)S(1)} %pad_maximum_fusion.3), channel_id=1, source_target_pairs={{32,0},{64,32},{96,64},{128,96},{160,128},{192,160},{224,192},{33,... | collective-permute-start | bytes 344072 | tf_op jit(solution)/shard_map/ppermute | solution.py:747
  9.3 0.0 copy-done
  9.4 0.0 copy-start.9
  9.4 0.7 copy-done.9
  10.1 0.1 copy.16
  10.2 0.0 copy-start.6
  10.2 0.1 reshape.33
  10.3 0.6 copy-done.6
  10.9 0.1 pad.62.clone
  11.0 0.0 collective-permute-done.top
  11.0 0.1 copy.21
  11.1 0.1 copy.22
  11.2 6.5 %collective-permute-done.1.bot = bf16[14,32,128]{2,1,0:T(8,128)(2,1)S(1)} collective-permute-done((bf16[14,32,128]{2,1,0:T(8,128)(2,1)S(1)}, bf16[14,32,128]{2,1,0:T(8,128)(2,1)S(1)}, u32[]{:S(2)}, u32[]{:S(2)}) %collective-permute-start.1) | collective-permute-done | bytes 114720 | tf_op jit(solution)/shard_map/ppermute | solution.py:747
  17.7 0.1 copy.23
  17.8 0.0 copy-start.5
  17.8 0.1 copy.24
  17.9 0.6 copy-done.5
  18.5 0.1 maximum_maximum_fusion.tall
  18.7 0.0 copy-start.1
  18.7 1.4 %collective-permute-start.3 = (bf16[93,8,128]{2,1,0:T(8,128)(2,1)S(1)}, bf16[93,8,128]{2,1,0:T(8,128)(2,1)S(1)}, u32[]{:S(2)}, u32[]{:S(2)}) collective-permute-start(bf16[93,8,128]{2,1,0:T(8,128)(2,1)S(1)} %pad_maximum_fusion.1), channel_id=1, source_target_pairs={{1,0},{2,1},{3,2},{4,3},{5,4},{6,5},{7,6},{8,7},{9,8},{10,9},{11,1... | collective-permute-start | bytes 571400 | tf_op jit(solution)/shard_map/ppermute | solution.py:747
  20.1 0.0 copy-start.10
  20.2 0.0 copy-start.7
  20.2 3.0 %collective-permute-start.2 = (bf16[93,8,128]{2,1,0:T(8,128)(2,1)S(1)}, bf16[93,8,128]{2,1,0:T(8,128)(2,1)S(1)}, u32[]{:S(2)}, u32[]{:S(2)}) collective-permute-start(bf16[93,8,128]{2,1,0:T(8,128)(2,1)S(1)} %pad_maximum_fusion), channel_id=1, source_target_pairs={{0,1},{1,2},{2,3},{3,4},{4,5},{5,6},{6,7},{7,8},{8,9},{9,10},{10,1... | collective-permute-start | bytes 571400 | tf_op jit(solution)/shard_map/ppermute | solution.py:747
  23.2 0.0 copy-done.10
  23.3 0.1 pad_add_fusion.meta
  23.3 0.0 copy-done.7
  23.4 0.0 collective-permute-done.3.right
  23.4 0.9 collective-permute-done.2.left
  24.3 0.0 copy-done.1
  24.3 6.8 %shard_map.118 = (bf16[32,16,384]{2,1,0:T(8,128)(2,1)}, f32[1024,128]{1,0:T(8,128)S(1)}, bf16[68,48,128]{2,1,0:T(8,128)(2,1)}) custom-call(s32[194]{0:T(256)S(1)} %pad_add_fusion.meta, bf16[14,32,128]{2,1,0:T(8,128)(2,1)S(1)} %collective-permute-done.top, bf16[64,32,128]{2,1,0:T(8,128)(2,1)S(1)} %bitcast.46, ...), custom_call_target="tpu_custom_call" | custom-call | tf_op jit(solution)/shard_map/pallas_call | solution.py:618
  31.1 0.0 copy-start.4
  31.1 13.8 %all-to-all-start = ((bf16[32,16,384]{2,1,0:T(8,128)(2,1)}), bf16[32,16,384]{2,1,0:T(8,128)(2,1)S(1)}, u32[]{:S(2)}, u32[]{:S(2)}) async-start(bf16[32,16,384]{2,1,0:T(8,128)(2,1)} %get-tuple-element.11), calls=%async_computation | async-start | bytes 786432 | tf_op jit(solution)/shard_map/all_to_all | solution.py:797
  44.9 0.1 fusion.4
  45.0 0.0 copy-start.11
  45.0 0.0 copy-done.4
  45.0 0.6 copy-done.11
  45.6 0.0 copy-start.12
  45.6 0.0 copy-start.8
  45.6 0.0 copy-start.3
  45.6 0.4 collective-permute-start.4
  46.0 0.3 copy-done.12
  46.3 0.0 copy-done.8
  46.3 0.2 copy-done.3
  46.6 9.0 %shard_map.119 = (bf16[3456,128]{1,0:T(8,128)(2,1)}, bf16[3648,128]{1,0:T(8,128)(2,1)}, f32[8,128]{1,0:T(8,128)S(1)}) custom-call(s32[194]{0:T(256)S(1)} %pad_add_fusion.meta, f32[1024,128]{1,0:T(8,128)S(1)} %get-tuple-element.12.dec, bf16[3,32,128]{2,1,0:T(8,128)(2,1)S(1)} %maximum_maximum_fusion.tall, bf16[93,8,128]{2,1,0:T(8,128)(2,1)S(1)} %collective-permute-done.2.left, ...), custom_call_target="tpu_custom_call" | custom-call | tf_op jit(solution)/shard_map/pallas_call | solution.py:618
  55.6 0.0 collective-permute-done.4.other
  55.6 5.2 %all-to-all-done.strip = bf16[32,16,384]{2,1,0:T(8,128)(2,1)S(1)} async-done(((bf16[32,16,384]{2,1,0:T(8,128)(2,1)}), bf16[32,16,384]{2,1,0:T(8,128)(2,1)S(1)}, u32[]{:S(2)}, u32[]{:S(2)}) %all-to-all-start) | async-done | bytes 393248 | tf_op jit(solution)/shard_map/all_to_all | solution.py:797
  60.8 19.0 %shard_map.120 = bf16[32,40,128]{2,1,0:T(8,128)(2,1)} custom-call(s32[194]{0:T(256)S(1)} %pad_add_fusion.meta, bf16[32,16,384]{2,1,0:T(8,128)(2,1)S(1)} %all-to-all-done.strip, bf16[1136,128]{1,0:T(8,128)(2,1)S(1)} %fusion.1.mine, bf16[1136,128]{1,0:T(8,128)(2,1)S(1)} %collective-permute-done.4.other, f32[8,128]{1,0:T(8,128)S(1)} %get-tuple-element.13._), custom_call_target="tpu_custom_call" | custom-call | tf_op jit(solution)/shard_map/pallas_call | solution.py:618
  79.8 6.7 %all-to-all-start.1 = ((bf16[32,40,128]{2,1,0:T(8,128)(2,1)}), bf16[32,40,128]{2,1,0:T(8,128)(2,1)S(1)}, u32[]{:S(2)}, u32[]{:S(2)}) async-start(bf16[32,40,128]{2,1,0:T(8,128)(2,1)} %shard_map.120), calls=%async_computation.1 | async-start | bytes 655360 | tf_op jit(solution)/shard_map/all_to_all | solution.py:804
  86.5 0.0 copy-start.2
  86.5 5.4 %shard_map.121.lpips = f32[640,128]{1,0:T(8,128)S(1)} custom-call(s32[194]{0:T(256)S(1)} %pad_add_fusion.meta, bf16[3456,128]{1,0:T(8,128)(2,1)} %get-tuple-element.14.feat, bf16[3648,128]{1,0:T(8,128)(2,1)} %get-tuple-element.15.slope_one, f32[3,32,128]{2,1,0:T(8,128)S(1)} %bitcast_convert_fusion.1.v_first, bf16[3,3,64,64]{3,2,1,0:T(8,128)(2,1)S(1)} %copy-done.3), custom_call_target="tpu_custom_call" | custom-call | tf_op jit(solution)/shard_map/pallas_call | solution.py:618
  91.9 9.1 %all-to-all-done.1.parts = bf16[32,40,128]{2,1,0:T(8,128)(2,1)S(1)} async-done(((bf16[32,40,128]{2,1,0:T(8,128)(2,1)}), bf16[32,40,128]{2,1,0:T(8,128)(2,1)S(1)}, u32[]{:S(2)}, u32[]{:S(2)}) %all-to-all-start.1) | async-done | bytes 327712 | tf_op jit(solution)/shard_map/all_to_all | solution.py:804
  101.0 0.0 copy-done.2
  101.0 4.2 %shard_map.122 = bf16[64,32,128]{2,1,0:T(8,128)(2,1)} custom-call(s32[194]{0:T(256)S(1)} %pad_add_fusion.meta, bf16[32,40,128]{2,1,0:T(8,128)(2,1)S(1)} %all-to-all-done.1.parts, f32[640,128]{1,0:T(8,128)S(1)} %shard_map.121.lpips, bf16[68,48,128]{2,1,0:T(8,128)(2,1)S(1)} %copy-done.2, bf16[64,32,128]{2,1,0:T(8,128)(2,1)S(1)} %bitcast.47, ...), custom_call_target="tpu_custom_call" | custom-call | tf_op jit(solution)/shard_map/pallas_call | solution.py:618
  (24 shorter events, 0.3 us)
Async XLA Ops:
  0.9 8.4 %copy-start = (bf16[1,64,32,128]{3,2,1,0:T(8,128)(2,1)S(1)}, bf16[1,64,32,128]{3,2,1,0:T(8,128)(2,1)}, u32[]{:S(2)}) copy-start(bf16[1,64,32,128]{3,2,1,0:T(8,128)(2,1)} %param.12) | copy-start | bytes 1572868
  2.1 8.9 %collective-permute-start = (bf16[14,32,128]{2,1,0:T(8,128)(2,1)S(1)}, bf16[14,32,128]{2,1,0:T(8,128)(2,1)S(1)}, u32[]{:S(2)}, u32[]{:S(2)}) collective-permute-start(bf16[14,32,128]{2,1,0:T(8,128)(2,1)S(1)} %pad_maximum_fusion.2), channel_id=1, source_target_pairs={{0,32},{32,64},{64,96},{96,128},{128,160},{160,192},{192,224},{1,3... | collective-permute-start | bytes 344072 | tf_op jit(solution)/shard_map/ppermute | solution.py:747
  7.4 10.3 %collective-permute-start.1 = (bf16[14,32,128]{2,1,0:T(8,128)(2,1)S(1)}, bf16[14,32,128]{2,1,0:T(8,128)(2,1)S(1)}, u32[]{:S(2)}, u32[]{:S(2)}) collective-permute-start(bf16[14,32,128]{2,1,0:T(8,128)(2,1)S(1)} %pad_maximum_fusion.3), channel_id=1, source_target_pairs={{32,0},{64,32},{96,64},{128,96},{160,128},{192,160},{224,192},{33,... | collective-permute-start | bytes 344072 | tf_op jit(solution)/shard_map/ppermute | solution.py:747
  9.4 0.7 copy-start.9
  10.2 0.7 copy-start.6
  17.8 0.7 copy-start.5
  18.7 5.6 %copy-start.1 = (bf16[3,3,128,128]{3,2,1,0:T(8,128)(2,1)S(1)}, bf16[3,3,128,128]{3,2,1,0:T(8,128)(2,1)}, u32[]{:S(2)}) copy-start(bf16[3,3,128,128]{3,2,1,0:T(8,128)(2,1)} %w_mid.3) | copy-start | bytes 884740
  18.7 4.6 %collective-permute-start.3 = (bf16[93,8,128]{2,1,0:T(8,128)(2,1)S(1)}, bf16[93,8,128]{2,1,0:T(8,128)(2,1)S(1)}, u32[]{:S(2)}, u32[]{:S(2)}) collective-permute-start(bf16[93,8,128]{2,1,0:T(8,128)(2,1)S(1)} %pad_maximum_fusion.1), channel_id=1, source_target_pairs={{1,0},{2,1},{3,2},{4,3},{5,4},{6,5},{7,6},{8,7},{9,8},{10,9},{11,1... | collective-permute-start | bytes 571400 | tf_op jit(solution)/shard_map/ppermute | solution.py:747
  20.1 3.1 %copy-start.10 = (s32[1,64,1]{1,2,0:T(1,128)S(1)}, s32[1,64,1]{1,2,0:T(1,128)}, u32[]{:S(2)}) copy-start(s32[1,64,1]{1,2,0:T(1,128)} %param.20) | copy-start | bytes 772
  20.2 3.2 %copy-start.7 = (bf16[3,3,128,3]{2,3,1,0:T(4,128)(2,1)S(1)}, bf16[3,3,128,3]{2,3,1,0:T(4,128)(2,1)}, u32[]{:S(2)}) copy-start(bf16[3,3,128,3]{2,3,1,0:T(4,128)(2,1)} %param.14) | copy-start | bytes 20740
  20.2 4.1 %collective-permute-start.2 = (bf16[93,8,128]{2,1,0:T(8,128)(2,1)S(1)}, bf16[93,8,128]{2,1,0:T(8,128)(2,1)S(1)}, u32[]{:S(2)}, u32[]{:S(2)}) collective-permute-start(bf16[93,8,128]{2,1,0:T(8,128)(2,1)S(1)} %pad_maximum_fusion), channel_id=1, source_target_pairs={{0,1},{1,2},{2,3},{3,4},{4,5},{5,6},{6,7},{7,8},{8,9},{9,10},{10,1... | collective-permute-start | bytes 571400 | tf_op jit(solution)/shard_map/ppermute | solution.py:747
  31.1 13.9 %copy-start.4 = (bf16[1,4,4,64,128]{4,3,2,1,0:T(8,128)(2,1)S(1)}, bf16[1,4,4,64,128]{4,3,2,1,0:T(8,128)(2,1)}, u32[]{:S(2)}) copy-start(bf16[1,4,4,64,128]{4,3,2,1,0:T(8,128)(2,1)} %param.22) | copy-start | bytes 786436
  31.1 29.7 %all-to-all-start = ((bf16[32,16,384]{2,1,0:T(8,128)(2,1)}), bf16[32,16,384]{2,1,0:T(8,128)(2,1)S(1)}, u32[]{:S(2)}, u32[]{:S(2)}) async-start(bf16[32,16,384]{2,1,0:T(8,128)(2,1)} %get-tuple-element.11), calls=%async_computation | async-start | bytes 786432 | tf_op jit(solution)/shard_map/all_to_all | solution.py:797
  45.0 0.7 copy-start.11
  45.6 0.7 copy-start.12
  45.6 0.7 copy-start.8
  45.6 0.9 copy-start.3
  45.6 9.9 %collective-permute-start.4 = (bf16[1136,128]{1,0:T(8,128)(2,1)S(1)}, bf16[1136,128]{1,0:T(8,128)(2,1)S(1)}, u32[]{:S(2)}, u32[]{:S(2)}) collective-permute-start(bf16[1136,128]{1,0:T(8,128)(2,1)S(1)} %fusion.1.mine), channel_id=1, source_target_pairs={{0,1},{1,0},{2,3},{3,2},{4,5},{5,4},{6,7},{7,6},{8,9},{9,8},{10,11... | collective-permute-start | bytes 872456 | tf_op jit(solution)/shard_map/ppermute | solution.py:799
  79.8 21.2 %all-to-all-start.1 = ((bf16[32,40,128]{2,1,0:T(8,128)(2,1)}), bf16[32,40,128]{2,1,0:T(8,128)(2,1)S(1)}, u32[]{:S(2)}, u32[]{:S(2)}) async-start(bf16[32,40,128]{2,1,0:T(8,128)(2,1)} %shard_map.120), calls=%async_computation.1 | async-start | bytes 655360 | tf_op jit(solution)/shard_map/all_to_all | solution.py:804
  86.5 14.5 %copy-start.2 = (bf16[68,48,128]{2,1,0:T(8,128)(2,1)S(1)}, bf16[68,48,128]{2,1,0:T(8,128)(2,1)}, u32[]{:S(2)}) copy-start(bf16[68,48,128]{2,1,0:T(8,128)(2,1)} %get-tuple-element.16.slope) | copy-start | bytes 2506756

commit v3 on v2

--- a/solution.py
+++ b/solution.py
@@ -253,9 +253,7 @@
     ones = ((iota((128, 128), 0) >> 6) == (iota((128, 128), 1) >> 6)).astype(F32).astype(BF)
 
     def half_sum(v):
-        high = v.astype(BF)
-        low = (v - high.astype(F32)).astype(BF)
-        return mm(high, ones) + mm(low, ones)
+        return mm(v.astype(BF), ones)
 
     def second(i, carry):
         v = conv_rows(one, i * 8, 8, w2[...])
@@ -307,6 +305,7 @@
 
 
 STOP = object()
+FAR = 16
 STEPS = 6
 HALF = STEPS + 1
 TILES = 2 * HALF
@@ -315,7 +314,7 @@
 
 
 def critic_kernel(
-    meta, strip, mine, other, _, out,
+    meta, strip, mine, other, far, far_other, _, out,
     strip32, grads, w_pre, w_one, w_two, w_back, score, distance, row_gap, row_gap_back, x_all, x_all_b, pre, pre_b, act, act_b,
     two, two_b, cols, cols_b, jobs,
 ):
@@ -338,21 +337,19 @@
     strip32[IMG_W:, :] = jnp.zeros((8, 256), F32)
     grads[...] = jnp.zeros(grads.shape, F32)
     w_back[...] = jnp.zeros(w_back.shape, BF)
-    for g, source in enumerate((mine, other)):
+    for g, source in enumerate((mine, other, far, far_other)):
         w_one[g] = source[1024:1120, :]
         w_pre[g] = (0.5 * taller(source[1024:1120, :].astype(F32))).T.astype(BF)
         score[g] = taller(source[1120:1136, :].astype(F32)).T
         for i in range(4):
             first, second = (
-                pltpu.roll(
-                    source[i * 256 + k * 128 : i * 256 + (k + 1) * 128, :].astype(F32).T, 64, 1
-                )
+                source[i * 256 + k * 128 : i * 256 + (k + 1) * 128, :].astype(F32).T
                 for k in range(2)
             )
             at = slice((i // 2) * 128, (i // 2 + 1) * 128)
-            w_two[g, i % 2, 0:128, at] = jnp.where(upper, second, first).astype(BF)
-            w_two[g, i % 2, 128:256, at] = jnp.where(upper, first, 0.0).astype(BF)
-            w_two[g, i % 2, 256:384, at] = jnp.where(upper, 0.0, second).astype(BF)
+            w_two[g, i % 2, 0:128, at] = jnp.where(upper, first, second).astype(BF)
+            w_two[g, i % 2, 128:256, at] = jnp.where(upper, 0.0, first).astype(BF)
+            w_two[g, i % 2, 256:384, at] = jnp.where(upper, second, 0.0).astype(BF)
         for par in range(2):
             for p in range(2):
                 for t in range(2):
@@ -360,7 +357,7 @@
                     for kind, j in ((0, 1 + p), (1 + p, 3 - 3 * p)):
                         w_back[
                             g,
-                            (par * 2 + p) * 64 : (par * 2 + p + 1) * 64,
+                            (par * 2 + 1 - p) * 64 : (par * 2 + 2 - p) * 64,
                             (t * 3 + kind) * 128 : (t * 3 + kind + 1) * 128,
                         ] = 0.5 * source[i * 256 + j * 64 : i * 256 + (j + 1) * 64, :]
     for t in (two, two_b):
@@ -391,7 +388,8 @@
         return meta[2 + 2 * CROPS + q]
 
     def job(q, live, x_all, pre, act, two, cols):
-        top, left, g = anchor(q, 0), anchor(q, 1), (owner_of(q) ^ me) & 1
+        top, left, apart = anchor(q, 0), anchor(q, 1), owner_of(q) ^ me
+        g = (apart & 1) + 2 * ((apart // FAR) & 1)
         y0 = first_row - top
         v0 = lax.shift_right_arithmetic(y0 - 3, 2)
         e = 4 * v0 - y0 + 6
@@ -518,13 +516,14 @@
         here = pl.ds(aligned((left >> 3) * 8 + GRAD_PAD, 8), CROP + 8)
         grads[here, :] = grads[here, :] + jnp.where(keep, placed, 0.0)
 
-    count = jnp.int32(0)
+    count, seen, turn = jnp.int32(0), jnp.int32(0), (me // FAR) & 1
     for q in range(CROPS):
         y0 = first_row - anchor(q, 0)
-        shared = (owner_of(q) >> 1) == (me >> 1)
-        shared = shared & (y0 < CROP) & (y0 + SHARE > 0)
+        shared = ((owner_of(q) ^ me) & (COLS - 2 - FAR)) == 0
+        shared = (shared & (y0 < CROP) & (y0 + SHARE > 0)).astype(jnp.int32)
         jobs[count] = q
-        count = count + shared.astype(jnp.int32)
+        count = count + shared * ((seen & 1) == turn).astype(jnp.int32)
+        seen = seen + shared
 
     def two_crops(k, carry):
         last = jnp.minimum(2 * k + 1, count - 1)
@@ -684,13 +683,13 @@
     w = jnp.pad(first, ((0, 0), (0, 0), (0, 1), (0, 0)))
     w = jnp.transpose(w, (1, 0, 2, 3)).reshape(4, 16, 64)
     w = jnp.concatenate(
-        [jnp.pad(w, ((0, 2), (0, 0), (0, 0))), jnp.pad(w, ((2, 0), (0, 0), (0, 0)))], -1
+        [jnp.pad(w, ((2, 0), (0, 0), (0, 0))), jnp.pad(w, ((0, 2), (0, 0), (0, 0)))], -1
     ).reshape(96, 128)
     score = jnp.pad(score[None], ((0, 15), (0, 0)))
     return jnp.concatenate([second.reshape(1024, 128), w, score], 0)
 
 
-def critics(meta, strip, mine, other, after):
+def critics(meta, strip, weights, after):
     pair = [
         ((96, LANES), BF),
         ((128, LANES), F32),
@@ -704,17 +703,17 @@
         [
             ((IMG_W + 8, 256), F32),
             ((IMG_W + 24, 256), F32),
-            ((2, 128, 128), BF),
-            ((2, 96, 128), BF),
-            ((2, 2, 384, 256), BF),
-            ((2, 256, 768), BF),
-            ((2, 128, 128), F32),
+            ((4, 128, 128), BF),
+            ((4, 96, 128), BF),
+            ((4, 2, 384, 256), BF),
+            ((4, 256, 768), BF),
+            ((4, 128, 128), F32),
             ((CROP + 8, 384), F32),
             ((TILES * 16, 128), F32),
             ((128, TILES * 16), F32),
         ]
         + [buffer for buffer in pair for _ in range(2)],
-        (meta, strip, mine, other, after),
+        (meta, strip, *weights, after),
         unused=1,
         lists=[pltpu.SMEM((CROPS,), jnp.int32)],
     )
@@ -797,10 +796,12 @@
     strip = lax.all_to_all(pay, "col", split_axis=0, concat_axis=0, tiled=True)
     mine = critic_weights(critic_first[0], critic_second[0], critic_score[0])
     other = lax.ppermute(mine, "col", [(i, i ^ 1) for i in range(COLS)])
+    far = lax.ppermute(mine, "col", [(i, i ^ FAR) for i in range(COLS)])
+    far_other = lax.ppermute(far, "col", [(i, i ^ 1) for i in range(COLS)])
     feat, slope_one, done = percept(
         meta, dec, tall, left, right, vgg_small, vgg_second, perceptual_weights
     )
-    grads = critics(meta, strip, mine, other, done)
+    grads = critics(meta, strip, (mine, other, far, far_other), done)
     parts = lax.all_to_all(grads, "col", split_axis=0, concat_axis=0, tiled=True)
     lpips = percept_back(meta, in_hbm(feat), in_hbm(slope_one), vgg_small, vgg_second)
     return finish(meta, parts, lpips, slope, feats, conv_mid, out_small)[None]

time: 106 us -> 113 us (1.066)
  starting transfers between devices: 32.2 us -> 38.6 us
  Pallas kernels: 44.4 us -> 38.5 us
  waiting for transfers between devices: 21.7 us -> 27 us
    ppermute x0 -> x2, waiting for transfers between devices: none -> 10.8 us  [the longest x1 10.8 us: local(): far = lax.ppermute(mine, 'col', [(i, i ^ FAR) for i in range(COLS)])]
    pallas_call x5, Pallas kernels: 44.4 us -> 38.5 us  [call(): pl.pallas_call(kernel, in_specs=specs, out_specs=jax.tree.map(lambda _: p...]
    all_to_all x1, waiting for transfers between devices: 5.19 us -> 0.01 us  [local(): strip = lax.all_to_all(pay, 'col', split_axis=0, concat_axis=0, tiled=True)]
    all_to_all x1, starting transfers between devices: 6.65 us -> 11.5 us  [local(): lax.all_to_all(grads, 'col', split_axis=0, concat_axis=0, tiled=True)]
    ppermute x0 -> x2, starting transfers between devices: none -> 1.89 us  [the longest x1 1.88 us: local(): far = lax.ppermute(mine, 'col', [(i, i ^ FAR) for i in range(COLS)])]
    unnamed x27 -> x31, local copies, waits for them, and re-layouts: 3.16 us -> 4.29 us
  transfers between devices with their start and end apart: 7 -> 9, of which waited for: 4 -> 4; matrix products, arithmetic and copies ran while one was open for 1% -> 1% of each run, Pallas kernels for 14% -> 12%
where the time goes in v3:
time: 113 us; the launch traced here: 112 us
  starting transfers between devices  38.6 us (34%)
  Pallas kernels  38.5 us (34%)
  waiting for transfers between devices  27 us (24%)
  local copies, waits for them, and re-layouts  7.33 us (6%)
    pallas_call x5, Pallas kernels, call(): pl.pallas_call(kernel, in_specs=specs, out_specs=jax.tree.map(lambda _: p...  38.5 us
    all_to_all x1, starting transfers between devices, local(): strip = lax.all_to_all(pay, 'col', split_axis=0, concat_axis=0, tiled=True)  13.8 us
    all_to_all x1, starting transfers between devices, local(): lax.all_to_all(grads, 'col', split_axis=0, concat_axis=0, tiled=True)  11.5 us
    ppermute x1, waiting for transfers between devices, local(): far = lax.ppermute(mine, 'col', [(i, i ^ FAR) for i in range(COLS)])  10.8 us
    all_to_all x1, waiting for transfers between devices, local(): lax.all_to_all(grads, 'col', split_axis=0, concat_axis=0, tiled=True)  8.9 us
    ppermute x2, starting transfers between devices, exchange(): lax.ppermute(low, axis, forward)  8.06 us
    ppermute x2, waiting for transfers between devices, exchange(): lax.ppermute(high, axis, backward)  6.4 us
    unnamed x31, local copies, waits for them, and re-layouts  4.29 us
  transfers between devices with their start and end apart: 9, of which 4 were waited for; matrix products, arithmetic and copies ran while one was open for 1% of the time, Pallas kernels for 12%

profile of v3, /device:TPU:6, one launch (start us, length us, event | category | flops | bytes accessed | tf_op | source)
XLA Modules:
  0.0 112.1 jit_solution(16924537032797192286)
XLA Ops:
  0.0 0.9 slice_bitcast_fusion.2
  0.9 0.0 copy-start
  0.9 0.1 copy.17
  1.0 0.1 copy.18
  1.1 1.0 slice_bitcast_fusion
  2.1 5.0 %collective-permute-start = (bf16[14,32,128]{2,1,0:T(8,128)(2,1)S(1)}, bf16[14,32,128]{2,1,0:T(8,128)(2,1)S(1)}, u32[]{:S(2)}, u32[]{:S(2)}) collective-permute-start(bf16[14,32,128]{2,1,0:T(8,128)(2,1)S(1)} %pad_maximum_fusion.2), channel_id=1, source_target_pairs={{0,32},{32,64},{64,96},{96,128},{128,160},{160,192},{192,224},{1,3... | collective-permute-start | bytes 344072 | tf_op jit(solution)/shard_map/ppermute | solution.py:746
  7.2 0.1 copy.19
  7.3 0.1 copy.20
  7.4 1.9 %collective-permute-start.1 = (bf16[14,32,128]{2,1,0:T(8,128)(2,1)S(1)}, bf16[14,32,128]{2,1,0:T(8,128)(2,1)S(1)}, u32[]{:S(2)}, u32[]{:S(2)}) collective-permute-start(bf16[14,32,128]{2,1,0:T(8,128)(2,1)S(1)} %pad_maximum_fusion.3), channel_id=1, source_target_pairs={{32,0},{64,32},{96,64},{128,96},{160,128},{192,160},{224,192},{33,... | collective-permute-start | bytes 344072 | tf_op jit(solution)/shard_map/ppermute | solution.py:746
  9.3 0.0 copy-done
  9.4 0.0 copy-start.11
  9.4 0.7 copy-done.11
  10.1 0.1 copy.16
  10.2 0.0 copy-start.8
  10.2 0.1 reshape.33
  10.3 0.6 copy-done.8
  10.9 0.1 pad.62.clone
  11.0 0.1 fusion.4
  11.1 0.0 collective-permute-done.top
  11.1 0.1 copy.21
  11.2 0.1 copy.22
  11.3 6.4 %collective-permute-done.1.bot = bf16[14,32,128]{2,1,0:T(8,128)(2,1)S(1)} collective-permute-done((bf16[14,32,128]{2,1,0:T(8,128)(2,1)S(1)}, bf16[14,32,128]{2,1,0:T(8,128)(2,1)S(1)}, u32[]{:S(2)}, u32[]{:S(2)}) %collective-permute-start.1) | collective-permute-done | bytes 114720 | tf_op jit(solution)/shard_map/ppermute | solution.py:746
  17.7 0.1 copy.23
  17.8 0.0 copy-start.7
  17.8 0.1 copy.24
  17.9 0.6 copy-done.7
  18.5 0.1 maximum_maximum_fusion.tall
  18.7 0.0 copy-start.1
  18.7 1.4 %collective-permute-start.3 = (bf16[93,8,128]{2,1,0:T(8,128)(2,1)S(1)}, bf16[93,8,128]{2,1,0:T(8,128)(2,1)S(1)}, u32[]{:S(2)}, u32[]{:S(2)}) collective-permute-start(bf16[93,8,128]{2,1,0:T(8,128)(2,1)S(1)} %pad_maximum_fusion.1), channel_id=1, source_target_pairs={{1,0},{2,1},{3,2},{4,3},{5,4},{6,5},{7,6},{8,7},{9,8},{10,9},{11,1... | collective-permute-start | bytes 571400 | tf_op jit(solution)/shard_map/ppermute | solution.py:746
  20.1 0.0 copy-start.12
  20.2 0.0 copy-start.9
  20.2 3.0 %collective-permute-start.2 = (bf16[93,8,128]{2,1,0:T(8,128)(2,1)S(1)}, bf16[93,8,128]{2,1,0:T(8,128)(2,1)S(1)}, u32[]{:S(2)}, u32[]{:S(2)}) collective-permute-start(bf16[93,8,128]{2,1,0:T(8,128)(2,1)S(1)} %pad_maximum_fusion), channel_id=1, source_target_pairs={{0,1},{1,2},{2,3},{3,4},{4,5},{5,6},{6,7},{7,8},{8,9},{9,10},{10,1... | collective-permute-start | bytes 571400 | tf_op jit(solution)/shard_map/ppermute | solution.py:746
  23.2 0.0 copy-done.12
  23.3 0.1 pad_add_fusion.meta
  23.3 0.0 copy-done.9
  23.4 0.0 collective-permute-done.3.right
  23.4 0.9 collective-permute-done.2.left
  24.3 0.0 copy-done.1
  24.3 6.8 %shard_map.118 = (bf16[32,16,384]{2,1,0:T(8,128)(2,1)}, f32[1024,128]{1,0:T(8,128)S(1)}, bf16[68,48,128]{2,1,0:T(8,128)(2,1)}) custom-call(s32[194]{0:T(256)S(1)} %pad_add_fusion.meta, bf16[14,32,128]{2,1,0:T(8,128)(2,1)S(1)} %collective-permute-done.top, bf16[64,32,128]{2,1,0:T(8,128)(2,1)S(1)} %bitcast.46, ...), custom_call_target="tpu_custom_call" | custom-call | tf_op jit(solution)/shard_map/pallas_call | solution.py:617
  31.1 13.8 %all-to-all-start = ((bf16[32,16,384]{2,1,0:T(8,128)(2,1)}), bf16[32,16,384]{2,1,0:T(8,128)(2,1)S(1)}, u32[]{:S(2)}, u32[]{:S(2)}) async-start(bf16[32,16,384]{2,1,0:T(8,128)(2,1)} %get-tuple-element.11), calls=%async_computation | async-start | bytes 786432 | tf_op jit(solution)/shard_map/all_to_all | solution.py:796
  44.9 0.0 copy-start.13
  44.9 0.0 copy-done.6
  44.9 0.6 copy-done.13
  45.6 1.9 %collective-permute-start.5 = (bf16[1136,128]{1,0:T(8,128)(2,1)S(1)}, bf16[1136,128]{1,0:T(8,128)(2,1)S(1)}, u32[]{:S(2)}, u32[]{:S(2)}) collective-permute-start(bf16[1136,128]{1,0:T(8,128)(2,1)S(1)} %fusion.1.mine), channel_id=1, source_target_pairs={{0,16},{1,17},{2,18},{3,19},{4,20},{5,21},{6,22},{7,23},{8,24},{9,... | collective-permute-start | bytes 872456 | tf_op jit(solution)/shard_map/ppermute | solution.py:799
  47.5 0.0 collective-permute-start.4
  47.5 10.8 %collective-permute-done.5.far = bf16[1136,128]{1,0:T(8,128)(2,1)S(1)} collective-permute-done((bf16[1136,128]{1,0:T(8,128)(2,1)S(1)}, bf16[1136,128]{1,0:T(8,128)(2,1)S(1)}, u32[]{:S(2)}, u32[]{:S(2)}) %collective-permute-start.5) | collective-permute-done | bytes 290848 | tf_op jit(solution)/shard_map/ppermute | solution.py:799
  58.2 0.0 collective-permute-start.6
  58.2 0.0 copy-done.14
  58.3 0.0 copy-done.10
  58.3 0.0 copy-done.3
  58.3 8.0 %shard_map.119 = (bf16[3456,128]{1,0:T(8,128)(2,1)}, bf16[3648,128]{1,0:T(8,128)(2,1)}, f32[8,128]{1,0:T(8,128)S(1)}) custom-call(s32[194]{0:T(256)S(1)} %pad_add_fusion.meta, f32[1024,128]{1,0:T(8,128)S(1)} %get-tuple-element.12.dec, bf16[3,32,128]{2,1,0:T(8,128)(2,1)S(1)} %maximum_maximum_fusion.tall, bf16[93,8,128]{2,1,0:T(8,128)(2,1)S(1)} %collective-permute-done.2.left, ...), custom_call_target="tpu_custom_call" | custom-call | tf_op jit(solution)/shard_map/pallas_call | solution.py:617
  66.2 0.0 collective-permute-done.4.other
  66.3 0.0 collective-permute-done.6.far_other
  66.3 0.0 copy-start.4
  66.3 0.7 copy-done.4
  67.0 0.0 all-to-all-done.strip
  67.0 1.0 copy-done.5
  67.9 14.2 %shard_map.120 = bf16[32,40,128]{2,1,0:T(8,128)(2,1)} custom-call(s32[194]{0:T(256)S(1)} %pad_add_fusion.meta, bf16[32,16,384]{2,1,0:T(8,128)(2,1)S(1)} %all-to-all-done.strip, bf16[1136,128]{1,0:T(8,128)(2,1)S(1)} %fusion.1.mine, bf16[1136,128]{1,0:T(8,128)(2,1)S(1)} %collective-permute-done.4.other, bf16[1136,128]{1,0:T(8,128)(2,1)S(1)} %collective-permute-done.5.far, ...), custom_call_target="tpu_custom_call" | custom-call | tf_op jit(solution)/shard_map/pallas_call | solution.py:617
  82.1 11.5 %all-to-all-start.1 = ((bf16[32,40,128]{2,1,0:T(8,128)(2,1)}), bf16[32,40,128]{2,1,0:T(8,128)(2,1)S(1)}, u32[]{:S(2)}, u32[]{:S(2)}) async-start(bf16[32,40,128]{2,1,0:T(8,128)(2,1)} %shard_map.120), calls=%async_computation.1 | async-start | bytes 655360 | tf_op jit(solution)/shard_map/all_to_all | solution.py:805
  93.6 0.0 copy-start.2
  93.6 5.4 %shard_map.121.lpips = f32[640,128]{1,0:T(8,128)S(1)} custom-call(s32[194]{0:T(256)S(1)} %pad_add_fusion.meta, bf16[3456,128]{1,0:T(8,128)(2,1)} %get-tuple-element.14.feat, bf16[3648,128]{1,0:T(8,128)(2,1)} %get-tuple-element.15.slope_one, f32[3,32,128]{2,1,0:T(8,128)S(1)} %bitcast_convert_fusion.1.v_first, bf16[3,3,64,64]{3,2,1,0:T(8,128)(2,1)S(1)} %copy-done.3), custom_call_target="tpu_custom_call" | custom-call | tf_op jit(solution)/shard_map/pallas_call | solution.py:617
  99.0 8.9 %all-to-all-done.1.parts = bf16[32,40,128]{2,1,0:T(8,128)(2,1)S(1)} async-done(((bf16[32,40,128]{2,1,0:T(8,128)(2,1)}), bf16[32,40,128]{2,1,0:T(8,128)(2,1)S(1)}, u32[]{:S(2)}, u32[]{:S(2)}) %all-to-all-start.1) | async-done | bytes 327712 | tf_op jit(solution)/shard_map/all_to_all | solution.py:805
  107.9 0.0 copy-done.2
  107.9 4.2 %shard_map.122 = bf16[64,32,128]{2,1,0:T(8,128)(2,1)} custom-call(s32[194]{0:T(256)S(1)} %pad_add_fusion.meta, bf16[32,40,128]{2,1,0:T(8,128)(2,1)S(1)} %all-to-all-done.1.parts, f32[640,128]{1,0:T(8,128)S(1)} %shard_map.121.lpips, bf16[68,48,128]{2,1,0:T(8,128)(2,1)S(1)} %copy-done.2, bf16[64,32,128]{2,1,0:T(8,128)(2,1)S(1)} %bitcast.47, ...), custom_call_target="tpu_custom_call" | custom-call | tf_op jit(solution)/shard_map/pallas_call | solution.py:617
  (29 shorter events, 0.3 us)
Async XLA Ops:
  0.9 8.4 %copy-start = (bf16[1,64,32,128]{3,2,1,0:T(8,128)(2,1)S(1)}, bf16[1,64,32,128]{3,2,1,0:T(8,128)(2,1)}, u32[]{:S(2)}) copy-start(bf16[1,64,32,128]{3,2,1,0:T(8,128)(2,1)} %param.12) | copy-start | bytes 1572868
  2.1 8.9 %collective-permute-start = (bf16[14,32,128]{2,1,0:T(8,128)(2,1)S(1)}, bf16[14,32,128]{2,1,0:T(8,128)(2,1)S(1)}, u32[]{:S(2)}, u32[]{:S(2)}) collective-permute-start(bf16[14,32,128]{2,1,0:T(8,128)(2,1)S(1)} %pad_maximum_fusion.2), channel_id=1, source_target_pairs={{0,32},{32,64},{64,96},{96,128},{128,160},{160,192},{192,224},{1,3... | collective-permute-start | bytes 344072 | tf_op jit(solution)/shard_map/ppermute | solution.py:746
  7.4 10.3 %collective-permute-start.1 = (bf16[14,32,128]{2,1,0:T(8,128)(2,1)S(1)}, bf16[14,32,128]{2,1,0:T(8,128)(2,1)S(1)}, u32[]{:S(2)}, u32[]{:S(2)}) collective-permute-start(bf16[14,32,128]{2,1,0:T(8,128)(2,1)S(1)} %pad_maximum_fusion.3), channel_id=1, source_target_pairs={{32,0},{64,32},{96,64},{128,96},{160,128},{192,160},{224,192},{33,... | collective-permute-start | bytes 344072 | tf_op jit(solution)/shard_map/ppermute | solution.py:746
  9.4 0.7 copy-start.11
  10.2 0.7 copy-start.8
  17.8 0.7 copy-start.7
  18.7 5.6 %copy-start.1 = (bf16[3,3,128,128]{3,2,1,0:T(8,128)(2,1)S(1)}, bf16[3,3,128,128]{3,2,1,0:T(8,128)(2,1)}, u32[]{:S(2)}) copy-start(bf16[3,3,128,128]{3,2,1,0:T(8,128)(2,1)} %w_mid.3) | copy-start | bytes 884740
  18.7 4.6 %collective-permute-start.3 = (bf16[93,8,128]{2,1,0:T(8,128)(2,1)S(1)}, bf16[93,8,128]{2,1,0:T(8,128)(2,1)S(1)}, u32[]{:S(2)}, u32[]{:S(2)}) collective-permute-start(bf16[93,8,128]{2,1,0:T(8,128)(2,1)S(1)} %pad_maximum_fusion.1), channel_id=1, source_target_pairs={{1,0},{2,1},{3,2},{4,3},{5,4},{6,5},{7,6},{8,7},{9,8},{10,9},{11,1... | collective-permute-start | bytes 571400 | tf_op jit(solution)/shard_map/ppermute | solution.py:746
  20.1 3.1 %copy-start.12 = (s32[1,64,1]{1,2,0:T(1,128)S(1)}, s32[1,64,1]{1,2,0:T(1,128)}, u32[]{:S(2)}) copy-start(s32[1,64,1]{1,2,0:T(1,128)} %param.20) | copy-start | bytes 772
  20.2 3.2 %copy-start.9 = (bf16[3,3,128,3]{2,3,1,0:T(4,128)(2,1)S(1)}, bf16[3,3,128,3]{2,3,1,0:T(4,128)(2,1)}, u32[]{:S(2)}) copy-start(bf16[3,3,128,3]{2,3,1,0:T(4,128)(2,1)} %param.14) | copy-start | bytes 20740
  20.2 4.1 %collective-permute-start.2 = (bf16[93,8,128]{2,1,0:T(8,128)(2,1)S(1)}, bf16[93,8,128]{2,1,0:T(8,128)(2,1)S(1)}, u32[]{:S(2)}, u32[]{:S(2)}) collective-permute-start(bf16[93,8,128]{2,1,0:T(8,128)(2,1)S(1)} %pad_maximum_fusion), channel_id=1, source_target_pairs={{0,1},{1,2},{2,3},{3,4},{4,5},{5,6},{6,7},{7,8},{8,9},{9,10},{10,1... | collective-permute-start | bytes 571400 | tf_op jit(solution)/shard_map/ppermute | solution.py:746
  31.1 13.8 %copy-start.6 = (bf16[1,4,4,64,128]{4,3,2,1,0:T(8,128)(2,1)S(1)}, bf16[1,4,4,64,128]{4,3,2,1,0:T(8,128)(2,1)}, u32[]{:S(2)}) copy-start(bf16[1,4,4,64,128]{4,3,2,1,0:T(8,128)(2,1)} %param.22) | copy-start | bytes 786436
  31.1 35.9 %all-to-all-start = ((bf16[32,16,384]{2,1,0:T(8,128)(2,1)}), bf16[32,16,384]{2,1,0:T(8,128)(2,1)S(1)}, u32[]{:S(2)}, u32[]{:S(2)}) async-start(bf16[32,16,384]{2,1,0:T(8,128)(2,1)} %get-tuple-element.11), calls=%async_computation | async-start | bytes 786432 | tf_op jit(solution)/shard_map/all_to_all | solution.py:796
  44.9 0.7 copy-start.13
  45.5 12.7 %copy-start.14 = (f32[64]{0:T(128)S(1)}, f32[64]{0:T(128)}, u32[]{:S(2)}) copy-start(f32[64]{0:T(128)} %param.18) | copy-start | bytes 772
  45.5 12.7 %copy-start.10 = (bf16[3,3,3,64]{3,2,1,0:T(4,128)(2,1)S(1)}, bf16[3,3,3,64]{3,2,1,0:T(4,128)(2,1)}, u32[]{:S(2)}) copy-start(bf16[3,3,3,64]{3,2,1,0:T(4,128)(2,1)} %param.16) | copy-start | bytes 10372
  45.5 12.7 %copy-start.3 = (bf16[3,3,64,64]{3,2,1,0:T(8,128)(2,1)S(1)}, bf16[3,3,64,64]{3,2,1,0:T(8,128)(2,1)}, u32[]{:S(2)}) copy-start(bf16[3,3,64,64]{3,2,1,0:T(8,128)(2,1)} %v_second.3) | copy-start | bytes 221188
  45.6 12.7 %collective-permute-start.5 = (bf16[1136,128]{1,0:T(8,128)(2,1)S(1)}, bf16[1136,128]{1,0:T(8,128)(2,1)S(1)}, u32[]{:S(2)}, u32[]{:S(2)}) collective-permute-start(bf16[1136,128]{1,0:T(8,128)(2,1)S(1)} %fusion.1.mine), channel_id=1, source_target_pairs={{0,16},{1,17},{2,18},{3,19},{4,20},{5,21},{6,22},{7,23},{8,24},{9,... | collective-permute-start | bytes 872456 | tf_op jit(solution)/shard_map/ppermute | solution.py:799
  47.5 18.8 %collective-permute-start.4 = (bf16[1136,128]{1,0:T(8,128)(2,1)S(1)}, bf16[1136,128]{1,0:T(8,128)(2,1)S(1)}, u32[]{:S(2)}, u32[]{:S(2)}) collective-permute-start(bf16[1136,128]{1,0:T(8,128)(2,1)S(1)} %fusion.1.mine), channel_id=1, source_target_pairs={{0,1},{1,0},{2,3},{3,2},{4,5},{5,4},{6,7},{7,6},{8,9},{9,8},{10,11... | collective-permute-start | bytes 872456 | tf_op jit(solution)/shard_map/ppermute | solution.py:798
  58.2 8.0 %collective-permute-start.6 = (bf16[1136,128]{1,0:T(8,128)(2,1)S(1)}, bf16[1136,128]{1,0:T(8,128)(2,1)S(1)}, u32[]{:S(2)}, u32[]{:S(2)}) collective-permute-start(bf16[1136,128]{1,0:T(8,128)(2,1)S(1)} %collective-permute-done.5.far), channel_id=1, source_target_pairs={{0,1},{1,0},{2,3},{3,2},{4,5},{5,4},{6,7},{7,6},{8,9},{9,8},{10,11... | collective-permute-start | bytes 872456 | tf_op jit(solution)/shard_map/ppermute | solution.py:800
  66.3 0.7 copy-start.4
  67.0 1.0 copy-start.5
  82.1 25.8 %all-to-all-start.1 = ((bf16[32,40,128]{2,1,0:T(8,128)(2,1)}), bf16[32,40,128]{2,1,0:T(8,128)(2,1)S(1)}, u32[]{:S(2)}, u32[]{:S(2)}) async-start(bf16[32,40,128]{2,1,0:T(8,128)(2,1)} %shard_map.120), calls=%async_computation.1 | async-start | bytes 655360 | tf_op jit(solution)/shard_map/all_to_all | solution.py:805
  93.6 14.3 %copy-start.2 = (bf16[68,48,128]{2,1,0:T(8,128)(2,1)S(1)}, bf16[68,48,128]{2,1,0:T(8,128)(2,1)}, u32[]{:S(2)}) copy-start(bf16[68,48,128]{2,1,0:T(8,128)(2,1)} %get-tuple-element.16.slope) | copy-start | bytes 2506756

commit v4 on v3

--- a/solution.py
+++ b/solution.py
@@ -387,7 +387,7 @@
     def owner_of(q):
         return meta[2 + 2 * CROPS + q]
 
-    def job(q, live, x_all, pre, act, two, cols):
+    def job(q, x_all, pre, act, two, cols):
         top, left, apart = anchor(q, 0), anchor(q, 1), owner_of(q) ^ me
         g = (apart & 1) + 2 * ((apart // FAR) & 1)
         y0 = first_row - top
@@ -511,7 +511,7 @@
         yield
         placed = mm(pick, cols[...].astype(BF), 1, 1)
         y = wide & 63
-        keep = in_crop & (y >= 9) & (y < 9 + SHARE) & live
+        keep = in_crop & (y >= 9) & (y < 9 + SHARE)
         yield
         here = pl.ds(aligned((left >> 3) * 8 + GRAD_PAD, 8), CROP + 8)
         grads[here, :] = grads[here, :] + jnp.where(keep, placed, 0.0)
@@ -525,17 +525,20 @@
         count = count + shared * ((seen & 1) == turn).astype(jnp.int32)
         seen = seen + shared
 
+    first_set, second_set = (x_all, pre, act, two, cols), (x_all_b, pre_b, act_b, two_b, cols_b)
+
     def two_crops(k, carry):
-        last = jnp.minimum(2 * k + 1, count - 1)
-        running = [
-            job(jobs[2 * k], True, x_all, pre, act, two, cols),
-            job(jobs[last], 2 * k + 1 < count, x_all_b, pre_b, act_b, two_b, cols_b),
-        ]
+        running = [job(jobs[2 * k], *first_set), job(jobs[2 * k + 1], *second_set)]
         while running:
             running = [g for g in running if next(g, STOP) is not STOP]
         return carry
 
-    lax.fori_loop(0, (count + 1) >> 1, two_crops, 0)
+    lax.fori_loop(0, count >> 1, two_crops, 0)
+
+    @pl.when((count & 1) == 1)
+    def _():
+        for _ in job(jobs[count - 1], *first_set):
+            pass
 
     def pack(k, carry):
         block = grads[pl.ds(aligned(k * TW, 32), 48), :][GRAD_PAD - 2 : GRAD_PAD + 38]
@@ -792,11 +795,13 @@
     left, right = exchange(edge(TW - COL_HALO, TW), edge(0, COL_HALO), "col")
     out_small = colour_first(jnp.transpose(conv_out, (0, 1, 3, 2)))
     vgg_small = colour_first(vgg_first)
+    mine = critic_weights(critic_first[0], critic_second[0], critic_score[0])
+    left, right, sent = lax.optimization_barrier((left, right, mine))
+    far = lax.ppermute(sent, "col", [(i, i ^ FAR) for i in range(COLS)])
     pay, dec, slope = decode(meta, top, feats, bot, left, right, conv_mid, out_small)
+    pay, far = lax.optimization_barrier((pay, far))
     strip = lax.all_to_all(pay, "col", split_axis=0, concat_axis=0, tiled=True)
-    mine = critic_weights(critic_first[0], critic_second[0], critic_score[0])
     other = lax.ppermute(mine, "col", [(i, i ^ 1) for i in range(COLS)])
-    far = lax.ppermute(mine, "col", [(i, i ^ FAR) for i in range(COLS)])
     far_other = lax.ppermute(far, "col", [(i, i ^ 1) for i in range(COLS)])
     feat, slope_one, done = percept(
         meta, dec, tall, left, right, vgg_small, vgg_second, perceptual_weights

time: 113 us -> 106 us (0.938)
  starting transfers between devices: 38.6 us -> 34.4 us
  waiting for transfers between devices: 27 us -> 23 us
    ppermute x1, waiting for transfers between devices: 10.8 us -> 0.01 us  [local(): far = lax.ppermute(sent, 'col', [(i, i ^ FAR) for i in range(COLS)])]
    all_to_all x1, starting transfers between devices: 13.8 us -> 4.14 us  [local(): strip = lax.all_to_all(pay, 'col', split_axis=0, concat_axis=0, tiled=True)]
    ppermute x1, starting transfers between devices: 1.88 us -> 11 us  [local(): far = lax.ppermute(sent, 'col', [(i, i ^ FAR) for i in range(COLS)])]
    all_to_all x1, waiting for transfers between devices: 0.01 us -> 6.52 us  [local(): strip = lax.all_to_all(pay, 'col', split_axis=0, concat_axis=0, tiled=True)]
    all_to_all x1, starting transfers between devices: 11.5 us -> 7.22 us  [local(): lax.all_to_all(grads, 'col', split_axis=0, concat_axis=0, tiled=True)]
  transfers between devices with their start and end apart: 9 -> 9, of which waited for: 4 -> 4; matrix products, arithmetic and copies ran while one was open for 1% -> 1% of each run, Pallas kernels for 12% -> 19%
where the time goes in v4:
time: 106 us; the launch traced here: 105 us
  Pallas kernels  38.7 us (37%)
  starting transfers between devices  34.4 us (32%)
  waiting for transfers between devices  23 us (22%)
  local copies, waits for them, and re-layouts  8.05 us (8%)
    pallas_call x5, Pallas kernels, call(): pl.pallas_call(kernel, in_specs=specs, out_specs=jax.tree.map(lambda _: p...  38.7 us
    ppermute x1, starting transfers between devices, local(): far = lax.ppermute(sent, 'col', [(i, i ^ FAR) for i in range(COLS)])  11 us
    all_to_all x1, waiting for transfers between devices, local(): lax.all_to_all(grads, 'col', split_axis=0, concat_axis=0, tiled=True)  8.9 us
    ppermute x2, starting transfers between devices, exchange(): lax.ppermute(low, axis, forward)  8.06 us
    all_to_all x1, starting transfers between devices, local(): lax.all_to_all(grads, 'col', split_axis=0, concat_axis=0, tiled=True)  7.22 us
    ppermute x2, waiting for transfers between devices, exchange(): lax.ppermute(high, axis, backward)  7.21 us
    all_to_all x1, waiting for transfers between devices, local(): strip = lax.all_to_all(pay, 'col', split_axis=0, concat_axis=0, tiled=True)  6.52 us
    unnamed x31, local copies, waits for them, and re-layouts  5.01 us
  transfers between devices with their start and end apart: 9, of which 4 were waited for; matrix products, arithmetic and copies ran while one was open for 1% of the time, Pallas kernels for 19%

profile of v4, /device:TPU:6, one launch (start us, length us, event | category | flops | bytes accessed | tf_op | source)
XLA Modules:
  0.0 104.8 jit_solution(11392087966229812629)
XLA Ops:
  0.0 0.9 slice_bitcast_fusion.2
  0.9 0.0 copy-start
  0.9 0.1 copy.17
  1.0 0.1 copy.18
  1.1 1.0 slice_bitcast_fusion
  2.1 5.0 %collective-permute-start = (bf16[14,32,128]{2,1,0:T(8,128)(2,1)S(1)}, bf16[14,32,128]{2,1,0:T(8,128)(2,1)S(1)}, u32[]{:S(2)}, u32[]{:S(2)}) collective-permute-start(bf16[14,32,128]{2,1,0:T(8,128)(2,1)S(1)} %pad_maximum_fusion.2), channel_id=1, source_target_pairs={{0,32},{32,64},{64,96},{96,128},{128,160},{160,192},{192,224},{1,3... | collective-permute-start | bytes 344072 | tf_op jit(solution)/shard_map/ppermute | solution.py:749
  7.2 0.1 copy.19
  7.3 0.1 copy.20
  7.4 1.9 %collective-permute-start.1 = (bf16[14,32,128]{2,1,0:T(8,128)(2,1)S(1)}, bf16[14,32,128]{2,1,0:T(8,128)(2,1)S(1)}, u32[]{:S(2)}, u32[]{:S(2)}) collective-permute-start(bf16[14,32,128]{2,1,0:T(8,128)(2,1)S(1)} %pad_maximum_fusion.3), channel_id=1, source_target_pairs={{32,0},{64,32},{96,64},{128,96},{160,128},{192,160},{224,192},{33,... | collective-permute-start | bytes 344072 | tf_op jit(solution)/shard_map/ppermute | solution.py:749
  9.3 0.0 copy-done
  9.3 0.0 copy-start.8
  9.4 0.7 copy-done.8
  10.1 0.1 pad.62.clone
  10.2 0.1 fusion.4
  10.2 0.0 collective-permute-done.top
  10.3 0.1 copy.21
  10.4 0.1 copy.22
  10.5 7.2 %collective-permute-done.1.bot = bf16[14,32,128]{2,1,0:T(8,128)(2,1)S(1)} collective-permute-done((bf16[14,32,128]{2,1,0:T(8,128)(2,1)S(1)}, bf16[14,32,128]{2,1,0:T(8,128)(2,1)S(1)}, u32[]{:S(2)}, u32[]{:S(2)}) %collective-permute-start.1) | collective-permute-done | bytes 114720 | tf_op jit(solution)/shard_map/ppermute | solution.py:749
  17.7 0.1 copy.23
  17.8 0.0 copy-start.7
  17.8 0.1 copy.24
  17.9 0.6 copy-done.7
  18.5 0.1 maximum_maximum_fusion.tall
  18.7 0.0 copy-start.6
  18.7 1.4 %collective-permute-start.3 = (bf16[93,8,128]{2,1,0:T(8,128)(2,1)S(1)}, bf16[93,8,128]{2,1,0:T(8,128)(2,1)S(1)}, u32[]{:S(2)}, u32[]{:S(2)}) collective-permute-start(bf16[93,8,128]{2,1,0:T(8,128)(2,1)S(1)} %pad_maximum_fusion.1), channel_id=1, source_target_pairs={{1,0},{2,1},{3,2},{4,3},{5,4},{6,5},{7,6},{8,7},{9,8},{10,9},{11,1... | collective-permute-start | bytes 571400 | tf_op jit(solution)/shard_map/ppermute | solution.py:749
  20.2 3.0 %collective-permute-start.2 = (bf16[93,8,128]{2,1,0:T(8,128)(2,1)S(1)}, bf16[93,8,128]{2,1,0:T(8,128)(2,1)S(1)}, u32[]{:S(2)}, u32[]{:S(2)}) collective-permute-start(bf16[93,8,128]{2,1,0:T(8,128)(2,1)S(1)} %pad_maximum_fusion), channel_id=1, source_target_pairs={{0,1},{1,2},{2,3},{3,4},{4,5},{5,6},{6,7},{7,8},{8,9},{9,10},{10,1... | collective-permute-start | bytes 571400 | tf_op jit(solution)/shard_map/ppermute | solution.py:749
  23.2 0.0 copy-start.13
  23.2 0.0 copy-done.6
  23.2 0.6 copy-done.13
  23.9 0.0 copy-start.1
  23.9 0.0 collective-permute-done.3.right
  23.9 0.3 collective-permute-done.2.left
  24.3 11.0 %collective-permute-start.4 = (bf16[1136,128]{1,0:T(8,128)(2,1)S(1)}, bf16[1136,128]{1,0:T(8,128)(2,1)S(1)}, u32[]{:S(2)}, u32[]{:S(2)}) collective-permute-start(bf16[1136,128]{1,0:T(8,128)(2,1)S(1)} %fusion.1.mine), channel_id=1, source_target_pairs={{0,16},{1,17},{2,18},{3,19},{4,20},{5,21},{6,22},{7,23},{8,24},{9,... | collective-permute-start | bytes 872456 | tf_op jit(solution)/shard_map/ppermute | solution.py:800
  35.3 0.7 copy-done.11
  35.9 0.1 copy.16
  36.0 0.1 reshape.33
  36.2 0.0 copy-start.9
  36.2 0.5 copy-done.12
  36.7 0.1 pad_add_fusion.meta
  36.8 0.1 copy-done.9
  36.9 0.0 copy-done.1
  36.9 6.8 %shard_map.118 = (bf16[32,16,384]{2,1,0:T(8,128)(2,1)}, f32[1024,128]{1,0:T(8,128)S(1)}, bf16[68,48,128]{2,1,0:T(8,128)(2,1)}) custom-call(s32[194]{0:T(256)S(1)} %pad_add_fusion.meta, bf16[14,32,128]{2,1,0:T(8,128)(2,1)S(1)} %collective-permute-done.top, bf16[64,32,128]{2,1,0:T(8,128)(2,1)S(1)} %bitcast.46, ...), custom_call_target="tpu_custom_call" | custom-call | tf_op jit(solution)/shard_map/pallas_call | solution.py:620
  43.7 0.0 collective-permute-done.4.far
  43.7 0.0 copy-start.3
  43.7 4.1 %all-to-all-start = ((bf16[32,16,384]{2,1,0:T(8,128)(2,1)}), bf16[32,16,384]{2,1,0:T(8,128)(2,1)S(1)}, u32[]{:S(2)}, u32[]{:S(2)}) async-start(bf16[32,16,384]{2,1,0:T(8,128)(2,1)} %get-tuple-element.20), calls=%async_computation | async-start | bytes 786432 | tf_op jit(solution)/shard_map/all_to_all | solution.py:803
  47.9 0.4 collective-permute-start.5
  48.2 0.3 collective-permute-start.6
  48.5 0.0 copy-done.14
  48.5 0.0 copy-done.10
  48.5 0.0 copy-done.3
  48.6 8.0 %shard_map.119 = (bf16[3456,128]{1,0:T(8,128)(2,1)}, bf16[3648,128]{1,0:T(8,128)(2,1)}, f32[8,128]{1,0:T(8,128)S(1)}) custom-call(s32[194]{0:T(256)S(1)} %pad_add_fusion.meta, f32[1024,128]{1,0:T(8,128)S(1)} %get-tuple-element.22.dec, bf16[3,32,128]{2,1,0:T(8,128)(2,1)S(1)} %maximum_maximum_fusion.tall, bf16[93,8,128]{2,1,0:T(8,128)(2,1)S(1)} %collective-permute-done.2.left, ...), custom_call_target="tpu_custom_call" | custom-call | tf_op jit(solution)/shard_map/pallas_call | solution.py:620
  56.5 0.0 collective-permute-done.5.other
  56.5 0.0 collective-permute-done.6.far_other
  56.5 0.0 copy-start.4
  56.5 0.7 copy-done.4
  57.2 6.5 %all-to-all-done.strip = bf16[32,16,384]{2,1,0:T(8,128)(2,1)S(1)} async-done(((bf16[32,16,384]{2,1,0:T(8,128)(2,1)}), bf16[32,16,384]{2,1,0:T(8,128)(2,1)S(1)}, u32[]{:S(2)}, u32[]{:S(2)}) %all-to-all-start) | async-done | bytes 393248 | tf_op jit(solution)/shard_map/all_to_all | solution.py:803
  63.8 1.0 copy-done.5
  64.7 14.3 %shard_map.120 = bf16[32,40,128]{2,1,0:T(8,128)(2,1)} custom-call(s32[194]{0:T(256)S(1)} %pad_add_fusion.meta, bf16[32,16,384]{2,1,0:T(8,128)(2,1)S(1)} %all-to-all-done.strip, bf16[1136,128]{1,0:T(8,128)(2,1)S(1)} %fusion.1.mine, bf16[1136,128]{1,0:T(8,128)(2,1)S(1)} %collective-permute-done.5.other, bf16[1136,128]{1,0:T(8,128)(2,1)S(1)} %collective-permute-done.4.far, ...), custom_call_target="tpu_custom_call" | custom-call | tf_op jit(solution)/shard_map/pallas_call | solution.py:620
  79.1 7.2 %all-to-all-start.1 = ((bf16[32,40,128]{2,1,0:T(8,128)(2,1)}), bf16[32,40,128]{2,1,0:T(8,128)(2,1)S(1)}, u32[]{:S(2)}, u32[]{:S(2)}) async-start(bf16[32,40,128]{2,1,0:T(8,128)(2,1)} %shard_map.120), calls=%async_computation.1 | async-start | bytes 655360 | tf_op jit(solution)/shard_map/all_to_all | solution.py:810
  86.3 0.0 copy-start.2
  86.3 5.4 %shard_map.121.lpips = f32[640,128]{1,0:T(8,128)S(1)} custom-call(s32[194]{0:T(256)S(1)} %pad_add_fusion.meta, bf16[3456,128]{1,0:T(8,128)(2,1)} %get-tuple-element.24.feat, bf16[3648,128]{1,0:T(8,128)(2,1)} %get-tuple-element.25.slope_one, f32[3,32,128]{2,1,0:T(8,128)S(1)} %bitcast_convert_fusion.1.v_first, bf16[3,3,64,64]{3,2,1,0:T(8,128)(2,1)S(1)} %copy-done.3), custom_call_target="tpu_custom_call" | custom-call | tf_op jit(solution)/shard_map/pallas_call | solution.py:620
  91.7 8.9 %all-to-all-done.1.parts = bf16[32,40,128]{2,1,0:T(8,128)(2,1)S(1)} async-done(((bf16[32,40,128]{2,1,0:T(8,128)(2,1)}), bf16[32,40,128]{2,1,0:T(8,128)(2,1)S(1)}, u32[]{:S(2)}, u32[]{:S(2)}) %all-to-all-start.1) | async-done | bytes 327712 | tf_op jit(solution)/shard_map/all_to_all | solution.py:810
  100.6 0.0 copy-done.2
  100.6 4.2 %shard_map.122 = bf16[64,32,128]{2,1,0:T(8,128)(2,1)} custom-call(s32[194]{0:T(256)S(1)} %pad_add_fusion.meta, bf16[32,40,128]{2,1,0:T(8,128)(2,1)S(1)} %all-to-all-done.1.parts, f32[640,128]{1,0:T(8,128)S(1)} %shard_map.121.lpips, bf16[68,48,128]{2,1,0:T(8,128)(2,1)S(1)} %copy-done.2, bf16[64,32,128]{2,1,0:T(8,128)(2,1)S(1)} %bitcast.47, ...), custom_call_target="tpu_custom_call" | custom-call | tf_op jit(solution)/shard_map/pallas_call | solution.py:620
  (29 shorter events, 0.3 us)
Async XLA Ops:
  0.9 8.4 %copy-start = (bf16[1,64,32,128]{3,2,1,0:T(8,128)(2,1)S(1)}, bf16[1,64,32,128]{3,2,1,0:T(8,128)(2,1)}, u32[]{:S(2)}) copy-start(bf16[1,64,32,128]{3,2,1,0:T(8,128)(2,1)} %param.12) | copy-start | bytes 1572868
  2.1 8.1 %collective-permute-start = (bf16[14,32,128]{2,1,0:T(8,128)(2,1)S(1)}, bf16[14,32,128]{2,1,0:T(8,128)(2,1)S(1)}, u32[]{:S(2)}, u32[]{:S(2)}) collective-permute-start(bf16[14,32,128]{2,1,0:T(8,128)(2,1)S(1)} %pad_maximum_fusion.2), channel_id=1, source_target_pairs={{0,32},{32,64},{64,96},{96,128},{128,160},{160,192},{192,224},{1,3... | collective-permute-start | bytes 344072 | tf_op jit(solution)/shard_map/ppermute | solution.py:749
  7.4 10.3 %collective-permute-start.1 = (bf16[14,32,128]{2,1,0:T(8,128)(2,1)S(1)}, bf16[14,32,128]{2,1,0:T(8,128)(2,1)S(1)}, u32[]{:S(2)}, u32[]{:S(2)}) collective-permute-start(bf16[14,32,128]{2,1,0:T(8,128)(2,1)S(1)} %pad_maximum_fusion.3), channel_id=1, source_target_pairs={{32,0},{64,32},{96,64},{128,96},{160,128},{192,160},{224,192},{33,... | collective-permute-start | bytes 344072 | tf_op jit(solution)/shard_map/ppermute | solution.py:749
  9.3 0.7 copy-start.8
  17.8 0.7 copy-start.7
  18.7 4.5 %copy-start.6 = (bf16[1,4,4,64,128]{4,3,2,1,0:T(8,128)(2,1)S(1)}, bf16[1,4,4,64,128]{4,3,2,1,0:T(8,128)(2,1)}, u32[]{:S(2)}) copy-start(bf16[1,4,4,64,128]{4,3,2,1,0:T(8,128)(2,1)} %param.22) | copy-start | bytes 786436
  18.7 5.2 %collective-permute-start.3 = (bf16[93,8,128]{2,1,0:T(8,128)(2,1)S(1)}, bf16[93,8,128]{2,1,0:T(8,128)(2,1)S(1)}, u32[]{:S(2)}, u32[]{:S(2)}) collective-permute-start(bf16[93,8,128]{2,1,0:T(8,128)(2,1)S(1)} %pad_maximum_fusion.1), channel_id=1, source_target_pairs={{1,0},{2,1},{3,2},{4,3},{5,4},{6,5},{7,6},{8,7},{9,8},{10,9},{11,1... | collective-permute-start | bytes 571400 | tf_op jit(solution)/shard_map/ppermute | solution.py:749
  20.2 4.1 %collective-permute-start.2 = (bf16[93,8,128]{2,1,0:T(8,128)(2,1)S(1)}, bf16[93,8,128]{2,1,0:T(8,128)(2,1)S(1)}, u32[]{:S(2)}, u32[]{:S(2)}) collective-permute-start(bf16[93,8,128]{2,1,0:T(8,128)(2,1)S(1)} %pad_maximum_fusion), channel_id=1, source_target_pairs={{0,1},{1,2},{2,3},{3,4},{4,5},{5,6},{6,7},{7,8},{8,9},{9,10},{10,1... | collective-permute-start | bytes 571400 | tf_op jit(solution)/shard_map/ppermute | solution.py:749
  23.2 0.7 copy-start.13
  23.9 13.0 %copy-start.1 = (bf16[3,3,128,128]{3,2,1,0:T(8,128)(2,1)S(1)}, bf16[3,3,128,128]{3,2,1,0:T(8,128)(2,1)}, u32[]{:S(2)}) copy-start(bf16[3,3,128,128]{3,2,1,0:T(8,128)(2,1)} %w_mid.3) | copy-start | bytes 884740
  24.3 19.4 %collective-permute-start.4 = (bf16[1136,128]{1,0:T(8,128)(2,1)S(1)}, bf16[1136,128]{1,0:T(8,128)(2,1)S(1)}, u32[]{:S(2)}, u32[]{:S(2)}) collective-permute-start(bf16[1136,128]{1,0:T(8,128)(2,1)S(1)} %fusion.1.mine), channel_id=1, source_target_pairs={{0,16},{1,17},{2,18},{3,19},{4,20},{5,21},{6,22},{7,23},{8,24},{9,... | collective-permute-start | bytes 872456 | tf_op jit(solution)/shard_map/ppermute | solution.py:800
  35.3 0.7 copy-start.11
  36.0 0.7 copy-start.12
  36.2 0.7 copy-start.9
  43.7 4.8 %copy-start.14 = (f32[64]{0:T(128)S(1)}, f32[64]{0:T(128)}, u32[]{:S(2)}) copy-start(f32[64]{0:T(128)} %param.18) | copy-start | bytes 772
  43.7 4.8 %copy-start.10 = (bf16[3,3,3,64]{3,2,1,0:T(4,128)(2,1)S(1)}, bf16[3,3,3,64]{3,2,1,0:T(4,128)(2,1)}, u32[]{:S(2)}) copy-start(bf16[3,3,3,64]{3,2,1,0:T(4,128)(2,1)} %param.16) | copy-start | bytes 10372
  43.7 4.8 %copy-start.3 = (bf16[3,3,64,64]{3,2,1,0:T(8,128)(2,1)S(1)}, bf16[3,3,64,64]{3,2,1,0:T(8,128)(2,1)}, u32[]{:S(2)}) copy-start(bf16[3,3,64,64]{3,2,1,0:T(8,128)(2,1)} %v_second.3) | copy-start | bytes 221188
  43.7 20.0 %all-to-all-start = ((bf16[32,16,384]{2,1,0:T(8,128)(2,1)}), bf16[32,16,384]{2,1,0:T(8,128)(2,1)S(1)}, u32[]{:S(2)}, u32[]{:S(2)}) async-start(bf16[32,16,384]{2,1,0:T(8,128)(2,1)} %get-tuple-element.20), calls=%async_computation | async-start | bytes 786432 | tf_op jit(solution)/shard_map/all_to_all | solution.py:803
  47.9 8.7 %collective-permute-start.5 = (bf16[1136,128]{1,0:T(8,128)(2,1)S(1)}, bf16[1136,128]{1,0:T(8,128)(2,1)S(1)}, u32[]{:S(2)}, u32[]{:S(2)}) collective-permute-start(bf16[1136,128]{1,0:T(8,128)(2,1)S(1)} %fusion.1.mine), channel_id=1, source_target_pairs={{0,1},{1,0},{2,3},{3,2},{4,5},{5,4},{6,7},{7,6},{8,9},{9,8},{10,11... | collective-permute-start | bytes 872456 | tf_op jit(solution)/shard_map/ppermute | solution.py:804
  48.2 8.3 %collective-permute-start.6 = (bf16[1136,128]{1,0:T(8,128)(2,1)S(1)}, bf16[1136,128]{1,0:T(8,128)(2,1)S(1)}, u32[]{:S(2)}, u32[]{:S(2)}) collective-permute-start(bf16[1136,128]{1,0:T(8,128)(2,1)S(1)} %collective-permute-done.4.far), channel_id=1, source_target_pairs={{0,1},{1,0},{2,3},{3,2},{4,5},{5,4},{6,7},{7,6},{8,9},{9,8},{10,11... | collective-permute-start | bytes 872456 | tf_op jit(solution)/shard_map/ppermute | solution.py:805
  56.5 0.7 copy-start.4
  63.8 1.0 copy-start.5
  79.1 21.5 %all-to-all-start.1 = ((bf16[32,40,128]{2,1,0:T(8,128)(2,1)}), bf16[32,40,128]{2,1,0:T(8,128)(2,1)S(1)}, u32[]{:S(2)}, u32[]{:S(2)}) async-start(bf16[32,40,128]{2,1,0:T(8,128)(2,1)} %shard_map.120), calls=%async_computation.1 | async-start | bytes 655360 | tf_op jit(solution)/shard_map/all_to_all | solution.py:810
  86.3 14.3 %copy-start.2 = (bf16[68,48,128]{2,1,0:T(8,128)(2,1)S(1)}, bf16[68,48,128]{2,1,0:T(8,128)(2,1)}, u32[]{:S(2)}) copy-start(bf16[68,48,128]{2,1,0:T(8,128)(2,1)} %get-tuple-element.26.slope) | copy-start | bytes 2506756

commit v5 on v4

--- a/solution.py
+++ b/solution.py
@@ -82,6 +82,10 @@
     return ok & (row < limit)
 
 
+def wider(v):
+    return jnp.concatenate([v, jnp.zeros((v.shape[0], 128 - v.shape[1]), F32)], axis=1)
+
+
 def taller(v):
     return jnp.concatenate([v, jnp.zeros((128 - v.shape[0], 128), F32)], axis=0)
 
@@ -124,6 +128,46 @@
 def from_colours(px, tile, count, w):
     at = [pl.ds(aligned((tile + k) * WIDE, 16), count * WIDE) for k in range(2)]
     return mm(jnp.concatenate([px[at[0], :], px[at[1], :]], axis=1), w[...])
+
+
+def pack_rows_kernel(feats, target, low, high, own):
+    lane = iota((TW, 128), 1)
+    n = TGT_HALO
+    colours = [wider(target[k].astype(F32)) for k in range(3)]
+    for k in range(3):
+        own[k] = colours[k].astype(BF)
+    for out, y0, t0 in ((low, TH - FEAT_HALO, TH - n), (high, 0, 0)):
+        extra = jnp.zeros((TW, 128), F32)
+        for k in range(3):
+            amount = (n * k - t0) % 128
+            moved = pltpu.roll(colours[k], amount, 1) if amount else colours[k]
+            extra = jnp.where((lane >= n * k) & (lane < n * k + n), moved, extra)
+        out[0:FEAT_HALO] = feats[y0 : y0 + FEAT_HALO]
+        out[FEAT_HALO] = extra.astype(BF)
+
+
+def pack_sides_kernel(feats, own, top, bot, side_l, side_r, tall):
+    lane = iota((TW, 128), 1)
+    n = TGT_HALO
+    above, below = top[FEAT_HALO].astype(F32), bot[FEAT_HALO].astype(F32)
+    colours = []
+    for k in range(3):
+        first = pltpu.roll(above, 128 - n * k, 1) if k else above
+        last = pltpu.roll(below, n + TH - n * k, 1)
+        v = jnp.where(lane < n, first, pltpu.roll(own[k].astype(F32), n, 1))
+        v = jnp.where(lane < n + TH, v, jnp.where(lane < 2 * n + TH, last, 0.0))
+        tall[k] = v.astype(BF)
+        colours.append(v)
+    parts = (
+        (0, top[0:FEAT_HALO]),
+        (FEAT_HALO, feats[...]),
+        (FEAT_HALO + TH, bot[0:FEAT_HALO]),
+        (2 * FEAT_HALO + TH, jnp.stack(colours)),
+    )
+    for y, v in parts:
+        v = v.astype(F32)
+        for out, x0 in ((side_l, TW - COL_HALO), (side_r, 0)):
+            out[y : y + v.shape[0]] = v[:, x0 : x0 + COL_HALO, :].astype(BF)
 
 
 def decode_kernel(
@@ -763,40 +807,28 @@
     feats = features[0]
     planar = jnp.transpose(target[0], (2, 1, 0))
 
-    def row_part(rows, colours):
-        colours = jnp.transpose(colours, (1, 0, 2)).reshape(TW, 3 * TGT_HALO)
-        colours = jnp.pad(colours, ((0, 0), (0, 128 - 3 * TGT_HALO)))
-        return jnp.concatenate([rows, colours[None]], 0)
-
-    top, bot = exchange(
-        row_part(feats[TH - FEAT_HALO :], planar[:, :, TH - TGT_HALO :]),
-        row_part(feats[:FEAT_HALO], planar[:, :, :TGT_HALO]),
-        "row",
-    )
-
-    def colours_of(part):
-        part = part[FEAT_HALO, :, : 3 * TGT_HALO].reshape(TW, 3, TGT_HALO)
-        return jnp.transpose(part, (1, 0, 2))
-
-    tall = jnp.concatenate(
-        [
-            colours_of(top),
-            planar,
-            colours_of(bot),
-            jnp.zeros((3, TW, 128 - TH - 2 * TGT_HALO), BF),
-        ],
-        2,
-    )
-
-    def edge(first, last):
-        parts = (top[:FEAT_HALO], feats, bot[:FEAT_HALO], tall)
-        return jnp.concatenate([a[:, first:last] for a in parts], 0)
-
-    left, right = exchange(edge(TW - COL_HALO, TW), edge(0, COL_HALO), "col")
+    low, high, own = call(
+        pack_rows_kernel,
+        (shape((FEAT_HALO + 1, TW, 128), BF),) * 2 + (shape((3, TW, 128), BF),),
+        [],
+        (in_hbm(feats), in_hbm(planar)),
+        scalars=0,
+    )
+    top, bot = exchange(low, high, "row")
+    side_l, side_r, tall = call(
+        pack_sides_kernel,
+        (shape((2 * FEAT_HALO + TH + 3, COL_HALO, 128), BF),) * 2 + (shape((3, TW, 128), BF),),
+        [],
+        (feats, own, top, bot),
+        scalars=0,
+    )
+    left, right = exchange(side_l, side_r, "col")
     out_small = colour_first(jnp.transpose(conv_out, (0, 1, 3, 2)))
     vgg_small = colour_first(vgg_first)
     mine = critic_weights(critic_first[0], critic_second[0], critic_score[0])
-    left, right, sent = lax.optimization_barrier((left, right, mine))
+    left, right, sent, meta, out_small = lax.optimization_barrier(
+        (left, right, mine, meta, out_small)
+    )
     far = lax.ppermute(sent, "col", [(i, i ^ FAR) for i in range(COLS)])
     pay, dec, slope = decode(meta, top, feats, bot, left, right, conv_mid, out_small)
     pay, far = lax.optimization_barrier((pay, far))
@@ -806,7 +838,7 @@
     feat, slope_one, done = percept(
         meta, dec, tall, left, right, vgg_small, vgg_second, perceptual_weights
     )
-    grads = critics(meta, strip, (mine, other, far, far_other), done)
+    grads = critics(meta, strip, (mine, other, far, in_hbm(far_other)), done)
     parts = lax.all_to_all(grads, "col", split_axis=0, concat_axis=0, tiled=True)
     lpips = percept_back(meta, in_hbm(feat), in_hbm(slope_one), vgg_small, vgg_second)
     return finish(meta, parts, lpips, slope, feats, conv_mid, out_small)[None]

time: 106 us -> 101 us (0.953)
  local copies, waits for them, and re-layouts: 8.05 us -> 1.59 us
  waiting for transfers between devices: 23 us -> 27.5 us
  starting transfers between devices: 34.4 us -> 32.3 us
    ppermute x1, starting transfers between devices: 11 us -> 5.5 us  [local(): far = lax.ppermute(sent, 'col', [(i, i ^ FAR) for i in range(COLS)])]
    all_to_all x1, starting transfers between devices: 4.14 us -> 8.2 us  [local(): strip = lax.all_to_all(pay, 'col', split_axis=0, concat_axis=0, tiled=True)]
    unnamed x31 -> x25, local copies, waits for them, and re-layouts: 5.01 us -> 1.43 us
    ppermute x2, waiting for transfers between devices: 7.21 us -> 10.7 us  [exchange(): lax.ppermute(high, axis, backward)]
    ppermute x2, starting transfers between devices: 8.06 us -> 6.45 us  [exchange(): lax.ppermute(low, axis, forward)]
    slice x9 -> x0, local copies, waits for them, and re-layouts: 1.2 us -> none  [the longest x1 0.97 us: local(): feats[:FEAT_HALO]]
    all_to_all x1, starting transfers between devices: 7.22 us -> 8.32 us  [local(): lax.all_to_all(grads, 'col', split_axis=0, concat_axis=0, tiled=True)]
    transpose x3 -> x0, local copies, waits for them, and re-layouts: 1.08 us -> none  [row_part(): colours = jnp.transpose(colours, (1, 0, 2)).reshape(TW, 3 * TGT_HALO)]
  transfers between devices with their start and end apart: 9 -> 9, of which waited for: 4 -> 5; matrix products, arithmetic and copies ran while one was open for 1% -> 0% of each run, Pallas kernels for 19% -> 20%
where the time goes in v5:
time: 101 us
  Pallas kernels  38.8 us (38%)
  starting transfers between devices  32.3 us (32%)
  waiting for transfers between devices  27.5 us (27%)
  local copies, waits for them, and re-layouts  1.59 us (2%)
    pallas_call x7, Pallas kernels, call(): pl.pallas_call(kernel, in_specs=specs, out_specs=jax.tree.map(lambda _: p...  38.8 us
    ppermute x2, waiting for transfers between devices, exchange(): lax.ppermute(high, axis, backward)  10.7 us
    all_to_all x1, waiting for transfers between devices, local(): lax.all_to_all(grads, 'col', split_axis=0, concat_axis=0, tiled=True)  8.9 us
    all_to_all x1, starting transfers between devices, local(): lax.all_to_all(grads, 'col', split_axis=0, concat_axis=0, tiled=True)  8.32 us
    all_to_all x1, starting transfers between devices, local(): strip = lax.all_to_all(pay, 'col', split_axis=0, concat_axis=0, tiled=True)  8.2 us
    all_to_all x1, waiting for transfers between devices, local(): strip = lax.all_to_all(pay, 'col', split_axis=0, concat_axis=0, tiled=True)  7.22 us
    ppermute x2, starting transfers between devices, exchange(): lax.ppermute(low, axis, forward)  6.45 us
    ppermute x1, starting transfers between devices, local(): far = lax.ppermute(sent, 'col', [(i, i ^ FAR) for i in range(COLS)])  5.5 us
  transfers between devices with their start and end apart: 9, of which 5 were waited for; matrix products, arithmetic and copies ran while one was open for 0% of the time, Pallas kernels for 20%

profile of v5, /device:TPU:6, one launch (start us, length us, event | category | flops | bytes accessed | tf_op | source)
XLA Modules:
  0.0 100.6 jit_solution(7560626028974149000)
XLA Ops:
  0.0 0.0 copy-start
  0.0 0.0 copy-start.5
  0.0 1.2 %shard_map.118 = (bf16[14,32,128]{2,1,0:T(8,128)(2,1)S(1)}, bf16[14,32,128]{2,1,0:T(8,128)(2,1)S(1)}, bf16[3,32,128]{2,1,0:T(8,128)(2,1)S(1)}) custom-call(bf16[64,32,128]{2,1,0:T(8,128)(2,1)} %bitcast.23, bf16[3,32,64]{2,1,0:T(8,128)(2,1)} %bitcast.30), custom_call_target="tpu_custom_call" | custom-call | tf_op jit(solution)/shard_map/pallas_call | solution.py:664
  1.2 5.0 %collective-permute-start = (bf16[14,32,128]{2,1,0:T(8,128)(2,1)S(1)}, bf16[14,32,128]{2,1,0:T(8,128)(2,1)S(1)}, u32[]{:S(2)}, u32[]{:S(2)}) collective-permute-start(bf16[14,32,128]{2,1,0:T(8,128)(2,1)S(1)} %get-tuple-element.25), channel_id=1, source_target_pairs={{0,32},{32,64},{64,96},{96,128},{128,160},{160,192},{192,224},{1,3... | collective-permute-start | bytes 344072 | tf_op jit(solution)/shard_map/ppermute | solution.py:793
  6.2 1.9 %collective-permute-start.1 = (bf16[14,32,128]{2,1,0:T(8,128)(2,1)S(1)}, bf16[14,32,128]{2,1,0:T(8,128)(2,1)S(1)}, u32[]{:S(2)}, u32[]{:S(2)}) collective-permute-start(bf16[14,32,128]{2,1,0:T(8,128)(2,1)S(1)} %get-tuple-element.26), channel_id=1, source_target_pairs={{32,0},{64,32},{96,64},{128,96},{160,128},{192,160},{224,192},{33,... | collective-permute-start | bytes 344072 | tf_op jit(solution)/shard_map/ppermute | solution.py:793
  8.2 0.0 copy-done.5
  8.2 0.1 fusion.4
  8.3 0.0 copy-start.8
  8.3 0.7 copy-done.8
  9.0 0.1 copy.18
  9.1 0.0 copy-start.9
  9.1 0.1 reshape.28
  9.2 0.0 copy-start.6
  9.2 0.5 copy-done.9
  9.7 0.1 pad_add_fusion.meta
  9.8 0.1 copy-done.6
  9.9 0.0 collective-permute-done.top
  9.9 6.6 %collective-permute-done.1.bot = bf16[14,32,128]{2,1,0:T(8,128)(2,1)S(1)} collective-permute-done((bf16[14,32,128]{2,1,0:T(8,128)(2,1)S(1)}, bf16[14,32,128]{2,1,0:T(8,128)(2,1)S(1)}, u32[]{:S(2)}, u32[]{:S(2)}) %collective-permute-start.1) | collective-permute-done | bytes 114720 | tf_op jit(solution)/shard_map/ppermute | solution.py:793
  16.5 0.0 copy-done
  16.5 0.0 copy-start.4
  16.5 0.0 copy-start.10
  16.5 0.1 shard_map.119
  16.7 0.0 copy-start.1
  16.7 1.4 %collective-permute-start.2 = (bf16[93,8,128]{2,1,0:T(8,128)(2,1)S(1)}, bf16[93,8,128]{2,1,0:T(8,128)(2,1)S(1)}, u32[]{:S(2)}, u32[]{:S(2)}) collective-permute-start(bf16[93,8,128]{2,1,0:T(8,128)(2,1)S(1)} %get-tuple-element.27), channel_id=1, source_target_pairs={{0,1},{1,2},{2,3},{3,4},{4,5},{5,6},{6,7},{7,8},{8,9},{9,10},{10,1... | collective-permute-start | bytes 571400 | tf_op jit(solution)/shard_map/ppermute | solution.py:793
  18.1 1.3 %collective-permute-start.3 = (bf16[93,8,128]{2,1,0:T(8,128)(2,1)S(1)}, bf16[93,8,128]{2,1,0:T(8,128)(2,1)S(1)}, u32[]{:S(2)}, u32[]{:S(2)}) collective-permute-start(bf16[93,8,128]{2,1,0:T(8,128)(2,1)S(1)} %get-tuple-element.28), channel_id=1, source_target_pairs={{1,0},{2,1},{3,2},{4,3},{5,4},{6,5},{7,6},{8,7},{9,8},{10,9},{11,1... | collective-permute-start | bytes 571400 | tf_op jit(solution)/shard_map/ppermute | solution.py:793
  19.4 0.0 copy-done.4
  19.5 0.0 copy-done.10
  19.5 0.0 collective-permute-done.2.left
  19.5 4.1 %collective-permute-done.3.right = bf16[93,8,128]{2,1,0:T(8,128)(2,1)S(1)} collective-permute-done((bf16[93,8,128]{2,1,0:T(8,128)(2,1)S(1)}, bf16[93,8,128]{2,1,0:T(8,128)(2,1)S(1)}, u32[]{:S(2)}, u32[]{:S(2)}) %collective-permute-start.3) | collective-permute-done | bytes 190496 | tf_op jit(solution)/shard_map/ppermute | solution.py:793
  23.6 5.5 %collective-permute-start.4 = (bf16[1136,128]{1,0:T(8,128)(2,1)S(1)}, bf16[1136,128]{1,0:T(8,128)(2,1)S(1)}, u32[]{:S(2)}, u32[]{:S(2)}) collective-permute-start(bf16[1136,128]{1,0:T(8,128)(2,1)S(1)} %fusion.1.mine), channel_id=1, source_target_pairs={{0,16},{1,17},{2,18},{3,19},{4,20},{5,21},{6,22},{7,23},{8,24},{9,... | collective-permute-start | bytes 872456 | tf_op jit(solution)/shard_map/ppermute | solution.py:832
  29.1 0.0 copy-done.1
  29.1 6.8 %shard_map.120 = (bf16[32,16,384]{2,1,0:T(8,128)(2,1)}, f32[1024,128]{1,0:T(8,128)S(1)}, bf16[68,48,128]{2,1,0:T(8,128)(2,1)}) custom-call(s32[194]{0:T(256)S(1)} %pad_add_fusion.meta, bf16[14,32,128]{2,1,0:T(8,128)(2,1)S(1)} %collective-permute-done.top, bf16[64,32,128]{2,1,0:T(8,128)(2,1)S(1)} %bitcast.25, ...), custom_call_target="tpu_custom_call" | custom-call | tf_op jit(solution)/shard_map/pallas_call | solution.py:664
  35.9 0.6 collective-permute-done.4.far
  36.5 0.0 copy-start.11
  36.5 0.0 copy-start.7
  36.5 0.0 copy-start.3
  36.5 8.2 %all-to-all-start = ((bf16[32,16,384]{2,1,0:T(8,128)(2,1)}), bf16[32,16,384]{2,1,0:T(8,128)(2,1)S(1)}, u32[]{:S(2)}, u32[]{:S(2)}) async-start(bf16[32,16,384]{2,1,0:T(8,128)(2,1)} %get-tuple-element.35), calls=%async_computation | async-start | bytes 786432 | tf_op jit(solution)/shard_map/all_to_all | solution.py:835
  44.8 0.4 collective-permute-start.5
  45.1 0.3 collective-permute-start.6
  45.4 0.0 copy-done.11
  45.4 0.0 copy-done.7
  45.4 0.0 copy-done.3
  45.4 8.0 %shard_map.121 = (bf16[3456,128]{1,0:T(8,128)(2,1)}, bf16[3648,128]{1,0:T(8,128)(2,1)}, f32[8,128]{1,0:T(8,128)S(1)}) custom-call(s32[194]{0:T(256)S(1)} %pad_add_fusion.meta, f32[1024,128]{1,0:T(8,128)S(1)} %get-tuple-element.37.dec, bf16[3,32,128]{2,1,0:T(8,128)(2,1)S(1)} %get-tuple-element.38.tall, bf16[93,8,128]{2,1,0:T(8,128)(2,1)S(1)} %collective-permute-done.2.left, ...), custom_call_target="tpu_custom_call" | custom-call | tf_op jit(solution)/shard_map/pallas_call | solution.py:664
  53.4 0.0 collective-permute-done.5.other
  53.4 0.0 collective-permute-done.6.far_other
  53.4 7.2 %all-to-all-done.strip = bf16[32,16,384]{2,1,0:T(8,128)(2,1)S(1)} async-done(((bf16[32,16,384]{2,1,0:T(8,128)(2,1)}), bf16[32,16,384]{2,1,0:T(8,128)(2,1)S(1)}, u32[]{:S(2)}, u32[]{:S(2)}) %all-to-all-start) | async-done | bytes 393248 | tf_op jit(solution)/shard_map/all_to_all | solution.py:835
  60.6 13.1 %shard_map.122 = bf16[32,40,128]{2,1,0:T(8,128)(2,1)} custom-call(s32[194]{0:T(256)S(1)} %pad_add_fusion.meta, bf16[32,16,384]{2,1,0:T(8,128)(2,1)S(1)} %all-to-all-done.strip, bf16[1136,128]{1,0:T(8,128)(2,1)S(1)} %fusion.1.mine, bf16[1136,128]{1,0:T(8,128)(2,1)S(1)} %collective-permute-done.5.other, bf16[1136,128]{1,0:T(8,128)(2,1)S(1)} %collective-permute-done.4.far, ...), custom_call_target="tpu_custom_call" | custom-call | tf_op jit(solution)/shard_map/pallas_call | solution.py:664
  73.8 8.3 %all-to-all-start.1 = ((bf16[32,40,128]{2,1,0:T(8,128)(2,1)}), bf16[32,40,128]{2,1,0:T(8,128)(2,1)S(1)}, u32[]{:S(2)}, u32[]{:S(2)}) async-start(bf16[32,40,128]{2,1,0:T(8,128)(2,1)} %shard_map.122), calls=%async_computation.1 | async-start | bytes 655360 | tf_op jit(solution)/shard_map/all_to_all | solution.py:842
  82.1 0.0 copy-start.2
  82.1 5.4 %shard_map.123.lpips = f32[640,128]{1,0:T(8,128)S(1)} custom-call(s32[194]{0:T(256)S(1)} %pad_add_fusion.meta, bf16[3456,128]{1,0:T(8,128)(2,1)} %get-tuple-element.40.feat, bf16[3648,128]{1,0:T(8,128)(2,1)} %get-tuple-element.41.slope_one, f32[3,32,128]{2,1,0:T(8,128)S(1)} %bitcast_convert_fusion.1.v_first, bf16[3,3,64,64]{3,2,1,0:T(8,128)(2,1)S(1)} %copy-done.3), custom_call_target="tpu_custom_call" | custom-call | tf_op jit(solution)/shard_map/pallas_call | solution.py:664
  87.5 8.9 %all-to-all-done.1.parts = bf16[32,40,128]{2,1,0:T(8,128)(2,1)S(1)} async-done(((bf16[32,40,128]{2,1,0:T(8,128)(2,1)}), bf16[32,40,128]{2,1,0:T(8,128)(2,1)S(1)}, u32[]{:S(2)}, u32[]{:S(2)}) %all-to-all-start.1) | async-done | bytes 327712 | tf_op jit(solution)/shard_map/all_to_all | solution.py:842
  96.4 0.0 copy-done.2
  96.4 4.2 %shard_map.124 = bf16[64,32,128]{2,1,0:T(8,128)(2,1)} custom-call(s32[194]{0:T(256)S(1)} %pad_add_fusion.meta, bf16[32,40,128]{2,1,0:T(8,128)(2,1)S(1)} %all-to-all-done.1.parts, f32[640,128]{1,0:T(8,128)S(1)} %shard_map.123.lpips, bf16[68,48,128]{2,1,0:T(8,128)(2,1)S(1)} %copy-done.2, bf16[64,32,128]{2,1,0:T(8,128)(2,1)S(1)} %bitcast.26, ...), custom_call_target="tpu_custom_call" | custom-call | tf_op jit(solution)/shard_map/pallas_call | solution.py:664
  (7 shorter events, 0.1 us)
Async XLA Ops:
  0.0 16.5 %copy-start = (bf16[1,64,32,128]{3,2,1,0:T(8,128)(2,1)S(1)}, bf16[1,64,32,128]{3,2,1,0:T(8,128)(2,1)}, u32[]{:S(2)}) copy-start(bf16[1,64,32,128]{3,2,1,0:T(8,128)(2,1)} %param.12) | copy-start | bytes 1572868
  0.0 8.2 %copy-start.5 = (bf16[1,4,4,3,64]{4,2,3,1,0:T(4,128)(2,1)S(1)}, bf16[1,4,4,3,64]{4,2,3,1,0:T(4,128)(2,1)}, u32[]{:S(2)}) copy-start(bf16[1,4,4,3,64]{4,2,3,1,0:T(4,128)(2,1)} %param.21) | copy-start | bytes 18436
  1.2 8.7 %collective-permute-start = (bf16[14,32,128]{2,1,0:T(8,128)(2,1)S(1)}, bf16[14,32,128]{2,1,0:T(8,128)(2,1)S(1)}, u32[]{:S(2)}, u32[]{:S(2)}) collective-permute-start(bf16[14,32,128]{2,1,0:T(8,128)(2,1)S(1)} %get-tuple-element.25), channel_id=1, source_target_pairs={{0,32},{32,64},{64,96},{96,128},{128,160},{160,192},{192,224},{1,3... | collective-permute-start | bytes 344072 | tf_op jit(solution)/shard_map/ppermute | solution.py:793
  6.2 10.3 %collective-permute-start.1 = (bf16[14,32,128]{2,1,0:T(8,128)(2,1)S(1)}, bf16[14,32,128]{2,1,0:T(8,128)(2,1)S(1)}, u32[]{:S(2)}, u32[]{:S(2)}) collective-permute-start(bf16[14,32,128]{2,1,0:T(8,128)(2,1)S(1)} %get-tuple-element.26), channel_id=1, source_target_pairs={{32,0},{64,32},{96,64},{128,96},{160,128},{192,160},{224,192},{33,... | collective-permute-start | bytes 344072 | tf_op jit(solution)/shard_map/ppermute | solution.py:793
  8.3 0.7 copy-start.8
  9.1 0.7 copy-start.9
  9.2 0.7 copy-start.6
  16.5 2.9 %copy-start.4 = (bf16[1,4,4,64,128]{4,3,2,1,0:T(8,128)(2,1)S(1)}, bf16[1,4,4,64,128]{4,3,2,1,0:T(8,128)(2,1)}, u32[]{:S(2)}) copy-start(bf16[1,4,4,64,128]{4,3,2,1,0:T(8,128)(2,1)} %param.22) | copy-start | bytes 786436
  16.5 2.9 %copy-start.10 = (bf16[1,128]{1,0:T(2,128)(2,1)S(1)}, bf16[1,128]{1,0:T(2,128)(2,1)}, u32[]{:S(2)}) copy-start(bf16[1,128]{1,0:T(2,128)(2,1)} %param.23) | copy-start | bytes 772
  16.7 12.4 %copy-start.1 = (bf16[3,3,128,128]{3,2,1,0:T(8,128)(2,1)S(1)}, bf16[3,3,128,128]{3,2,1,0:T(8,128)(2,1)}, u32[]{:S(2)}) copy-start(bf16[3,3,128,128]{3,2,1,0:T(8,128)(2,1)} %w_mid.3) | copy-start | bytes 884740
  16.7 2.8 %collective-permute-start.2 = (bf16[93,8,128]{2,1,0:T(8,128)(2,1)S(1)}, bf16[93,8,128]{2,1,0:T(8,128)(2,1)S(1)}, u32[]{:S(2)}, u32[]{:S(2)}) collective-permute-start(bf16[93,8,128]{2,1,0:T(8,128)(2,1)S(1)} %get-tuple-element.27), channel_id=1, source_target_pairs={{0,1},{1,2},{2,3},{3,4},{4,5},{5,6},{6,7},{7,8},{8,9},{9,10},{10,1... | collective-permute-start | bytes 571400 | tf_op jit(solution)/shard_map/ppermute | solution.py:793
  18.1 5.5 %collective-permute-start.3 = (bf16[93,8,128]{2,1,0:T(8,128)(2,1)S(1)}, bf16[93,8,128]{2,1,0:T(8,128)(2,1)S(1)}, u32[]{:S(2)}, u32[]{:S(2)}) collective-permute-start(bf16[93,8,128]{2,1,0:T(8,128)(2,1)S(1)} %get-tuple-element.28), channel_id=1, source_target_pairs={{1,0},{2,1},{3,2},{4,3},{5,4},{6,5},{7,6},{8,7},{9,8},{10,9},{11,1... | collective-permute-start | bytes 571400 | tf_op jit(solution)/shard_map/ppermute | solution.py:793
  23.6 12.9 %collective-permute-start.4 = (bf16[1136,128]{1,0:T(8,128)(2,1)S(1)}, bf16[1136,128]{1,0:T(8,128)(2,1)S(1)}, u32[]{:S(2)}, u32[]{:S(2)}) collective-permute-start(bf16[1136,128]{1,0:T(8,128)(2,1)S(1)} %fusion.1.mine), channel_id=1, source_target_pairs={{0,16},{1,17},{2,18},{3,19},{4,20},{5,21},{6,22},{7,23},{8,24},{9,... | collective-permute-start | bytes 872456 | tf_op jit(solution)/shard_map/ppermute | solution.py:832
  36.5 8.9 %copy-start.11 = (f32[64]{0:T(128)S(1)}, f32[64]{0:T(128)}, u32[]{:S(2)}) copy-start(f32[64]{0:T(128)} %param.18) | copy-start | bytes 772
  36.5 8.9 %copy-start.7 = (bf16[3,3,3,64]{3,2,1,0:T(4,128)(2,1)S(1)}, bf16[3,3,3,64]{3,2,1,0:T(4,128)(2,1)}, u32[]{:S(2)}) copy-start(bf16[3,3,3,64]{3,2,1,0:T(4,128)(2,1)} %param.16) | copy-start | bytes 10372
  36.5 8.9 %copy-start.3 = (bf16[3,3,64,64]{3,2,1,0:T(8,128)(2,1)S(1)}, bf16[3,3,64,64]{3,2,1,0:T(8,128)(2,1)}, u32[]{:S(2)}) copy-start(bf16[3,3,64,64]{3,2,1,0:T(8,128)(2,1)} %v_second.3) | copy-start | bytes 221188
  36.5 24.1 %all-to-all-start = ((bf16[32,16,384]{2,1,0:T(8,128)(2,1)}), bf16[32,16,384]{2,1,0:T(8,128)(2,1)S(1)}, u32[]{:S(2)}, u32[]{:S(2)}) async-start(bf16[32,16,384]{2,1,0:T(8,128)(2,1)} %get-tuple-element.35), calls=%async_computation | async-start | bytes 786432 | tf_op jit(solution)/shard_map/all_to_all | solution.py:835
  44.8 8.7 %collective-permute-start.5 = (bf16[1136,128]{1,0:T(8,128)(2,1)S(1)}, bf16[1136,128]{1,0:T(8,128)(2,1)S(1)}, u32[]{:S(2)}, u32[]{:S(2)}) collective-permute-start(bf16[1136,128]{1,0:T(8,128)(2,1)S(1)} %fusion.1.mine), channel_id=1, source_target_pairs={{0,1},{1,0},{2,3},{3,2},{4,5},{5,4},{6,7},{7,6},{8,9},{9,8},{10,11... | collective-permute-start | bytes 872456 | tf_op jit(solution)/shard_map/ppermute | solution.py:836
  45.1 8.3 %collective-permute-start.6 = (bf16[1136,128]{1,0:T(8,128)(2,1)S(1)}, bf16[1136,128]{1,0:T(8,128)(2,1)}, u32[]{:S(2)}, u32[]{:S(2)}) collective-permute-start(bf16[1136,128]{1,0:T(8,128)(2,1)S(1)} %collective-permute-done.4.far), channel_id=1, source_target_pairs={{0,1},{1,0},{2,3},{3,2},{4,5},{5,4},{6,7},{7,6},{8,9},{9,8},{10,11... | collective-permute-start | bytes 872456 | tf_op jit(solution)/shard_map/ppermute | solution.py:837
  73.8 22.6 %all-to-all-start.1 = ((bf16[32,40,128]{2,1,0:T(8,128)(2,1)}), bf16[32,40,128]{2,1,0:T(8,128)(2,1)S(1)}, u32[]{:S(2)}, u32[]{:S(2)}) async-start(bf16[32,40,128]{2,1,0:T(8,128)(2,1)} %shard_map.122), calls=%async_computation.1 | async-start | bytes 655360 | tf_op jit(solution)/shard_map/all_to_all | solution.py:842
  82.1 14.3 %copy-start.2 = (bf16[68,48,128]{2,1,0:T(8,128)(2,1)S(1)}, bf16[68,48,128]{2,1,0:T(8,128)(2,1)}, u32[]{:S(2)}) copy-start(bf16[68,48,128]{2,1,0:T(8,128)(2,1)} %get-tuple-element.42.slope) | copy-start | bytes 2506756

commit v6 on v5

--- a/solution.py
+++ b/solution.py
@@ -23,6 +23,7 @@
 TGT_HALO = 6
 GRAD_PAD = 8
 SHARE = 34
+SPAN = 52
 VMEM = 20 * 1024 * 1024
 
 
@@ -223,17 +224,22 @@
     planes = [
         dec[pl.ds(k, 128, stride=8), :].T[COL_HALO : COL_HALO + TW, :] for k in range(3)
     ]
-    upper = iota((16, 128), 1) >= 64
+    lane = iota((8, 128), 1)
     for half in range(2):
-        low, high = [], []
-        for x in range(2):
-            for p in planes:
-                p = p[x * 16 : (x + 1) * 16]
-                start = half * SHARE
-                low.append(pltpu.roll(p, 128 - start, 1) if start else p)
-                high.append(pltpu.roll(p, 64 - start, 1))
-        packed = [jnp.where(upper, high[k + 1], low[k]) for k in (0, 2, 4)]
-        packed = jnp.concatenate(packed, axis=1).astype(BF)
+        tiles = [jnp.zeros((8, 128), F32) for _ in range(5)]
+        for g in range(4):
+            for k in range(3):
+                piece = planes[k][g * 8 : (g + 1) * 8]
+                if half:
+                    piece = pltpu.roll(piece, 128 - SHARE, 1)
+                piece = jnp.where(lane < SPAN, piece, 0.0)
+                at, off = divmod((g * 3 + k) * SPAN, 128)
+                if off:
+                    piece = pltpu.roll(piece, off, 1)
+                tiles[at] = tiles[at] + jnp.where(lane >= off, piece, 0.0)
+                if off + SPAN > 128:
+                    tiles[at + 1] = tiles[at + 1] + jnp.where(lane < off, piece, 0.0)
+        packed = jnp.concatenate(tiles, axis=1).astype(BF)
         for k in range(COLS // 2):
             pay[2 * k + half] = packed
 
@@ -313,7 +319,10 @@
     lax.fori_loop(0, 9, second, 0, unroll=3)
 
 
-def percept_back_kernel(meta, feat, slope_one, v_first, v_second, out, bv, w3, w4):
+def percept_back_kernel(
+    meta, feat, slope_one, v_first, v_second, feats, w_mid, w_out, out, feats_slope, w, w1,
+    bv, w3, w4,
+):
     r, c = meta[0], meta[1]
     col_ok = column_mask(c * TW - COL_HALO)
 
@@ -322,6 +331,21 @@
         return jnp.concatenate(parts + [jnp.zeros((8, 128), F32)], axis=0)
 
     colour_weights(w4, last_small)
+    for dy in range(3):
+        for dx in range(3):
+            w[dx * 128 : (dx + 1) * 128, dy * 128 : (dy + 1) * 128] = w_mid[2 - dy, 2 - dx]
+
+    def small(dy):
+        flipped = [w_out[2 - dy, (2 - dx) * 8 : (3 - dx) * 8, :] for dx in range(3)]
+        return jnp.concatenate(flipped + [jnp.zeros((8, 128), F32)], axis=0)
+
+    patch_weights(w1, small)
+    def feature_slope(i, carry):
+        at = pl.ds(i * 8, 8)
+        feats_slope[at] = silu_parts(feats[at].astype(F32))[1].astype(BF)
+        return carry
+
+    lax.fori_loop(0, TH // 8, feature_slope, 0, unroll=2)
     for dy in range(3):
         for dx in range(3):
             v = v_second[dy, dx].astype(F32)
@@ -359,9 +383,10 @@
 
 def critic_kernel(
     meta, strip, mine, other, far, far_other, _, out,
-    strip32, grads, w_pre, w_one, w_two, w_back, score, distance, row_gap, row_gap_back, x_all, x_all_b, pre, pre_b, act, act_b,
-    two, two_b, cols, cols_b, jobs,
+    strip32, grads, w_pre, w_one, w_two, w_back, score, distance, row_gap, row_gap_back, *rest,
 ):
+    x_all, pre, act, two, cols = (rest[k * 4 : (k + 1) * 4] for k in range(5))
+    jobs = rest[20]
     r, me = meta[0], meta[1]
     first_row = r * TH - 2 + SHARE * (me & 1)
     lane = iota((1, 128), 1)
@@ -371,10 +396,22 @@
 
     def unpack(k, carry):
         v = strip[k].astype(F32)
-        b, d = pltpu.roll(v[:, 128:256], 64, 1), pltpu.roll(v[:, 256:384], 64, 1)
-        at = aligned(k * TW, 32)
-        strip32[pl.ds(at, 16), :] = v[:, 0:256]
-        strip32[pl.ds(at + 16, 16), :] = jnp.concatenate([jnp.where(upper, d, b), d], axis=1)
+
+        def piece(g, j, place):
+            at, off = divmod((g * 3 + j) * SPAN, 128)
+            amount = (place - off) % 128
+            parts = [v[:, at * 128 : (at + 1) * 128]]
+            if off + SPAN > 128:
+                parts.append(v[:, (at + 1) * 128 : (at + 2) * 128])
+            parts = [pltpu.roll(p, amount, 1) if amount else p for p in parts]
+            if len(parts) == 1:
+                return parts[0]
+            return jnp.where(lane < place + 128 - off, parts[0], parts[1])
+
+        for g in range(4):
+            both = jnp.where(upper, piece(g, 1, 64), piece(g, 0, 0))
+            row = jnp.concatenate([both, piece(g, 2, 0)], axis=1)
+            strip32[pl.ds(aligned(k * TW + g * 8, 8), 8), :] = row
         return carry
 
     lax.fori_loop(0, COLS, unpack, 0, unroll=8)
@@ -404,10 +441,10 @@
                             (par * 2 + 1 - p) * 64 : (par * 2 + 2 - p) * 64,
                             (t * 3 + kind) * 128 : (t * 3 + kind + 1) * 128,
                         ] = 0.5 * source[i * 256 + j * 64 : i * 256 + (j + 1) * 64, :]
-    for t in (two, two_b):
+    for t in two:
         t[:, 0:128] = jnp.zeros((384, 128), BF)
         t[:, (STEPS + 1) * 128 :] = jnp.zeros((384, 128), BF)
-    for t in (cols, cols_b):
+    for t in cols:
         t[192:, :] = jnp.zeros((64, 384), F32)
     x, n = iota((CROP + 8, 384), 0), iota((CROP + 8, 384), 1)
     wanted = 4 * (n & 63) + (n >> 6) - 1
@@ -569,20 +606,26 @@
         count = count + shared * ((seen & 1) == turn).astype(jnp.int32)
         seen = seen + shared
 
-    first_set, second_set = (x_all, pre, act, two, cols), (x_all_b, pre_b, act_b, two_b, cols_b)
-
-    def two_crops(k, carry):
-        running = [job(jobs[2 * k], *first_set), job(jobs[2 * k + 1], *second_set)]
+    sets = tuple(zip(x_all, pre, act, two, cols))
+
+    def crops(first, number):
+        running = [job(jobs[first + k], *sets[k]) for k in range(number)]
         while running:
             running = [g for g in running if next(g, STOP) is not STOP]
-        return carry
-
-    lax.fori_loop(0, count >> 1, two_crops, 0)
+
+    def four_crops(k, carry):
+        crops(4 * k, 4)
+        return carry
+
+    lax.fori_loop(0, count >> 2, four_crops, 0)
+
+    @pl.when((count & 2) == 2)
+    def _():
+        crops((count >> 2) * 4, 2)
 
     @pl.when((count & 1) == 1)
     def _():
-        for _ in job(jobs[count - 1], *first_set):
-            pass
+        crops(count - 1, 1)
 
     def pack(k, carry):
         block = grads[pl.ds(aligned(k * TW, 32), 48), :][GRAD_PAD - 2 : GRAD_PAD + 38]
@@ -598,18 +641,9 @@
 
 
 def finish_kernel(
-    meta, parts, lpips, slope, feats, w_mid, w_out, out, turned, planes, px, bm, w, w1
+    meta, parts, lpips, slope, feats_slope, w, w1, out, turned, planes, px, bm
 ):
     r, c = meta[0], meta[1]
-    for dy in range(3):
-        for dx in range(3):
-            w[dx * 128 : (dx + 1) * 128, dy * 128 : (dy + 1) * 128] = w_mid[2 - dy, 2 - dx]
-
-    def small(dy):
-        flipped = [w_out[2 - dy, (2 - dx) * 8 : (3 - dx) * 8, :] for dx in range(3)]
-        return jnp.concatenate(flipped + [jnp.zeros((8, 128), F32)], axis=0)
-
-    patch_weights(w1, small)
     col_ok = column_mask(c * TW - 2)
     planes[...] = jnp.zeros(planes.shape, F32)
     for half in range(2):
@@ -650,14 +684,14 @@
     def last(i, carry):
         v = conv_rows(bm, i * 8, 8, w[...], transposed=True, shift=2)
         v = v.reshape(8, WIDE, 128)[:, 0:TW, :]
-        x = feats[pl.ds(i * 8, 8)].astype(F32)
-        out[pl.ds(i * 8, 8)] = (v * silu_parts(x)[1]).astype(BF)
-        return carry
-
-    lax.fori_loop(0, TH // 8, last, 0, unroll=4)
-
-
-def call(kernel, outs, scratch, args, scalars=1, unused=0, lists=()):
+        at = pl.ds(i * 8, 8)
+        out[at] = (v * feats_slope[at].astype(F32)).astype(BF)
+        return carry
+
+    lax.fori_loop(0, TH // 8, last, 0, unroll=True)
+
+
+def call(kernel, outs, scratch, args, scalars=1, unused=0, lists=(), vmem=VMEM):
     specs = [pl.BlockSpec(memory_space=pltpu.SMEM)] * scalars
     specs += [pl.BlockSpec(memory_space=pltpu.VMEM)] * (len(args) - scalars - unused)
     specs += [pl.BlockSpec(memory_space=pl.ANY)] * unused
@@ -667,7 +701,7 @@
         out_specs=jax.tree.map(lambda _: pl.BlockSpec(memory_space=pltpu.VMEM), outs),
         out_shape=outs,
         scratch_shapes=[pltpu.VMEM(s, t) for s, t in scratch] + list(lists),
-        compiler_params=pltpu.CompilerParams(vmem_limit_bytes=VMEM),
+        compiler_params=pltpu.CompilerParams(vmem_limit_bytes=vmem),
         interpret=INTERPRET,
     )(*args)
 
@@ -688,7 +722,7 @@
     return call(
         decode_kernel,
         (
-            shape((COLS, TW // 2, 384), BF),
+            shape((COLS, TW // 4, 640), BF),
             shape((1024, 128), F32),
             pltpu.HBM((68, WIDE, 128), BF),
         ),
@@ -717,12 +751,17 @@
     )
 
 
-def percept_back(meta, feat, slope_one, small, vgg_second):
+def percept_back(meta, feat, slope_one, small, vgg_second, feats, conv_mid, out_small):
     return call(
         percept_back_kernel,
-        shape((80 * 8, 128), F32),
+        (
+            shape((80 * 8, 128), F32),
+            shape((TH, TW, 128), BF),
+            shape((384, 384), BF),
+            shape((256, 512), BF),
+        ),
         [((82 * WIDE, 128), BF), ((384, 384), BF), ((384, 384), BF)],
-        (meta, feat, slope_one, small, vgg_second),
+        (meta, feat, slope_one, small, vgg_second, feats, conv_mid, out_small),
     )
 
 
@@ -759,14 +798,15 @@
             ((TILES * 16, 128), F32),
             ((128, TILES * 16), F32),
         ]
-        + [buffer for buffer in pair for _ in range(2)],
+        + [buffer for buffer in pair for _ in range(4)],
         (meta, strip, *weights, after),
         unused=1,
         lists=[pltpu.SMEM((CROPS,), jnp.int32)],
-    )
-
-
-def finish(meta, parts, lpips, slope, feats, conv_mid, small):
+        vmem=30 * 1024 * 1024,
+    )
+
+
+def finish(meta, parts, lpips, slope, feats_slope, w, w1):
     return call(
         finish_kernel,
         shape((TH, TW, 128), BF),
@@ -775,10 +815,8 @@
             ((80 * 8, 128), F32),
             ((18 * WIDE, 128), BF),
             ((68 * WIDE, 128), BF),
-            ((384, 384), BF),
-            ((256, 512), BF),
         ],
-        (meta, parts, lpips, slope, feats, conv_mid, small),
+        (meta, parts, lpips, slope, feats_slope, w, w1),
     )
 
 
@@ -840,8 +878,10 @@
     )
     grads = critics(meta, strip, (mine, other, far, in_hbm(far_other)), done)
     parts = lax.all_to_all(grads, "col", split_axis=0, concat_axis=0, tiled=True)
-    lpips = percept_back(meta, in_hbm(feat), in_hbm(slope_one), vgg_small, vgg_second)
-    return finish(meta, parts, lpips, slope, feats, conv_mid, out_small)[None]
+    lpips, *made = percept_back(
+        meta, in_hbm(feat), in_hbm(slope_one), vgg_small, vgg_second, feats, conv_mid, out_small
+    )
+    return finish(meta, parts, lpips, slope, *made)[None]
 
 
 def solution(mesh):

time: 101 us -> 99.8 us (0.988)
  waiting for transfers between devices: 27.5 us -> 24.8 us
  starting transfers between devices: 32.3 us -> 30 us
  local copies, waits for them, and re-layouts: 1.59 us -> 3.24 us
  Pallas kernels: 38.8 us -> 40.2 us
    all_to_all x1, starting transfers between devices: 8.32 us -> 6.02 us  [local(): lax.all_to_all(grads, 'col', split_axis=0, concat_axis=0, tiled=True)]
    unnamed x25 -> x29, local copies, waits for them, and re-layouts: 1.43 us -> 3.08 us
    pallas_call x7, Pallas kernels: 38.8 us -> 40.2 us  [call(): pl.pallas_call(kernel, in_specs=specs, out_specs=jax.tree.map(lambda _: p...]
    all_to_all x1, waiting for transfers between devices: 8.9 us -> 7.56 us  [local(): lax.all_to_all(grads, 'col', split_axis=0, concat_axis=0, tiled=True)]
    all_to_all x1, waiting for transfers between devices: 7.22 us -> 5.9 us  [local(): strip = lax.all_to_all(pay, 'col', split_axis=0, concat_axis=0, tiled=True)]
  transfers between devices with their start and end apart: 9 -> 9, of which waited for: 5 -> 5; matrix products, arithmetic and copies ran while one was open for 0% -> 0% of each run, Pallas kernels for 20% -> 21%
where the time goes in v6:
time: 99.8 us; the launch traced here: 98.7 us
  Pallas kernels  40.2 us (40%)
  starting transfers between devices  30 us (30%)
  waiting for transfers between devices  24.8 us (25%)
  local copies, waits for them, and re-layouts  3.24 us (3%)
    pallas_call x7, Pallas kernels, call(): pl.pallas_call(kernel, in_specs=specs, out_specs=jax.tree.map(lambda _: p...  40.2 us
    ppermute x2, waiting for transfers between devices, exchange(): lax.ppermute(high, axis, backward)  10.7 us
    all_to_all x1, starting transfers between devices, local(): strip = lax.all_to_all(pay, 'col', split_axis=0, concat_axis=0, tiled=True)  8.2 us
    all_to_all x1, waiting for transfers between devices, local(): lax.all_to_all(grads, 'col', split_axis=0, concat_axis=0, tiled=True)  7.56 us
    ppermute x2, starting transfers between devices, exchange(): lax.ppermute(low, axis, forward)  6.45 us
    all_to_all x1, starting transfers between devices, local(): lax.all_to_all(grads, 'col', split_axis=0, concat_axis=0, tiled=True)  6.02 us
    all_to_all x1, waiting for transfers between devices, local(): strip = lax.all_to_all(pay, 'col', split_axis=0, concat_axis=0, tiled=True)  5.9 us
    ppermute x1, starting transfers between devices, local(): far = lax.ppermute(sent, 'col', [(i, i ^ FAR) for i in range(COLS)])  5.5 us
  transfers between devices with their start and end apart: 9, of which 5 were waited for; matrix products, arithmetic and copies ran while one was open for 0% of the time, Pallas kernels for 21%

profile of v6, /device:TPU:6, one launch (start us, length us, event | category | flops | bytes accessed | tf_op | source)
XLA Modules:
  0.0 98.7 jit_solution(17388665872888392844)
XLA Ops:
  0.0 0.0 copy-start
  0.0 0.0 copy-start.7
  0.0 1.2 %shard_map.118 = (bf16[14,32,128]{2,1,0:T(8,128)(2,1)S(1)}, bf16[14,32,128]{2,1,0:T(8,128)(2,1)S(1)}, bf16[3,32,128]{2,1,0:T(8,128)(2,1)S(1)}) custom-call(bf16[64,32,128]{2,1,0:T(8,128)(2,1)} %bitcast.23, bf16[3,32,64]{2,1,0:T(8,128)(2,1)} %bitcast.30), custom_call_target="tpu_custom_call" | custom-call | tf_op jit(solution)/shard_map/pallas_call | solution.py:698
  1.2 5.0 %collective-permute-start = (bf16[14,32,128]{2,1,0:T(8,128)(2,1)S(1)}, bf16[14,32,128]{2,1,0:T(8,128)(2,1)S(1)}, u32[]{:S(2)}, u32[]{:S(2)}) collective-permute-start(bf16[14,32,128]{2,1,0:T(8,128)(2,1)S(1)} %get-tuple-element.29), channel_id=1, source_target_pairs={{0,32},{32,64},{64,96},{96,128},{128,160},{160,192},{192,224},{1,3... | collective-permute-start | bytes 344072 | tf_op jit(solution)/shard_map/ppermute | solution.py:831
  6.2 1.9 %collective-permute-start.1 = (bf16[14,32,128]{2,1,0:T(8,128)(2,1)S(1)}, bf16[14,32,128]{2,1,0:T(8,128)(2,1)S(1)}, u32[]{:S(2)}, u32[]{:S(2)}) collective-permute-start(bf16[14,32,128]{2,1,0:T(8,128)(2,1)S(1)} %get-tuple-element.30), channel_id=1, source_target_pairs={{32,0},{64,32},{96,64},{128,96},{160,128},{192,160},{224,192},{33,... | collective-permute-start | bytes 344072 | tf_op jit(solution)/shard_map/ppermute | solution.py:831
  8.2 0.0 copy-done.7
  8.2 0.1 fusion.4
  8.3 0.0 copy-start.10
  8.3 0.7 copy-done.10
  9.0 0.1 copy.18
  9.1 0.0 copy-start.11
  9.1 0.1 reshape.28
  9.2 0.0 copy-start.8
  9.2 0.5 copy-done.11
  9.7 0.1 pad_add_fusion.meta
  9.8 0.1 copy-done.8
  9.9 0.0 collective-permute-done.top
  9.9 6.6 %collective-permute-done.1.bot = bf16[14,32,128]{2,1,0:T(8,128)(2,1)S(1)} collective-permute-done((bf16[14,32,128]{2,1,0:T(8,128)(2,1)S(1)}, bf16[14,32,128]{2,1,0:T(8,128)(2,1)S(1)}, u32[]{:S(2)}, u32[]{:S(2)}) %collective-permute-start.1) | collective-permute-done | bytes 114720 | tf_op jit(solution)/shard_map/ppermute | solution.py:831
  16.5 0.0 copy-done
  16.5 0.0 copy-start.6
  16.5 0.0 copy-start.12
  16.5 0.1 shard_map.119
  16.7 0.0 copy-start.1
  16.7 1.4 %collective-permute-start.2 = (bf16[93,8,128]{2,1,0:T(8,128)(2,1)S(1)}, bf16[93,8,128]{2,1,0:T(8,128)(2,1)S(1)}, u32[]{:S(2)}, u32[]{:S(2)}) collective-permute-start(bf16[93,8,128]{2,1,0:T(8,128)(2,1)S(1)} %get-tuple-element.31), channel_id=1, source_target_pairs={{0,1},{1,2},{2,3},{3,4},{4,5},{5,6},{6,7},{7,8},{8,9},{9,10},{10,1... | collective-permute-start | bytes 571400 | tf_op jit(solution)/shard_map/ppermute | solution.py:831
  18.1 1.3 %collective-permute-start.3 = (bf16[93,8,128]{2,1,0:T(8,128)(2,1)S(1)}, bf16[93,8,128]{2,1,0:T(8,128)(2,1)S(1)}, u32[]{:S(2)}, u32[]{:S(2)}) collective-permute-start(bf16[93,8,128]{2,1,0:T(8,128)(2,1)S(1)} %get-tuple-element.32), channel_id=1, source_target_pairs={{1,0},{2,1},{3,2},{4,3},{5,4},{6,5},{7,6},{8,7},{9,8},{10,9},{11,1... | collective-permute-start | bytes 571400 | tf_op jit(solution)/shard_map/ppermute | solution.py:831
  19.4 0.0 copy-done.6
  19.5 0.0 copy-done.12
  19.5 0.0 collective-permute-done.2.left
  19.5 4.1 %collective-permute-done.3.right = bf16[93,8,128]{2,1,0:T(8,128)(2,1)S(1)} collective-permute-done((bf16[93,8,128]{2,1,0:T(8,128)(2,1)S(1)}, bf16[93,8,128]{2,1,0:T(8,128)(2,1)S(1)}, u32[]{:S(2)}, u32[]{:S(2)}) %collective-permute-start.3) | collective-permute-done | bytes 190496 | tf_op jit(solution)/shard_map/ppermute | solution.py:831
  23.6 5.5 %collective-permute-start.4 = (bf16[1136,128]{1,0:T(8,128)(2,1)S(1)}, bf16[1136,128]{1,0:T(8,128)(2,1)S(1)}, u32[]{:S(2)}, u32[]{:S(2)}) collective-permute-start(bf16[1136,128]{1,0:T(8,128)(2,1)S(1)} %fusion.1.mine), channel_id=1, source_target_pairs={{0,16},{1,17},{2,18},{3,19},{4,20},{5,21},{6,22},{7,23},{8,24},{9,... | collective-permute-start | bytes 872456 | tf_op jit(solution)/shard_map/ppermute | solution.py:870
  29.1 0.0 copy-done.1
  29.1 6.8 %shard_map.120 = (bf16[32,8,640]{2,1,0:T(8,128)(2,1)}, f32[1024,128]{1,0:T(8,128)S(1)}, bf16[68,48,128]{2,1,0:T(8,128)(2,1)}) custom-call(s32[194]{0:T(256)S(1)} %pad_add_fusion.meta, bf16[14,32,128]{2,1,0:T(8,128)(2,1)S(1)} %collective-permute-done.top, bf16[64,32,128]{2,1,0:T(8,128)(2,1)S(1)} %bitcast.25, ...), custom_call_target="tpu_custom_call" | custom-call | tf_op jit(solution)/shard_map/pallas_call | solution.py:698
  35.9 0.6 collective-permute-done.4.far
  36.5 0.0 copy-start.13
  36.5 0.0 copy-start.9
  36.5 0.0 copy-start.3
  36.5 8.2 %all-to-all-start = ((bf16[32,8,640]{2,1,0:T(8,128)(2,1)}), bf16[32,8,640]{2,1,0:T(8,128)(2,1)S(1)}, u32[]{:S(2)}, u32[]{:S(2)}) async-start(bf16[32,8,640]{2,1,0:T(8,128)(2,1)} %get-tuple-element.39), calls=%async_computation | async-start | bytes 655360 | tf_op jit(solution)/shard_map/all_to_all | solution.py:873
  44.8 0.4 collective-permute-start.5
  45.1 0.3 collective-permute-start.6
  45.4 0.0 copy-done.13
  45.4 0.0 copy-done.9
  45.4 0.0 copy-done.3
  45.4 7.9 %shard_map.121 = (bf16[3456,128]{1,0:T(8,128)(2,1)}, bf16[3648,128]{1,0:T(8,128)(2,1)}, f32[8,128]{1,0:T(8,128)S(1)}) custom-call(s32[194]{0:T(256)S(1)} %pad_add_fusion.meta, f32[1024,128]{1,0:T(8,128)S(1)} %get-tuple-element.41.dec, bf16[3,32,128]{2,1,0:T(8,128)(2,1)S(1)} %get-tuple-element.42.tall, bf16[93,8,128]{2,1,0:T(8,128)(2,1)S(1)} %collective-permute-done.2.left, ...), custom_call_target="tpu_custom_call" | custom-call | tf_op jit(solution)/shard_map/pallas_call | solution.py:698
  53.4 0.0 collective-permute-done.5.other
  53.4 0.0 collective-permute-done.6.far_other
  53.4 5.9 %all-to-all-done.strip = bf16[32,8,640]{2,1,0:T(8,128)(2,1)S(1)} async-done(((bf16[32,8,640]{2,1,0:T(8,128)(2,1)}), bf16[32,8,640]{2,1,0:T(8,128)(2,1)S(1)}, u32[]{:S(2)}, u32[]{:S(2)}) %all-to-all-start) | async-done | bytes 327712 | tf_op jit(solution)/shard_map/all_to_all | solution.py:873
  59.3 14.3 %shard_map.122 = bf16[32,40,128]{2,1,0:T(8,128)(2,1)} custom-call(s32[194]{0:T(256)S(1)} %pad_add_fusion.meta, bf16[32,8,640]{2,1,0:T(8,128)(2,1)S(1)} %all-to-all-done.strip, bf16[1136,128]{1,0:T(8,128)(2,1)S(1)} %fusion.1.mine, bf16[1136,128]{1,0:T(8,128)(2,1)S(1)} %collective-permute-done.5.other, bf16[1136,128]{1,0:T(8,128)(2,1)S(1)} %collective-permute-done.4.far, ...), custom_call_target="tpu_custom_call" | custom-call | tf_op jit(solution)/shard_map/pallas_call | solution.py:698
  73.6 6.0 %all-to-all-start.1 = ((bf16[32,40,128]{2,1,0:T(8,128)(2,1)}), bf16[32,40,128]{2,1,0:T(8,128)(2,1)S(1)}, u32[]{:S(2)}, u32[]{:S(2)}) async-start(bf16[32,40,128]{2,1,0:T(8,128)(2,1)} %shard_map.122), calls=%async_computation.1 | async-start | bytes 655360 | tf_op jit(solution)/shard_map/all_to_all | solution.py:880
  79.6 0.0 copy-start.2
  79.6 6.0 %shard_map.123 = (f32[640,128]{1,0:T(8,128)S(1)}, bf16[64,32,128]{2,1,0:T(8,128)(2,1)S(1)}, bf16[384,384]{1,0:T(8,128)(2,1)S(1)}, bf16[256,512]{1,0:T(8,128)(2,1)S(1)}) custom-call(s32[194]{0:T(256)S(1)} %pad_add_fusion.meta, bf16[3456,128]{1,0:T(8,128)(2,1)} %get-tuple-element.44.feat, bf16[3648,128]{1,0:T(8,128)(2,1)} %get-tuple-element.45.slope_one, ...), custom_call_target="tpu_custom_call" | custom-call | tf_op jit(solution)/shard_map/pallas_call | solution.py:698
  85.6 0.0 copy-start.4
  85.6 0.7 copy-done.4
  86.3 7.6 %all-to-all-done.1.parts = bf16[32,40,128]{2,1,0:T(8,128)(2,1)S(1)} async-done(((bf16[32,40,128]{2,1,0:T(8,128)(2,1)}), bf16[32,40,128]{2,1,0:T(8,128)(2,1)S(1)}, u32[]{:S(2)}, u32[]{:S(2)}) %all-to-all-start.1) | async-done | bytes 327712 | tf_op jit(solution)/shard_map/all_to_all | solution.py:880
  93.9 0.0 copy-done.2
  93.9 0.0 copy-start.5
  93.9 0.9 copy-done.5
  94.8 3.8 %shard_map.124 = bf16[64,32,128]{2,1,0:T(8,128)(2,1)} custom-call(s32[194]{0:T(256)S(1)} %pad_add_fusion.meta, bf16[32,40,128]{2,1,0:T(8,128)(2,1)S(1)} %all-to-all-done.1.parts, f32[640,128]{1,0:T(8,128)S(1)} %get-tuple-element.46.lpips, bf16[68,48,128]{2,1,0:T(8,128)(2,1)S(1)} %copy-done.2, bf16[64,32,128]{2,1,0:T(8,128)(2,1)S(1)} %get-tuple-element.48.feats_slope, ...), custom_call_target="tpu_custom_call" | custom-call | tf_op jit(solution)/shard_map/pallas_call | solution.py:698
  (7 shorter events, 0.1 us)
Async XLA Ops:
  0.0 16.5 %copy-start = (bf16[1,64,32,128]{3,2,1,0:T(8,128)(2,1)S(1)}, bf16[1,64,32,128]{3,2,1,0:T(8,128)(2,1)}, u32[]{:S(2)}) copy-start(bf16[1,64,32,128]{3,2,1,0:T(8,128)(2,1)} %param.12) | copy-start | bytes 1572868
  0.0 8.2 %copy-start.7 = (bf16[1,4,4,3,64]{4,2,3,1,0:T(4,128)(2,1)S(1)}, bf16[1,4,4,3,64]{4,2,3,1,0:T(4,128)(2,1)}, u32[]{:S(2)}) copy-start(bf16[1,4,4,3,64]{4,2,3,1,0:T(4,128)(2,1)} %param.21) | copy-start | bytes 18436
  1.2 8.7 %collective-permute-start = (bf16[14,32,128]{2,1,0:T(8,128)(2,1)S(1)}, bf16[14,32,128]{2,1,0:T(8,128)(2,1)S(1)}, u32[]{:S(2)}, u32[]{:S(2)}) collective-permute-start(bf16[14,32,128]{2,1,0:T(8,128)(2,1)S(1)} %get-tuple-element.29), channel_id=1, source_target_pairs={{0,32},{32,64},{64,96},{96,128},{128,160},{160,192},{192,224},{1,3... | collective-permute-start | bytes 344072 | tf_op jit(solution)/shard_map/ppermute | solution.py:831
  6.2 10.3 %collective-permute-start.1 = (bf16[14,32,128]{2,1,0:T(8,128)(2,1)S(1)}, bf16[14,32,128]{2,1,0:T(8,128)(2,1)S(1)}, u32[]{:S(2)}, u32[]{:S(2)}) collective-permute-start(bf16[14,32,128]{2,1,0:T(8,128)(2,1)S(1)} %get-tuple-element.30), channel_id=1, source_target_pairs={{32,0},{64,32},{96,64},{128,96},{160,128},{192,160},{224,192},{33,... | collective-permute-start | bytes 344072 | tf_op jit(solution)/shard_map/ppermute | solution.py:831
  8.3 0.7 copy-start.10
  9.1 0.7 copy-start.11
  9.2 0.7 copy-start.8
  16.5 2.9 %copy-start.6 = (bf16[1,4,4,64,128]{4,3,2,1,0:T(8,128)(2,1)S(1)}, bf16[1,4,4,64,128]{4,3,2,1,0:T(8,128)(2,1)}, u32[]{:S(2)}) copy-start(bf16[1,4,4,64,128]{4,3,2,1,0:T(8,128)(2,1)} %param.22) | copy-start | bytes 786436
  16.5 2.9 %copy-start.12 = (bf16[1,128]{1,0:T(2,128)(2,1)S(1)}, bf16[1,128]{1,0:T(2,128)(2,1)}, u32[]{:S(2)}) copy-start(bf16[1,128]{1,0:T(2,128)(2,1)} %param.23) | copy-start | bytes 772
  16.7 12.4 %copy-start.1 = (bf16[3,3,128,128]{3,2,1,0:T(8,128)(2,1)S(1)}, bf16[3,3,128,128]{3,2,1,0:T(8,128)(2,1)}, u32[]{:S(2)}) copy-start(bf16[3,3,128,128]{3,2,1,0:T(8,128)(2,1)} %w_mid.3) | copy-start | bytes 884740
  16.7 2.8 %collective-permute-start.2 = (bf16[93,8,128]{2,1,0:T(8,128)(2,1)S(1)}, bf16[93,8,128]{2,1,0:T(8,128)(2,1)S(1)}, u32[]{:S(2)}, u32[]{:S(2)}) collective-permute-start(bf16[93,8,128]{2,1,0:T(8,128)(2,1)S(1)} %get-tuple-element.31), channel_id=1, source_target_pairs={{0,1},{1,2},{2,3},{3,4},{4,5},{5,6},{6,7},{7,8},{8,9},{9,10},{10,1... | collective-permute-start | bytes 571400 | tf_op jit(solution)/shard_map/ppermute | solution.py:831
  18.1 5.5 %collective-permute-start.3 = (bf16[93,8,128]{2,1,0:T(8,128)(2,1)S(1)}, bf16[93,8,128]{2,1,0:T(8,128)(2,1)S(1)}, u32[]{:S(2)}, u32[]{:S(2)}) collective-permute-start(bf16[93,8,128]{2,1,0:T(8,128)(2,1)S(1)} %get-tuple-element.32), channel_id=1, source_target_pairs={{1,0},{2,1},{3,2},{4,3},{5,4},{6,5},{7,6},{8,7},{9,8},{10,9},{11,1... | collective-permute-start | bytes 571400 | tf_op jit(solution)/shard_map/ppermute | solution.py:831
  23.6 12.9 %collective-permute-start.4 = (bf16[1136,128]{1,0:T(8,128)(2,1)S(1)}, bf16[1136,128]{1,0:T(8,128)(2,1)S(1)}, u32[]{:S(2)}, u32[]{:S(2)}) collective-permute-start(bf16[1136,128]{1,0:T(8,128)(2,1)S(1)} %fusion.1.mine), channel_id=1, source_target_pairs={{0,16},{1,17},{2,18},{3,19},{4,20},{5,21},{6,22},{7,23},{8,24},{9,... | collective-permute-start | bytes 872456 | tf_op jit(solution)/shard_map/ppermute | solution.py:870
  36.5 8.9 %copy-start.13 = (f32[64]{0:T(128)S(1)}, f32[64]{0:T(128)}, u32[]{:S(2)}) copy-start(f32[64]{0:T(128)} %param.18) | copy-start | bytes 772
  36.5 8.9 %copy-start.9 = (bf16[3,3,3,64]{3,2,1,0:T(4,128)(2,1)S(1)}, bf16[3,3,3,64]{3,2,1,0:T(4,128)(2,1)}, u32[]{:S(2)}) copy-start(bf16[3,3,3,64]{3,2,1,0:T(4,128)(2,1)} %param.16) | copy-start | bytes 10372
  36.5 8.9 %copy-start.3 = (bf16[3,3,64,64]{3,2,1,0:T(8,128)(2,1)S(1)}, bf16[3,3,64,64]{3,2,1,0:T(8,128)(2,1)}, u32[]{:S(2)}) copy-start(bf16[3,3,64,64]{3,2,1,0:T(8,128)(2,1)} %v_second.3) | copy-start | bytes 221188
  36.5 22.7 %all-to-all-start = ((bf16[32,8,640]{2,1,0:T(8,128)(2,1)}), bf16[32,8,640]{2,1,0:T(8,128)(2,1)S(1)}, u32[]{:S(2)}, u32[]{:S(2)}) async-start(bf16[32,8,640]{2,1,0:T(8,128)(2,1)} %get-tuple-element.39), calls=%async_computation | async-start | bytes 655360 | tf_op jit(solution)/shard_map/all_to_all | solution.py:873
  44.8 8.6 %collective-permute-start.5 = (bf16[1136,128]{1,0:T(8,128)(2,1)S(1)}, bf16[1136,128]{1,0:T(8,128)(2,1)S(1)}, u32[]{:S(2)}, u32[]{:S(2)}) collective-permute-start(bf16[1136,128]{1,0:T(8,128)(2,1)S(1)} %fusion.1.mine), channel_id=1, source_target_pairs={{0,1},{1,0},{2,3},{3,2},{4,5},{5,4},{6,7},{7,6},{8,9},{9,8},{10,11... | collective-permute-start | bytes 872456 | tf_op jit(solution)/shard_map/ppermute | solution.py:874
  45.1 8.3 %collective-permute-start.6 = (bf16[1136,128]{1,0:T(8,128)(2,1)S(1)}, bf16[1136,128]{1,0:T(8,128)(2,1)}, u32[]{:S(2)}, u32[]{:S(2)}) collective-permute-start(bf16[1136,128]{1,0:T(8,128)(2,1)S(1)} %collective-permute-done.4.far), channel_id=1, source_target_pairs={{0,1},{1,0},{2,3},{3,2},{4,5},{5,4},{6,7},{7,6},{8,9},{9,8},{10,11... | collective-permute-start | bytes 872456 | tf_op jit(solution)/shard_map/ppermute | solution.py:875
  73.6 20.3 %all-to-all-start.1 = ((bf16[32,40,128]{2,1,0:T(8,128)(2,1)}), bf16[32,40,128]{2,1,0:T(8,128)(2,1)S(1)}, u32[]{:S(2)}, u32[]{:S(2)}) async-start(bf16[32,40,128]{2,1,0:T(8,128)(2,1)} %shard_map.122), calls=%async_computation.1 | async-start | bytes 655360 | tf_op jit(solution)/shard_map/all_to_all | solution.py:880
  79.6 14.3 %copy-start.2 = (bf16[68,48,128]{2,1,0:T(8,128)(2,1)S(1)}, bf16[68,48,128]{2,1,0:T(8,128)(2,1)}, u32[]{:S(2)}) copy-start(bf16[68,48,128]{2,1,0:T(8,128)(2,1)} %get-tuple-element.47.slope) | copy-start | bytes 2506756
  85.6 0.7 copy-start.4
  93.9 1.0 copy-start.5

commit v7 on v6

--- a/solution.py
+++ b/solution.py
@@ -320,7 +320,7 @@
 
 
 def percept_back_kernel(
-    meta, feat, slope_one, v_first, v_second, feats, w_mid, w_out, out, feats_slope, w, w1,
+    meta, feat, slope_one, v_first, v_second, feats, w_mid, out, feats_slope, w,
     bv, w3, w4,
 ):
     r, c = meta[0], meta[1]
@@ -335,11 +335,6 @@
         for dx in range(3):
             w[dx * 128 : (dx + 1) * 128, dy * 128 : (dy + 1) * 128] = w_mid[2 - dy, 2 - dx]
 
-    def small(dy):
-        flipped = [w_out[2 - dy, (2 - dx) * 8 : (3 - dx) * 8, :] for dx in range(3)]
-        return jnp.concatenate(flipped + [jnp.zeros((8, 128), F32)], axis=0)
-
-    patch_weights(w1, small)
     def feature_slope(i, carry):
         at = pl.ds(i * 8, 8)
         feats_slope[at] = silu_parts(feats[at].astype(F32))[1].astype(BF)
@@ -414,7 +409,7 @@
             strip32[pl.ds(aligned(k * TW + g * 8, 8), 8), :] = row
         return carry
 
-    lax.fori_loop(0, COLS, unpack, 0, unroll=8)
+    lax.fori_loop(0, COLS, unpack, 0, unroll=16)
     strip32[IMG_W:, :] = jnp.zeros((8, 256), F32)
     grads[...] = jnp.zeros(grads.shape, F32)
     w_back[...] = jnp.zeros(w_back.shape, BF)
@@ -637,13 +632,18 @@
         ).astype(BF)
         return carry
 
-    lax.fori_loop(0, COLS, pack, 0, unroll=4)
+    lax.fori_loop(0, COLS, pack, 0, unroll=8)
 
 
 def finish_kernel(
-    meta, parts, lpips, slope, feats_slope, w, w1, out, turned, planes, px, bm
+    meta, parts, lpips, slope, feats_slope, w, w_out, out, turned, planes, px, bm, w1
 ):
     r, c = meta[0], meta[1]
+    def small(dy):
+        flipped = [w_out[2 - dy, (2 - dx) * 8 : (3 - dx) * 8, :] for dx in range(3)]
+        return jnp.concatenate(flipped + [jnp.zeros((8, 128), F32)], axis=0)
+
+    patch_weights(w1, small)
     col_ok = column_mask(c * TW - 2)
     planes[...] = jnp.zeros(planes.shape, F32)
     for half in range(2):
@@ -751,17 +751,16 @@
     )
 
 
-def percept_back(meta, feat, slope_one, small, vgg_second, feats, conv_mid, out_small):
+def percept_back(meta, feat, slope_one, small, vgg_second, feats, conv_mid):
     return call(
         percept_back_kernel,
         (
             shape((80 * 8, 128), F32),
             shape((TH, TW, 128), BF),
             shape((384, 384), BF),
-            shape((256, 512), BF),
         ),
         [((82 * WIDE, 128), BF), ((384, 384), BF), ((384, 384), BF)],
-        (meta, feat, slope_one, small, vgg_second, feats, conv_mid, out_small),
+        (meta, feat, slope_one, small, vgg_second, feats, conv_mid),
     )
 
 
@@ -806,7 +805,7 @@
     )
 
 
-def finish(meta, parts, lpips, slope, feats_slope, w, w1):
+def finish(meta, parts, lpips, slope, feats_slope, w, small):
     return call(
         finish_kernel,
         shape((TH, TW, 128), BF),
@@ -815,8 +814,9 @@
             ((80 * 8, 128), F32),
             ((18 * WIDE, 128), BF),
             ((68 * WIDE, 128), BF),
+            ((256, 512), BF),
         ],
-        (meta, parts, lpips, slope, feats_slope, w, w1),
+        (meta, parts, lpips, slope, feats_slope, w, small),
     )
 
 
@@ -879,9 +879,9 @@
     grads = critics(meta, strip, (mine, other, far, in_hbm(far_other)), done)
     parts = lax.all_to_all(grads, "col", split_axis=0, concat_axis=0, tiled=True)
     lpips, *made = percept_back(
-        meta, in_hbm(feat), in_hbm(slope_one), vgg_small, vgg_second, feats, conv_mid, out_small
-    )
-    return finish(meta, parts, lpips, slope, *made)[None]
+        meta, in_hbm(feat), in_hbm(slope_one), vgg_small, vgg_second, feats, conv_mid
+    )
+    return finish(meta, parts, lpips, slope, *made, out_small)[None]
 
 
 def solution(mesh):

time: 99.8 us -> 97.8 us (0.980)
  local copies, waits for them, and re-layouts: 3.24 us -> 1.59 us
    unnamed x29 -> x25, local copies, waits for them, and re-layouts: 3.08 us -> 1.43 us
where the time goes in v7:
time: 97.8 us; the launch traced here: 96.8 us
  Pallas kernels  39.8 us (41%)
  starting transfers between devices  29.6 us (30%)
  waiting for transfers between devices  25.5 us (26%)
  local copies, waits for them, and re-layouts  1.59 us (2%)
    pallas_call x7, Pallas kernels, call(): pl.pallas_call(kernel, in_specs=specs, out_specs=jax.tree.map(lambda _: p...  39.8 us
    ppermute x2, waiting for transfers between devices, exchange(): lax.ppermute(high, axis, backward)  10.7 us
    all_to_all x1, waiting for transfers between devices, local(): lax.all_to_all(grads, 'col', split_axis=0, concat_axis=0, tiled=True)  8.27 us
    all_to_all x1, starting transfers between devices, local(): strip = lax.all_to_all(pay, 'col', split_axis=0, concat_axis=0, tiled=True)  8.2 us
    ppermute x2, starting transfers between devices, exchange(): lax.ppermute(low, axis, forward)  6.45 us
    all_to_all x1, waiting for transfers between devices, local(): strip = lax.all_to_all(pay, 'col', split_axis=0, concat_axis=0, tiled=True)  5.89 us
    all_to_all x1, starting transfers between devices, local(): lax.all_to_all(grads, 'col', split_axis=0, concat_axis=0, tiled=True)  5.59 us
    ppermute x1, starting transfers between devices, local(): far = lax.ppermute(sent, 'col', [(i, i ^ FAR) for i in range(COLS)])  5.5 us
  transfers between devices with their start and end apart: 9, of which 5 were waited for; matrix products, arithmetic and copies ran while one was open for 0% of the time, Pallas kernels for 21%

profile of v7, /device:TPU:6, one launch (start us, length us, event | category | flops | bytes accessed | tf_op | source)
XLA Modules:
  0.0 96.8 jit_solution(5973356524465406966)
XLA Ops:
  0.0 0.0 copy-start
  0.0 0.0 copy-start.5
  0.0 1.2 %shard_map.118 = (bf16[14,32,128]{2,1,0:T(8,128)(2,1)S(1)}, bf16[14,32,128]{2,1,0:T(8,128)(2,1)S(1)}, bf16[3,32,128]{2,1,0:T(8,128)(2,1)S(1)}) custom-call(bf16[64,32,128]{2,1,0:T(8,128)(2,1)} %bitcast.23, bf16[3,32,64]{2,1,0:T(8,128)(2,1)} %bitcast.30), custom_call_target="tpu_custom_call" | custom-call | tf_op jit(solution)/shard_map/pallas_call | solution.py:698
  1.2 5.0 %collective-permute-start = (bf16[14,32,128]{2,1,0:T(8,128)(2,1)S(1)}, bf16[14,32,128]{2,1,0:T(8,128)(2,1)S(1)}, u32[]{:S(2)}, u32[]{:S(2)}) collective-permute-start(bf16[14,32,128]{2,1,0:T(8,128)(2,1)S(1)} %get-tuple-element.28), channel_id=1, source_target_pairs={{0,32},{32,64},{64,96},{96,128},{128,160},{160,192},{192,224},{1,3... | collective-permute-start | bytes 344072 | tf_op jit(solution)/shard_map/ppermute | solution.py:831
  6.2 1.9 %collective-permute-start.1 = (bf16[14,32,128]{2,1,0:T(8,128)(2,1)S(1)}, bf16[14,32,128]{2,1,0:T(8,128)(2,1)S(1)}, u32[]{:S(2)}, u32[]{:S(2)}) collective-permute-start(bf16[14,32,128]{2,1,0:T(8,128)(2,1)S(1)} %get-tuple-element.29), channel_id=1, source_target_pairs={{32,0},{64,32},{96,64},{128,96},{160,128},{192,160},{224,192},{33,... | collective-permute-start | bytes 344072 | tf_op jit(solution)/shard_map/ppermute | solution.py:831
  8.2 0.0 copy-done.5
  8.2 0.1 fusion.4
  8.3 0.0 copy-start.8
  8.3 0.7 copy-done.8
  9.0 0.1 copy.18
  9.1 0.0 copy-start.9
  9.1 0.1 reshape.28
  9.2 0.0 copy-start.6
  9.2 0.5 copy-done.9
  9.7 0.1 pad_add_fusion.meta
  9.8 0.1 copy-done.6
  9.9 0.0 collective-permute-done.top
  9.9 6.6 %collective-permute-done.1.bot = bf16[14,32,128]{2,1,0:T(8,128)(2,1)S(1)} collective-permute-done((bf16[14,32,128]{2,1,0:T(8,128)(2,1)S(1)}, bf16[14,32,128]{2,1,0:T(8,128)(2,1)S(1)}, u32[]{:S(2)}, u32[]{:S(2)}) %collective-permute-start.1) | collective-permute-done | bytes 114720 | tf_op jit(solution)/shard_map/ppermute | solution.py:831
  16.5 0.0 copy-done
  16.5 0.0 copy-start.4
  16.5 0.0 copy-start.10
  16.5 0.1 shard_map.119
  16.7 0.0 copy-start.1
  16.7 1.4 %collective-permute-start.2 = (bf16[93,8,128]{2,1,0:T(8,128)(2,1)S(1)}, bf16[93,8,128]{2,1,0:T(8,128)(2,1)S(1)}, u32[]{:S(2)}, u32[]{:S(2)}) collective-permute-start(bf16[93,8,128]{2,1,0:T(8,128)(2,1)S(1)} %get-tuple-element.30), channel_id=1, source_target_pairs={{0,1},{1,2},{2,3},{3,4},{4,5},{5,6},{6,7},{7,8},{8,9},{9,10},{10,1... | collective-permute-start | bytes 571400 | tf_op jit(solution)/shard_map/ppermute | solution.py:831
  18.1 1.3 %collective-permute-start.3 = (bf16[93,8,128]{2,1,0:T(8,128)(2,1)S(1)}, bf16[93,8,128]{2,1,0:T(8,128)(2,1)S(1)}, u32[]{:S(2)}, u32[]{:S(2)}) collective-permute-start(bf16[93,8,128]{2,1,0:T(8,128)(2,1)S(1)} %get-tuple-element.31), channel_id=1, source_target_pairs={{1,0},{2,1},{3,2},{4,3},{5,4},{6,5},{7,6},{8,7},{9,8},{10,9},{11,1... | collective-permute-start | bytes 571400 | tf_op jit(solution)/shard_map/ppermute | solution.py:831
  19.4 0.0 copy-done.4
  19.5 0.0 copy-done.10
  19.5 0.0 collective-permute-done.2.left
  19.5 4.1 %collective-permute-done.3.right = bf16[93,8,128]{2,1,0:T(8,128)(2,1)S(1)} collective-permute-done((bf16[93,8,128]{2,1,0:T(8,128)(2,1)S(1)}, bf16[93,8,128]{2,1,0:T(8,128)(2,1)S(1)}, u32[]{:S(2)}, u32[]{:S(2)}) %collective-permute-start.3) | collective-permute-done | bytes 190496 | tf_op jit(solution)/shard_map/ppermute | solution.py:831
  23.6 5.5 %collective-permute-start.4 = (bf16[1136,128]{1,0:T(8,128)(2,1)S(1)}, bf16[1136,128]{1,0:T(8,128)(2,1)S(1)}, u32[]{:S(2)}, u32[]{:S(2)}) collective-permute-start(bf16[1136,128]{1,0:T(8,128)(2,1)S(1)} %fusion.1.mine), channel_id=1, source_target_pairs={{0,16},{1,17},{2,18},{3,19},{4,20},{5,21},{6,22},{7,23},{8,24},{9,... | collective-permute-start | bytes 872456 | tf_op jit(solution)/shard_map/ppermute | solution.py:870
  29.1 0.0 copy-done.1
  29.1 6.8 %shard_map.120 = (bf16[32,8,640]{2,1,0:T(8,128)(2,1)}, f32[1024,128]{1,0:T(8,128)S(1)}, bf16[68,48,128]{2,1,0:T(8,128)(2,1)}) custom-call(s32[194]{0:T(256)S(1)} %pad_add_fusion.meta, bf16[14,32,128]{2,1,0:T(8,128)(2,1)S(1)} %collective-permute-done.top, bf16[64,32,128]{2,1,0:T(8,128)(2,1)S(1)} %bitcast.25, ...), custom_call_target="tpu_custom_call" | custom-call | tf_op jit(solution)/shard_map/pallas_call | solution.py:698
  35.9 0.6 collective-permute-done.4.far
  36.5 0.0 copy-start.11
  36.5 0.0 copy-start.7
  36.5 0.0 copy-start.3
  36.5 8.2 %all-to-all-start = ((bf16[32,8,640]{2,1,0:T(8,128)(2,1)}), bf16[32,8,640]{2,1,0:T(8,128)(2,1)S(1)}, u32[]{:S(2)}, u32[]{:S(2)}) async-start(bf16[32,8,640]{2,1,0:T(8,128)(2,1)} %get-tuple-element.38), calls=%async_computation | async-start | bytes 655360 | tf_op jit(solution)/shard_map/all_to_all | solution.py:873
  44.8 0.4 collective-permute-start.5
  45.1 0.3 collective-permute-start.6
  45.4 0.0 copy-done.11
  45.4 0.0 copy-done.7
  45.4 0.0 copy-done.3
  45.4 7.9 %shard_map.121 = (bf16[3456,128]{1,0:T(8,128)(2,1)}, bf16[3648,128]{1,0:T(8,128)(2,1)}, f32[8,128]{1,0:T(8,128)S(1)}) custom-call(s32[194]{0:T(256)S(1)} %pad_add_fusion.meta, f32[1024,128]{1,0:T(8,128)S(1)} %get-tuple-element.40.dec, bf16[3,32,128]{2,1,0:T(8,128)(2,1)S(1)} %get-tuple-element.41.tall, bf16[93,8,128]{2,1,0:T(8,128)(2,1)S(1)} %collective-permute-done.2.left, ...), custom_call_target="tpu_custom_call" | custom-call | tf_op jit(solution)/shard_map/pallas_call | solution.py:698
  53.4 0.0 collective-permute-done.5.other
  53.4 0.0 collective-permute-done.6.far_other
  53.4 5.9 %all-to-all-done.strip = bf16[32,8,640]{2,1,0:T(8,128)(2,1)S(1)} async-done(((bf16[32,8,640]{2,1,0:T(8,128)(2,1)}), bf16[32,8,640]{2,1,0:T(8,128)(2,1)S(1)}, u32[]{:S(2)}, u32[]{:S(2)}) %all-to-all-start) | async-done | bytes 327712 | tf_op jit(solution)/shard_map/all_to_all | solution.py:873
  59.3 13.9 %shard_map.122 = bf16[32,40,128]{2,1,0:T(8,128)(2,1)} custom-call(s32[194]{0:T(256)S(1)} %pad_add_fusion.meta, bf16[32,8,640]{2,1,0:T(8,128)(2,1)S(1)} %all-to-all-done.strip, bf16[1136,128]{1,0:T(8,128)(2,1)S(1)} %fusion.1.mine, bf16[1136,128]{1,0:T(8,128)(2,1)S(1)} %collective-permute-done.5.other, bf16[1136,128]{1,0:T(8,128)(2,1)S(1)} %collective-permute-done.4.far, ...), custom_call_target="tpu_custom_call" | custom-call | tf_op jit(solution)/shard_map/pallas_call | solution.py:698
  73.1 5.6 %all-to-all-start.1 = ((bf16[32,40,128]{2,1,0:T(8,128)(2,1)}), bf16[32,40,128]{2,1,0:T(8,128)(2,1)S(1)}, u32[]{:S(2)}, u32[]{:S(2)}) async-start(bf16[32,40,128]{2,1,0:T(8,128)(2,1)} %shard_map.122), calls=%async_computation.1 | async-start | bytes 655360 | tf_op jit(solution)/shard_map/all_to_all | solution.py:880
  78.7 0.0 copy-start.2
  78.8 6.0 %shard_map.123 = (f32[640,128]{1,0:T(8,128)S(1)}, bf16[64,32,128]{2,1,0:T(8,128)(2,1)S(1)}, bf16[384,384]{1,0:T(8,128)(2,1)S(1)}) custom-call(s32[194]{0:T(256)S(1)} %pad_add_fusion.meta, bf16[3456,128]{1,0:T(8,128)(2,1)} %get-tuple-element.43.feat, bf16[3648,128]{1,0:T(8,128)(2,1)} %get-tuple-element.44.slope_one, ...), custom_call_target="tpu_custom_call" | custom-call | tf_op jit(solution)/shard_map/pallas_call | solution.py:698
  84.7 8.3 %all-to-all-done.1.parts = bf16[32,40,128]{2,1,0:T(8,128)(2,1)S(1)} async-done(((bf16[32,40,128]{2,1,0:T(8,128)(2,1)}), bf16[32,40,128]{2,1,0:T(8,128)(2,1)S(1)}, u32[]{:S(2)}, u32[]{:S(2)}) %all-to-all-start.1) | async-done | bytes 327712 | tf_op jit(solution)/shard_map/all_to_all | solution.py:880
  93.0 0.0 copy-done.2
  93.0 3.8 %shard_map.124 = bf16[64,32,128]{2,1,0:T(8,128)(2,1)} custom-call(s32[194]{0:T(256)S(1)} %pad_add_fusion.meta, bf16[32,40,128]{2,1,0:T(8,128)(2,1)S(1)} %all-to-all-done.1.parts, f32[640,128]{1,0:T(8,128)S(1)} %get-tuple-element.45.lpips, bf16[68,48,128]{2,1,0:T(8,128)(2,1)S(1)} %copy-done.2, bf16[64,32,128]{2,1,0:T(8,128)(2,1)S(1)} %get-tuple-element.47.feats_slope, ...), custom_call_target="tpu_custom_call" | custom-call | tf_op jit(solution)/shard_map/pallas_call | solution.py:698
  (7 shorter events, 0.1 us)
Async XLA Ops:
  0.0 16.5 %copy-start = (bf16[1,64,32,128]{3,2,1,0:T(8,128)(2,1)S(1)}, bf16[1,64,32,128]{3,2,1,0:T(8,128)(2,1)}, u32[]{:S(2)}) copy-start(bf16[1,64,32,128]{3,2,1,0:T(8,128)(2,1)} %param.12) | copy-start | bytes 1572868
  0.0 8.2 %copy-start.5 = (bf16[1,4,4,3,64]{4,2,3,1,0:T(4,128)(2,1)S(1)}, bf16[1,4,4,3,64]{4,2,3,1,0:T(4,128)(2,1)}, u32[]{:S(2)}) copy-start(bf16[1,4,4,3,64]{4,2,3,1,0:T(4,128)(2,1)} %param.21) | copy-start | bytes 18436
  1.2 8.7 %collective-permute-start = (bf16[14,32,128]{2,1,0:T(8,128)(2,1)S(1)}, bf16[14,32,128]{2,1,0:T(8,128)(2,1)S(1)}, u32[]{:S(2)}, u32[]{:S(2)}) collective-permute-start(bf16[14,32,128]{2,1,0:T(8,128)(2,1)S(1)} %get-tuple-element.28), channel_id=1, source_target_pairs={{0,32},{32,64},{64,96},{96,128},{128,160},{160,192},{192,224},{1,3... | collective-permute-start | bytes 344072 | tf_op jit(solution)/shard_map/ppermute | solution.py:831
  6.2 10.3 %collective-permute-start.1 = (bf16[14,32,128]{2,1,0:T(8,128)(2,1)S(1)}, bf16[14,32,128]{2,1,0:T(8,128)(2,1)S(1)}, u32[]{:S(2)}, u32[]{:S(2)}) collective-permute-start(bf16[14,32,128]{2,1,0:T(8,128)(2,1)S(1)} %get-tuple-element.29), channel_id=1, source_target_pairs={{32,0},{64,32},{96,64},{128,96},{160,128},{192,160},{224,192},{33,... | collective-permute-start | bytes 344072 | tf_op jit(solution)/shard_map/ppermute | solution.py:831
  8.3 0.7 copy-start.8
  9.1 0.7 copy-start.9
  9.2 0.7 copy-start.6
  16.5 2.9 %copy-start.4 = (bf16[1,4,4,64,128]{4,3,2,1,0:T(8,128)(2,1)S(1)}, bf16[1,4,4,64,128]{4,3,2,1,0:T(8,128)(2,1)}, u32[]{:S(2)}) copy-start(bf16[1,4,4,64,128]{4,3,2,1,0:T(8,128)(2,1)} %param.22) | copy-start | bytes 786436
  16.5 2.9 %copy-start.10 = (bf16[1,128]{1,0:T(2,128)(2,1)S(1)}, bf16[1,128]{1,0:T(2,128)(2,1)}, u32[]{:S(2)}) copy-start(bf16[1,128]{1,0:T(2,128)(2,1)} %param.23) | copy-start | bytes 772
  16.7 12.4 %copy-start.1 = (bf16[3,3,128,128]{3,2,1,0:T(8,128)(2,1)S(1)}, bf16[3,3,128,128]{3,2,1,0:T(8,128)(2,1)}, u32[]{:S(2)}) copy-start(bf16[3,3,128,128]{3,2,1,0:T(8,128)(2,1)} %w_mid.3) | copy-start | bytes 884740
  16.7 2.8 %collective-permute-start.2 = (bf16[93,8,128]{2,1,0:T(8,128)(2,1)S(1)}, bf16[93,8,128]{2,1,0:T(8,128)(2,1)S(1)}, u32[]{:S(2)}, u32[]{:S(2)}) collective-permute-start(bf16[93,8,128]{2,1,0:T(8,128)(2,1)S(1)} %get-tuple-element.30), channel_id=1, source_target_pairs={{0,1},{1,2},{2,3},{3,4},{4,5},{5,6},{6,7},{7,8},{8,9},{9,10},{10,1... | collective-permute-start | bytes 571400 | tf_op jit(solution)/shard_map/ppermute | solution.py:831
  18.1 5.5 %collective-permute-start.3 = (bf16[93,8,128]{2,1,0:T(8,128)(2,1)S(1)}, bf16[93,8,128]{2,1,0:T(8,128)(2,1)S(1)}, u32[]{:S(2)}, u32[]{:S(2)}) collective-permute-start(bf16[93,8,128]{2,1,0:T(8,128)(2,1)S(1)} %get-tuple-element.31), channel_id=1, source_target_pairs={{1,0},{2,1},{3,2},{4,3},{5,4},{6,5},{7,6},{8,7},{9,8},{10,9},{11,1... | collective-permute-start | bytes 571400 | tf_op jit(solution)/shard_map/ppermute | solution.py:831
  23.6 12.9 %collective-permute-start.4 = (bf16[1136,128]{1,0:T(8,128)(2,1)S(1)}, bf16[1136,128]{1,0:T(8,128)(2,1)S(1)}, u32[]{:S(2)}, u32[]{:S(2)}) collective-permute-start(bf16[1136,128]{1,0:T(8,128)(2,1)S(1)} %fusion.1.mine), channel_id=1, source_target_pairs={{0,16},{1,17},{2,18},{3,19},{4,20},{5,21},{6,22},{7,23},{8,24},{9,... | collective-permute-start | bytes 872456 | tf_op jit(solution)/shard_map/ppermute | solution.py:870
  36.5 8.9 %copy-start.11 = (f32[64]{0:T(128)S(1)}, f32[64]{0:T(128)}, u32[]{:S(2)}) copy-start(f32[64]{0:T(128)} %param.18) | copy-start | bytes 772
  36.5 8.9 %copy-start.7 = (bf16[3,3,3,64]{3,2,1,0:T(4,128)(2,1)S(1)}, bf16[3,3,3,64]{3,2,1,0:T(4,128)(2,1)}, u32[]{:S(2)}) copy-start(bf16[3,3,3,64]{3,2,1,0:T(4,128)(2,1)} %param.16) | copy-start | bytes 10372
  36.5 8.9 %copy-start.3 = (bf16[3,3,64,64]{3,2,1,0:T(8,128)(2,1)S(1)}, bf16[3,3,64,64]{3,2,1,0:T(8,128)(2,1)}, u32[]{:S(2)}) copy-start(bf16[3,3,64,64]{3,2,1,0:T(8,128)(2,1)} %v_second.3) | copy-start | bytes 221188
  36.5 22.7 %all-to-all-start = ((bf16[32,8,640]{2,1,0:T(8,128)(2,1)}), bf16[32,8,640]{2,1,0:T(8,128)(2,1)S(1)}, u32[]{:S(2)}, u32[]{:S(2)}) async-start(bf16[32,8,640]{2,1,0:T(8,128)(2,1)} %get-tuple-element.38), calls=%async_computation | async-start | bytes 655360 | tf_op jit(solution)/shard_map/all_to_all | solution.py:873
  44.8 8.6 %collective-permute-start.5 = (bf16[1136,128]{1,0:T(8,128)(2,1)S(1)}, bf16[1136,128]{1,0:T(8,128)(2,1)S(1)}, u32[]{:S(2)}, u32[]{:S(2)}) collective-permute-start(bf16[1136,128]{1,0:T(8,128)(2,1)S(1)} %fusion.1.mine), channel_id=1, source_target_pairs={{0,1},{1,0},{2,3},{3,2},{4,5},{5,4},{6,7},{7,6},{8,9},{9,8},{10,11... | collective-permute-start | bytes 872456 | tf_op jit(solution)/shard_map/ppermute | solution.py:874
  45.1 8.3 %collective-permute-start.6 = (bf16[1136,128]{1,0:T(8,128)(2,1)S(1)}, bf16[1136,128]{1,0:T(8,128)(2,1)}, u32[]{:S(2)}, u32[]{:S(2)}) collective-permute-start(bf16[1136,128]{1,0:T(8,128)(2,1)S(1)} %collective-permute-done.4.far), channel_id=1, source_target_pairs={{0,1},{1,0},{2,3},{3,2},{4,5},{5,4},{6,7},{7,6},{8,9},{9,8},{10,11... | collective-permute-start | bytes 872456 | tf_op jit(solution)/shard_map/ppermute | solution.py:875
  73.1 19.9 %all-to-all-start.1 = ((bf16[32,40,128]{2,1,0:T(8,128)(2,1)}), bf16[32,40,128]{2,1,0:T(8,128)(2,1)S(1)}, u32[]{:S(2)}, u32[]{:S(2)}) async-start(bf16[32,40,128]{2,1,0:T(8,128)(2,1)} %shard_map.122), calls=%async_computation.1 | async-start | bytes 655360 | tf_op jit(solution)/shard_map/all_to_all | solution.py:880
  78.7 14.3 %copy-start.2 = (bf16[68,48,128]{2,1,0:T(8,128)(2,1)S(1)}, bf16[68,48,128]{2,1,0:T(8,128)(2,1)}, u32[]{:S(2)}) copy-start(bf16[68,48,128]{2,1,0:T(8,128)(2,1)} %get-tuple-element.46.slope) | copy-start | bytes 2506756
